TPU v7x, 32 devices: a whole 2x2x4 slice. The times are simulated.
32 devices in a mesh: grp: 2 (over x), vocab: 8 (over z, y), row: 2 (over core).
Axes of the slice: x: 2, y: 2, z: 4, core: 2. Of those that a mesh axis runs over, the one named last changes fastest.
Arguments:
- hidden: bfloat16 [512, 2048], P(('grp', 'vocab'), 'row'), parts along dimension 0, may hold values from -160 to 160
- head_weight: bfloat16 [2048, 77824], P('row', 'vocab'), may hold values from -0.5 to 0.5
- teacher_ids: int32 [512, 32], P(('grp', 'row'), 'vocab'), parts along dimension 0, may hold values from 0 to 77823, as said below
- teacher_logprobs: float32 [512, 32], P(('grp', 'row'), 'vocab'), parts along dimension 0, may hold values from -14 to -0.5
- valid: int32 [512], P(('grp', 'row')), parts along dimension 0, may hold values 0 or 1
- row_weight: float32 [512], P(('grp', 'row')), parts along dimension 0, may hold values from 16384 to 131072
Outputs:
- hidden_grad: bfloat16 [512, 2048], P(('grp', 'vocab'), 'row'), parts along dimension 0
- weight_grad: bfloat16 [4096, 77824], P(('grp', 'row'), 'vocab'), parts along dimension 0
There are 2 independent parts, one for each index of `grp`. A program takes and returns all parts, laid end to end along the dimension named above; an argument that names none is the same for every part. Nothing has to cross between parts.
Inputs may be any that keep to these rules, and one draw needn't show every extreme that they name: `teacher_ids`: the 32 ids of a row are distinct.
All inputs are finite; a program needn't handle non-finite values. No bound on the sum of `valid` on one device may be relied on, other than what follows from the above.
Results may differ from a plain program's by a relative error of at most 0.0055.
Values may be sent and summed in bfloat16 or wider, within the bound.
No kernel may reach another device: no remote copies, remote signals or barrier semaphores. Data moves between devices by JAX's collectives and lax.ppermute only.
A program may use at most 192 MiB of HBM per device.

v0:
```python
import jax
import jax.numpy as jnp
from jax import lax
from jax.sharding import PartitionSpec as P


def per_device(hidden, head_weight, teacher_ids, teacher_logprobs, valid, row_weight):
    rows_all = lax.all_gather(hidden, "vocab", axis=0, tiled=True)
    half = rows_all.shape[0] // lax.axis_size("row")
    shard_width = head_weight.shape[1]
    whole = lax.all_gather(rows_all, "row", axis=1, tiled=True)
    mine = lax.dynamic_slice_in_dim(whole, lax.axis_index("row") * half, half, 0)
    logits = jnp.dot(
        mine,
        lax.all_gather(head_weight, "row", axis=0, tiled=True),
        preferred_element_type=jnp.float32,
    )
    ids_row, teacher_row = (
        lax.all_gather(teacher_ids, "vocab", axis=1, tiled=True),
        lax.all_gather(teacher_logprobs, "vocab", axis=1, tiled=True),
    )
    local_ids = ids_row - lax.axis_index("vocab") * shard_width
    inside = (local_ids >= 0) & (local_ids < shard_width)
    safe_ids = jnp.clip(local_ids, 0, shard_width - 1)
    picked = jnp.where(inside, jnp.take_along_axis(logits, safe_ids, axis=1), 0.0)
    local_top = jnp.max(logits, axis=1)
    top = lax.pmax(local_top, "vocab")
    local_sum = jnp.sum(jnp.exp(logits - top[:, None]), axis=1)
    summed, support_raw = lax.psum((local_sum, picked), "vocab")
    lse = top + jnp.log(summed)
    support = support_raw - lse[:, None]
    scale_rows = row_weight * valid.astype(jnp.float32)
    support_grad = scale_rows[:, None] * jnp.exp(support) * (support - teacher_row + 1.0)
    total = jnp.sum(support_grad, axis=1)
    dense = -jnp.exp(logits - lse[:, None]) * total[:, None]
    row_index = jnp.broadcast_to(jnp.arange(half, dtype=jnp.int32)[:, None], local_ids.shape)
    target_cols = jnp.where(inside, local_ids, shard_width)
    dense = dense.at[row_index, target_cols].add(support_grad, mode="drop")
    logit_grad = dense.astype(jnp.bfloat16)
    grads_all = lax.all_gather(logit_grad, "row", axis=0, tiled=True)
    feature_terms = lax.dot_general(
        grads_all, head_weight, (((1,), (1,)), ((), ())), preferred_element_type=jnp.float32
    )
    hidden_grad = lax.psum_scatter(feature_terms, "vocab", scatter_dimension=0, tiled=True).astype(
        jnp.bfloat16
    )
    weight_grad = lax.dot_general(
        rows_all, grads_all, (((0,), (0,)), ((), ())), preferred_element_type=jnp.float32
    )
    return (hidden_grad, weight_grad.astype(jnp.bfloat16))


def solution(mesh):
    return jax.shard_map(
        per_device,
        mesh=mesh,
        in_specs=(
            P(("grp", "vocab"), "row"),
            P("row", "vocab"),
            P(("grp", "row"), "vocab"),
            P(("grp", "row"), "vocab"),
            P(("grp", "row")),
            P(("grp", "row")),
        ),
        out_specs=(P(("grp", "vocab"), "row"), P(("grp", "row"), "vocab")),
        check_vma=False,
    )
```

profile of v0, /device:TPU:0, one launch (start us, length us, event | category | flops | bytes accessed | tf_op | source)
XLA Modules:
  0.0 492.9 jit_solution(12672410454295286413)
XLA Ops:
  7.2 35.4 %all_gather.18 = bf16[256,1024]{1,0:T(8,128)(2,1)} all-gather(bf16[32,1024]{1,0:T(8,128)(2,1)} %param.6), channel_id=1, replica_groups=mesh['grp'=2,'vocab'=8,'row'=2] {'vocab'}, dimensions={0}, use_global_device_ids=true | all-gather | bytes 589824 | tf_op jit(solution)/shard_map/all_gather | solution.py:8
  42.8 0.7 all-gather.8.cloned.1.call-update
  43.6 26.0 %all-gather = s32[8,4,128]{2,1,0:T(4,128)S(1)} all-gather(s32[1,4,128]{2,1,0:T(4,128)S(1)} %bitcast.32), channel_id=1, replica_groups=mesh['grp'=2,'vocab'=8,'row'=2] {'vocab'}, dimensions={0}, use_global_device_ids=true | all-gather | bytes 18432 | tf_op jit(solution)/shard_map/all_gather | solution.py:19
  69.6 0.1 copy.16
  70.0 0.1 copy.18
  70.2 26.0 %all-gather.1 = f32[8,4,128]{2,1,0:T(4,128)S(1)} all-gather(f32[1,4,128]{2,1,0:T(4,128)S(1)} %bitcast.33), channel_id=1, replica_groups=mesh['grp'=2,'vocab'=8,'row'=2] {'vocab'}, dimensions={0}, use_global_device_ids=true | all-gather | bytes 18432 | tf_op jit(solution)/shard_map/all_gather | solution.py:20
  96.2 19.3 %all-gather.8.cloned.1.call-done = bf16[2048,9728]{1,0:T(8,128)(2,1)} async-done(((bf16[1024,9728]{1,0:T(8,128)(2,1)}), bf16[2048,9728]{1,0:T(8,128)(2,1)}) %all-gather.8.cloned.1.call-update) | async-done | bytes 39845904 | tf_op jit(solution)/shard_map/all_gather | solution.py:15
  115.5 17.6 %fusion.5 = (f32[128]{0:T(128)S(1)}, f32[128,9728]{1,0:T(8,128)}) fusion(bf16[2048,9728]{1,0:T(8,128)(2,1)} %all-gather.8.cloned.1.call-done, bf16[256,2048]{1,0:T(8,128)(2,1)} %all-gather.6.cloned.1.call-done, s32[]{:T(128)S(6)} %select_n.24), kind=kOutput, calls=%fused_computation.23 | convolution fusion | flops 5101518848 | bytes 45351428 | tf_op jit(solution)/shard_map/dot_general | solution.py:13
  133.1 21.6 %pmax.7 = f32[128]{0:T(128)S(1)} all-reduce(f32[128]{0:T(128)S(1)} %get-tuple-element.14), channel_id=1, replica_groups=mesh['grp'=2,'vocab'=8,'row'=2] {'vocab'}, use_global_device_ids=true, to_apply=%region_1.2 | all-reduce | flops 128 | bytes 1024 | tf_op jit(solution)/shard_map/pmax | solution.py:27
  154.7 3.2 exponential_reduce_fusion
  157.9 163.2 %gather_fusion = f32[4096]{0:T(1024)S(1)} fusion(f32[128,9728]{1,0:T(8,128)} %get-tuple-element.15, s32[4096]{0:T(1024)S(1)} %reshape.35), kind=kCustom, calls=%fused_computation | custom fusion | bytes 65536 | tf_op jit(solution)/shard_map/jit(take_along_axis)/gather | solution.py:25
  321.3 33.0 %all-reduce = (f32[128,32]{0,1:T(8,128)S(1)}, f32[128]{0:T(128)S(1)}) all-reduce(f32[128,32]{0,1:T(8,128)S(1)} %select_select_fusion, f32[128]{0:T(128)S(1)} %exponential_reduce_fusion), channel_id=1, replica_groups=mesh['grp'=2,'vocab'=8,'row'=2] {'vocab'}, use_global_device_ids=true, to_apply=%region_4.5 | all-reduce | flops 4224 | bytes 33792 | tf_op jit(solution)/shard_map/psum | solution.py:29
  354.4 5.6 %negate_multiply_fusion = f32[128,9728]{1,0:T(8,128)} fusion(f32[128,9728]{1,0:T(8,128)} %get-tuple-element.15, f32[128]{0:T(128)S(1)} %get-tuple-element.12, f32[128]{0:T(128)S(1)} %log_add_fusion), kind=kLoop, calls=%fused_computation.3 | loop fusion | flops 3735552 | bytes 9962496 | tf_op jit(solution)/shard_map/mul | solution.py:35
  359.9 5.2 %reshape.31 = f32[1245184]{0:T(1024)} reshape(f32[128,9728]{1,0:T(8,128)} %negate_multiply_fusion) | data formatting | bytes 9961472
  365.3 24.7 %scatter_fusion = f32[1245184]{0:T(1024)} fusion(f32[1245184]{0:T(1024)} %reshape.31, s32[4096]{0:T(1024)S(1)} %reshape.41, f32[4096]{0:T(1024)S(1)} %reshape.43), kind=kCustom, calls=%fused_computation.1 | custom fusion | flops 4096 | bytes 65536
  390.0 2.6 convert_element_type.20
  392.6 3.7 reshape.34
  396.3 0.2 reduce-scatter.2.cloned.1.call-start
  396.6 11.6 %all-gather.10.cloned.1.call-done = bf16[256,9728]{1,0:T(8,128)(2,1)} async-done(((bf16[128,9728]{1,0:T(8,128)(2,1)}), bf16[256,9728]{1,0:T(8,128)(2,1)}) %all-gather.10.cloned.1.call-update) | async-done | bytes 4980752 | tf_op jit(solution)/shard_map/all_gather | solution.py:40
  408.2 11.7 %fusion.6 = f32[256,1024]{1,0:T(8,128)} fusion(bf16[256,9728]{1,0:T(8,128)(2,1)} %all-gather.10.cloned.1.call-done, bf16[1024,9728]{1,0:T(8,128)(2,1)} %param.7), kind=kOutput, calls=%fused_computation.24 | convolution fusion | flops 5100273664 | bytes 25952256 | tf_op jit(solution)/shard_map/dot_general | solution.py:41
  420.0 12.1 %convert_bitcast_fusion = bf16[1024,9728]{0,1:T(8,128)(2,1)} fusion(bf16[256,9728]{1,0:T(8,128)(2,1)} %all-gather.10.cloned.1.call-done, bf16[256,1024]{1,0:T(8,128)(2,1)S(1)} %copy-done), kind=kOutput, calls=%fused_computation.2 | convolution fusion | flops 5110235136 | bytes 25427968 | tf_op jit(solution)/shard_map/dot_general | solution.py:47
  432.1 25.0 %copy.20 = bf16[1024,9728]{1,0:T(8,128)(2,1)} copy(bf16[1024,9728]{0,1:T(8,128)(2,1)} %convert_bitcast_fusion) | data formatting | bytes 39845888
  457.1 27.7 %reduce-scatter.2.cloned.1.call-done = f32[32,1024]{1,0:T(8,128)} async-done(((f32[256,1024]{1,0:T(8,128)}), f32[32,1024]{1,0:T(8,128)}) %reduce-scatter.2.cloned.1.call-update) | async-done | bytes 131088 | tf_op jit(solution)/shard_map/reduce_scatter | solution.py:44
  484.8 1.5 convert_element_type.17
  (38 shorter events, 1.0 us)
Async XLA Ops:
  7.2 89.0 %all-gather.6.cloned.1.call-start = ((), (), s32[]{:S(2)}) async-start(), calls=%async_computation.1 | async-start | bytes 1572864 | tf_op jit(solution)/shard_map/all_gather | solution.py:11
  42.7 0.9 copy-start.1
  42.7 27.1 %copy-start.4 = (s32[2]{0:T(128)S(1)}, s32[2]{0:T(128)}, u32[]{:S(2)}) copy-start(s32[2]{0:T(128)} %constant.43) | copy-start | bytes 28
  42.7 27.2 %copy-start.3 = (s32[2]{0:T(128)S(1)}, s32[2]{0:T(128)}, u32[]{:S(2)}) copy-start(s32[2]{0:T(128)} %constant.46) | copy-start | bytes 28
  42.7 27.4 %copy-start.2 = (f32[128,4]{0,1:T(4,128)S(1)}, f32[128,4]{0,1:T(4,128)}, u32[]{:S(2)}) copy-start(f32[128,4]{0,1:T(4,128)} %param.9) | copy-start | bytes 6148
  42.7 53.4 %copy-start.5 = (f32[128]{0:T(128)S(1)}, f32[128]{0:T(128)}, u32[]{:S(2)}) copy-start(f32[128]{0:T(128)} %param.11) | copy-start | bytes 1540
  42.7 53.4 %copy-start.6 = (s32[128]{0:T(128)S(1)}, s32[128]{0:T(128)}, u32[]{:S(2)}) copy-start(s32[128]{0:T(128)} %param.10) | copy-start | bytes 1540
  42.8 72.7 %all-gather.8.cloned.1.call-start = ((), (), s32[]{:S(2)}) async-start(), calls=%async_computation.2 | async-start | bytes 59768832 | tf_op jit(solution)/shard_map/all_gather | solution.py:15
  43.5 364.7 %all-gather.10.cloned.1.call-start = ((), (), s32[]{:S(2)}) async-start(), calls=%async_computation.3 | async-start | bytes 7471104 | tf_op jit(solution)/shard_map/all_gather | solution.py:40
  396.3 23.6 %copy-start = (bf16[256,1024]{1,0:T(8,128)(2,1)S(1)}, bf16[256,1024]{1,0:T(8,128)(2,1)}, u32[]{:S(2)}) copy-start(bf16[256,1024]{1,0:T(8,128)(2,1)} %all_gather.18) | copy-start | bytes 1572868
  396.3 88.5 %reduce-scatter.2.cloned.1.call-start = ((), (), s32[]{:S(2)}) async-start(), calls=%async_computation.4 | async-start | bytes 1179648 | tf_op jit(solution)/shard_map/reduce_scatter | solution.py:44
Sparse Core Ops, SparseCore 0:
  42.8 10.0 all-gather.5
  54.4 60.9 all-gather.7
  396.4 11.7 all-gather.9
  420.1 64.6 reduce-scatter.1
where the time goes:
time: 497 us; the launch traced here: 493 us
  local copies, waits for them, and re-layouts  198 us (40%)
  blocking collectives  142 us (29%)
  waiting for transfers between devices  59.4 us (12%)
  matrix products  41.4 us (8%)
  other arithmetic  37.9 us (8%)
  between operations  13.9 us (3%)
    gather x5, local copies, waits for them, and re-layouts, per_device(): jnp.take_along_axis(logits, safe_ids, axis=1)  163 us
    all_gather x1, blocking collectives, per_device(): rows_all = lax.all_gather(hidden, 'vocab', axis=0, tiled=True)  35.4 us
    psum x1, blocking collectives, per_device(): summed, support_raw = lax.psum((local_sum, picked), 'vocab')  33 us
    unnamed x18, local copies, waits for them, and re-layouts  30.4 us
    reduce_scatter x1, waiting for transfers between devices, per_device(): lax.psum_scatter(feature_terms, 'vocab', scatter_dimension=0, tiled=True)  27.7 us
    all_gather x1, blocking collectives, per_device(): lax.all_gather(teacher_ids, 'vocab', axis=1, tiled=True)  26 us
    all_gather x1, blocking collectives, per_device(): lax.all_gather(teacher_logprobs, 'vocab', axis=1, tiled=True)  26 us
    unnamed x4, other arithmetic  24.8 us
  transfers between devices with their start and end apart: 4, of which 3 were waited for; matrix products, arithmetic and copies ran while one was open for 8% of the time, Pallas kernels for 0%

commit v1 on v0

v1 whole, which is shorter than its diff:
```python
import functools

import jax
import jax.numpy as jnp
from jax import lax
from jax.experimental import pallas as pl
from jax.experimental.pallas import tpu as pltpu
from jax.sharding import PartitionSpec as P

VMEM_LIMIT = 48 * 1024 * 1024
TILE = 8
STEP = 16
NT = (((1,), (1,)), ((), ()))
F32 = jnp.float32
BF16 = jnp.bfloat16


def _params():
    return pltpu.CompilerParams(vmem_limit_bytes=VMEM_LIMIT)


def _cost(flops, nbytes):
    return pl.CostEstimate(flops=int(flops), bytes_accessed=int(nbytes), transcendentals=0)


def _split(width):
    unit = 256 if width % 256 == 0 else 128
    units = width // unit
    first = (units + 1) // 2
    first += first % 2 if units > 4 else 0
    out = []
    start = 0
    for count in (first, units - first):
        if count:
            best = max(d for d in range(1, count + 1) if count % d == 0 and d * unit <= 1536)
            out.append((start * unit, count * unit, best * unit))
            start += count
    return out


def _xor(n, s):
    return [(i, i ^ s) for i in range(n)]


def _w_spec(depth, chunk):
    start, _, block = chunk
    return pl.BlockSpec(
        (pl.Element(depth), pl.Element(block)),
        lambda j: (0, pl.multiple_of(start + j * block, 128)),
    )


def _whole(shape):
    return pl.BlockSpec(shape, lambda j: (0,) * len(shape))


def _logits_body(h_ref, w_ref, own_ref, send_ref):
    part = jnp.dot(h_ref[...], w_ref[...], preferred_element_type=F32)
    half = own_ref.shape[0]
    own_ref[...] = part[:half]
    send_ref[...] = part[half:]


def _partial_logits(h, w, chunk):
    _, width, block = chunk
    rows, depth = h.shape
    half = rows // 2
    out = jax.ShapeDtypeStruct((half, width), F32)
    spec = pl.BlockSpec((half, block), lambda j: (0, j))
    return pl.pallas_call(
        _logits_body,
        grid=(width // block,),
        in_specs=[_whole((rows, depth)), _w_spec(depth, chunk)],
        out_specs=[spec, spec],
        out_shape=[out, out],
        compiler_params=_params(),
        cost_estimate=_cost(2 * rows * depth * width, 2 * depth * width + 4 * rows * width),
        name="partial_logits",
    )(h, w)


def _row_mask(lanes, terms):
    lane_row = lax.broadcasted_iota(jnp.int32, (TILE, lanes), 1) // terms
    return lane_row == lax.broadcasted_iota(jnp.int32, (TILE, lanes), 0)


def _exp_body(start, last, *refs):
    if last:
        own_ref, recv_ref, ids_ref, lps_ref, picks_in, stat_in, e_ref, picks_ref, stat_ref, tot_ref, hold = refs
    else:
        own_ref, recv_ref, ids_ref, e_ref, picks_ref, stat_ref = refs
    step = pl.program_id(0)
    width = own_ref.shape[1]
    lanes = ids_ref.shape[1]
    terms = lanes // TILE
    mask = _row_mask(lanes, terms)
    lane = lax.broadcasted_iota(jnp.int32, (TILE, 128), 1)
    for t in range(STEP // TILE):
        tile = step * (STEP // TILE) + t
        rows = slice(t * TILE, (t + 1) * TILE)
        rel = jnp.broadcast_to(ids_ref[pl.ds(tile, 1), :] - start, (TILE, lanes))
        key = jnp.where(mask, rel >> 7, -1)
        slot = rel & 127
        groups = range(lanes // 128)
        slots = [slot[:, g * 128 : (g + 1) * 128] for g in groups]
        keys = [key[:, g * 128 : (g + 1) * 128] for g in groups]
        acc = [jnp.zeros((TILE, 128), F32) for _ in groups]
        top = jnp.full((TILE, 128), -jnp.inf, F32)
        for c in range(width // 128):
            cols = slice(c * 128, (c + 1) * 128)
            logit = own_ref[rows, cols] + recv_ref[rows, cols]
            e_ref[rows, cols] = logit
            top = jnp.maximum(top, logit)
            for g in groups:
                got = jnp.take_along_axis(logit, slots[g], axis=1, mode="promise_in_bounds")
                acc[g] = jnp.where(keys[g] == c, got, acc[g])
        top = jnp.max(top, axis=1, keepdims=True)
        total = jnp.zeros((TILE, 128), F32)
        for c in range(width // 128):
            cols = slice(c * 128, (c + 1) * 128)
            e = jnp.exp(e_ref[rows, cols] - top)
            e_ref[rows, cols] = e
            total = total + e
        total = jnp.sum(total, axis=1, keepdims=True)
        picked = jnp.concatenate(acc, axis=1)
        if last:
            picked = picked + picks_in[rows, :]
        picks_ref[rows, :] = picked
        stat_ref[rows, :] = jnp.where(lane == 0, top, total)
        if last:
            before = stat_in[rows, :]
            top0, total0 = before[:, 0:1], before[:, 1:2]
            both = jnp.maximum(top, top0)
            total = total * jnp.exp(top - both) + total0 * jnp.exp(top0 - both)
            whole = jnp.broadcast_to(ids_ref[pl.ds(tile, 1), :], (TILE, lanes))
            inside = mask & (whole >= 0) & (whole < start + width)
            weight = jnp.where(inside, jnp.exp(picked - both), 0.0)
            teacher = jnp.broadcast_to(lps_ref[pl.ds(tile, 1), :], (TILE, lanes))
            first = jnp.sum(weight * (picked - both - teacher + 1.0), axis=1, keepdims=True)
            plain = jnp.sum(weight, axis=1, keepdims=True)
            hold[pl.ds(tile * TILE, TILE), :] = jnp.where(
                lane == 0, both, jnp.where(lane == 1, total, jnp.where(lane == 2, first, plain))
            )
    if last:

        @pl.when(step == pl.num_programs(0) - 1)
        def _():
            tot_ref[...] = hold[...].T[:TILE, :]


def _exponentials(own, recv, ids, chunk, lps=None, before=None):
    start, width, _ = chunk
    half = own.shape[0]
    tiles, lanes = ids.shape
    last = before is not None
    row = lambda w: pl.BlockSpec((STEP, w), lambda i: (i, 0))
    out_shape = [
        jax.ShapeDtypeStruct((half, width), F32),
        jax.ShapeDtypeStruct((half, lanes), F32),
        jax.ShapeDtypeStruct((half, 128), F32),
    ]
    out_specs = [row(width), row(lanes), row(128)]
    in_specs = [row(width), row(width), _whole((tiles, lanes))]
    args = [own, recv, ids]
    scratch = []
    if last:
        in_specs += [_whole((tiles, lanes)), row(lanes), row(128)]
        args += [lps, *before]
        out_shape.append(jax.ShapeDtypeStruct((TILE, half), F32))
        out_specs.append(_whole((TILE, half)))
        scratch = [pltpu.VMEM((half, 128), F32)]
    return pl.pallas_call(
        functools.partial(_exp_body, start, last),
        grid=(half // STEP,),
        in_specs=in_specs,
        out_specs=out_specs,
        out_shape=out_shape,
        scratch_shapes=scratch,
        compiler_params=_params(),
        cost_estimate=_cost(8 * half * width, 12 * half * width),
        name="exponentials",
    )(*args)


def _join_stats(a, b):
    top = jnp.maximum(a[0], b[0])
    da, db = a[0] - top, b[0] - top
    fa, fb = jnp.exp(da), jnp.exp(db)
    return jnp.stack(
        [
            top,
            a[1] * fa + b[1] * fb,
            (a[2] + da * a[3]) * fa + (b[2] + db * b[3]) * fb,
            a[3] * fa + b[3] * fb,
        ]
    )


def _grad_body(start, e_ref, stat_ref, picks_ref, ids_ref, lps_ref, tot_ref, g_ref, hold):
    step = pl.program_id(0)
    width = e_ref.shape[1]
    lanes = ids_ref.shape[1]
    terms = lanes // TILE
    half = tot_ref.shape[1]

    @pl.when(step == 0)
    def _():
        hold[...] = jnp.concatenate([tot_ref[...], jnp.zeros((128 - TILE, half), F32)], axis=0).T

    mask = _row_mask(lanes, terms)
    parts = (width + 255) // 256
    place = lax.broadcasted_iota(jnp.int32, (256, lanes), 0)
    coefs, terms_of = [], []
    for t in range(STEP // TILE):
        tile = step * (STEP // TILE) + t
        rows = slice(t * TILE, (t + 1) * TILE)
        tot = hold[pl.ds(tile * TILE, TILE), :]
        top, total, first, plain, scale = (tot[:, i : i + 1] for i in range(5))
        log_sum = jnp.log(total)
        lse = top + log_sum
        sum_grad = scale * jnp.exp(-log_sum) * (first - log_sum * plain)
        coefs.append(sum_grad * jnp.exp(stat_ref[rows, 0:1] - lse))
        rel_row = ids_ref[pl.ds(tile, 1), :] - start
        rel = jnp.broadcast_to(rel_row, (TILE, lanes))
        inside = mask & (rel >= 0) & (rel < width)
        support = picks_ref[rows, :] - lse
        grad = scale * jnp.exp(support) * (support - lps_ref[pl.ds(tile, 1), :] + 1.0)
        grad = jnp.where(inside, grad, 0.0)
        high = grad.astype(BF16).astype(F32)
        low = grad - high
        key = jnp.where(inside, rel >> 8, -1)
        lhs = jnp.concatenate(
            [
                jnp.concatenate([jnp.where(key == c, high, 0.0), jnp.where(key == c, low, 0.0)], axis=1)
                for c in range(parts)
            ],
            axis=0,
        ).astype(BF16)
        hot = (place == jnp.broadcast_to(rel_row & 255, (256, lanes))).astype(F32).astype(BF16)
        rhs = jnp.concatenate([hot, hot], axis=1)
        terms_of.append(lax.dot_general(lhs, rhs, NT, preferred_element_type=F32))
    for c in range(parts):
        size = min(256, width - c * 256)
        cols = slice(c * 256, c * 256 + size)
        out = [
            terms_of[t][c * TILE : (c + 1) * TILE, :size] - e_ref[t * TILE : (t + 1) * TILE, cols] * coefs[t]
            for t in range(STEP // TILE)
        ]
        g_ref[:, cols] = jnp.concatenate(out, axis=0).astype(BF16)


def _logit_grad(e, stat, picks, ids, lps, tot, chunk):
    start, width, _ = chunk
    half = e.shape[0]
    tiles, lanes = ids.shape
    row = lambda w: pl.BlockSpec((STEP, w), lambda i: (i, 0))
    return pl.pallas_call(
        functools.partial(_grad_body, start),
        grid=(half // STEP,),
        in_specs=[row(width), row(128), row(lanes), _whole((tiles, lanes)), _whole((tiles, lanes)), _whole(tot.shape)],
        out_specs=row(width),
        out_shape=jax.ShapeDtypeStruct((half, width), BF16),
        scratch_shapes=[pltpu.VMEM((half, 128), F32)],
        compiler_params=_params(),
        cost_estimate=_cost(8 * half * width, 6 * half * width),
        name="logit_grad",
    )(e, stat, picks, ids, lps, tot)


def _feature_body(last, count, *refs):
    if last:
        order_ref, own_ref, other_ref, w_ref, before_ref, keep_ref, send_ref, acc = refs
    else:
        own_ref, other_ref, w_ref, acc = refs
    step = pl.program_id(0)
    grads = jnp.concatenate([own_ref[...], other_ref[...]], axis=0)
    part = lax.dot_general(grads, w_ref[...], NT, preferred_element_type=F32)

    @pl.when(step == 0)
    def _():
        acc[...] = part + before_ref[...] if last else part

    @pl.when(step > 0)
    def _():
        acc[...] += part

    if last:

        @pl.when(step == pl.num_programs(0) - 1)
        def _():
            rows = acc.shape[0] // count
            near, far = [], []
            for d in range(count):
                at = pl.multiple_of(order_ref[d] * rows, rows)
                (far if d % 2 else near).append(acc[pl.ds(at, rows), :])
            keep_ref[...] = jnp.concatenate(near, axis=0)
            send_ref[...] = jnp.concatenate(far, axis=0).astype(BF16)


def _feature_terms(own, other, w, chunk, order=None, before=None):
    _, width, block = chunk
    half = own.shape[0]
    depth = w.shape[0]
    last = before is not None
    part = pl.BlockSpec((half, block), lambda j: (0, j))
    in_specs = [part, part, _w_spec(depth, chunk)]
    args = [own, other, w]
    if last:
        in_specs = [pl.BlockSpec(memory_space=pltpu.SMEM)] + in_specs + [_whole((2 * half, depth))]
        args = [order] + args + [before]
        out_shape = [jax.ShapeDtypeStruct((half, depth), F32), jax.ShapeDtypeStruct((half, depth), BF16)]
        out_specs = [_whole((half, depth))] * 2
        scratch = [pltpu.VMEM((2 * half, depth), F32)]
    else:
        out_shape = jax.ShapeDtypeStruct((2 * half, depth), F32)
        out_specs = _whole((2 * half, depth))
        scratch = []
    return pl.pallas_call(
        functools.partial(_feature_body, last, order.shape[0] if last else 0),
        grid=(width // block,),
        in_specs=in_specs,
        out_specs=out_specs,
        out_shape=out_shape,
        scratch_shapes=scratch,
        compiler_params=_params(),
        cost_estimate=_cost(4 * half * depth * width, 2 * depth * width + 4 * half * width),
        name="feature_terms",
    )(*args)


def _weight_body(ht_ref, own_ref, other_ref, *refs):
    grads = jnp.concatenate([own_ref[...], other_ref[...]], axis=0)
    refs[-1][...] = jnp.dot(ht_ref[...], grads, preferred_element_type=F32).astype(BF16)


def _weight_grad(ht, own, other, chunk, width_all, before=None):
    _, width, block = chunk
    depth, rows = ht.shape
    part = pl.BlockSpec((rows // 2, block), lambda j: (0, j))
    in_specs = [_whole((depth, rows)), part, part]
    args = [ht, own, other]
    aliases = {}
    if before is not None:
        in_specs.append(pl.BlockSpec(memory_space=pl.ANY))
        args.append(before)
        aliases = {3: 0}
    return pl.pallas_call(
        _weight_body,
        grid=(width // block,),
        in_specs=in_specs,
        out_specs=_w_spec(depth, chunk),
        out_shape=jax.ShapeDtypeStruct((depth, width_all), BF16),
        input_output_aliases=aliases,
        compiler_params=_params(),
        cost_estimate=_cost(2 * rows * depth * width, 2 * depth * width + 2 * rows * width),
        name="weight_grad",
    )(*args)


def per_device(hidden, head_weight, teacher_ids, teacher_logprobs, valid, row_weight):
    count = lax.axis_size("vocab")
    bits = count.bit_length() - 1
    r = lax.axis_index("row")
    v = lax.axis_index("vocab")
    depth, width = head_weight.shape
    half = teacher_ids.shape[0]
    swap = [(0, 1), (1, 0)]
    chunks = _split(width)

    h = hidden[None]
    for b in reversed(range(bits)):
        far = lax.ppermute(h, "vocab", _xor(count, 1 << b))
        bit = (v >> b) & 1
        first = bit == r if b == bits - 1 else bit == 0
        h = jnp.stack([jnp.where(first, h, far), jnp.where(first, far, h)], axis=1)
        h = h.reshape((-1,) + hidden.shape)
    h = h.reshape(-1, hidden.shape[1])
    ht = h.T

    own_terms = teacher_ids.shape[1]
    packed = jnp.concatenate([teacher_ids.astype(F32).T, teacher_logprobs.T], axis=0)
    packed = packed.reshape(1, 2, own_terms, half)
    for b in range(bits):
        packed = jnp.concatenate([packed, lax.ppermute(packed, "vocab", _xor(count, 1 << b))], axis=0)
    flat = packed.transpose(1, 3, 0, 2).reshape(2, half // TILE, -1)
    ids = flat[0].astype(jnp.int32) - v * width
    lps = flat[1]

    parts = []
    for chunk in chunks:
        own, send = _partial_logits(h, head_weight, chunk)
        parts.append((own, lax.ppermute(send, "row", swap)))
    e0, picks, stat0 = _exponentials(*parts[0], ids, chunks[0])
    e1, picks, stat1, stats = _exponentials(*parts[1], ids, chunks[1], lps, (picks, stat0))

    stats = stats[:4]
    for b in range(bits):
        stats = _join_stats(stats, lax.ppermute(stats, "vocab", _xor(count, 1 << b)))
    scale = row_weight * valid.astype(F32)
    tot = jnp.concatenate([stats, scale[None], jnp.zeros((3, half), F32)], axis=0)

    grads = []
    for chunk, e, stat in zip(chunks, (e0, e1), (stat0, stat1)):
        own = _logit_grad(e, stat, picks, ids, lps, tot, chunk)
        grads.append((own, lax.ppermute(own, "row", swap)))

    top_bit = count // 2
    order = (jnp.arange(count, dtype=jnp.int32) ^ v) ^ (r * top_bit)
    terms = _feature_terms(*grads[0], head_weight, chunks[0])
    keep, send = _feature_terms(*grads[1], head_weight, chunks[1], order, terms)

    keep = keep + lax.ppermute(send, "vocab", _xor(count, 1)).astype(F32)
    keep = keep.reshape((count // 2,) + hidden.shape)
    total = keep[0]
    for d in range(1, count // 2):
        far = lax.ppermute(keep[d].astype(BF16), "vocab", _xor(count, 2 * d))
        total = total + far.astype(F32)
    hidden_grad = total.astype(BF16)

    weight_grad = _weight_grad(ht, *grads[0], chunks[0], width)
    weight_grad = _weight_grad(ht, *grads[1], chunks[1], width, weight_grad)
    return hidden_grad, weight_grad


def solution(mesh):
    return jax.shard_map(
        per_device,
        mesh=mesh,
        in_specs=(
            P(("grp", "vocab"), "row"),
            P("row", "vocab"),
            P(("grp", "row"), "vocab"),
            P(("grp", "row"), "vocab"),
            P(("grp", "row")),
            P(("grp", "row")),
        ),
        out_specs=(P(("grp", "vocab"), "row"), P(("grp", "row"), "vocab")),
        check_vma=False,
    )
```

time: 497 us -> 131 us (0.26)
  local copies, waits for them, and re-layouts: 198 us -> 13.7 us
  blocking collectives: 142 us -> 0 us
  Pallas kernels: 0 us -> 61.8 us
  matrix products: 41.4 us -> 0 us
  other arithmetic: 37.9 us -> 2.84 us
  waiting for transfers between devices: 59.4 us -> 25 us
  starting transfers between devices: 0.34 us -> 25.7 us
  between operations: 13.9 us -> 0.88 us
    gather x5 -> x0, local copies, waits for them, and re-layouts: 163 us -> none  [per_device(): jnp.take_along_axis(logits, safe_ids, axis=1)]
    all_gather x3 -> x0, blocking collectives: 87.4 us -> none  [the longest x1 35.4 us: per_device(): rows_all = lax.all_gather(hidden, 'vocab', axis=0, tiled=True)]
    pallas_call x0 -> x10, Pallas kernels: none -> 61.8 us  [the longest x2 14.8 us: _partial_logits(): pl.pallas_call(_logits_body, grid=(width // block,), in_specs=[_whole((ro...]
    dot_general x3 -> x0, matrix products: 41.4 us -> none  [the longest x1 17.6 us: per_device(): jnp.dot(mine, lax.all_gather(head_weight, 'row', axis=0, tiled=True), pre...]
    psum x1 -> x0, blocking collectives: 33 us -> none  [per_device(): summed, support_raw = lax.psum((local_sum, picked), 'vocab')]
    all_gather x3 -> x0, waiting for transfers between devices: 30.9 us -> none  [the longest x1 19.3 us: per_device(): lax.all_gather(head_weight, 'row', axis=0, tiled=True)]
    reduce_scatter x1 -> x0, waiting for transfers between devices: 27.7 us -> none  [per_device(): lax.psum_scatter(feature_terms, 'vocab', scatter_dimension=0, tiled=True)]
    ppermute x0 -> x17, starting transfers between devices: none -> 25.7 us  [the longest x3 6.63 us: per_device(): far = lax.ppermute(h, 'vocab', _xor(count, 1 << b))]
  transfers between devices with their start and end apart: 4 -> 17, of which waited for: 3 -> 9; matrix products, arithmetic and copies ran while one was open for 8% -> 4% of each run, Pallas kernels for 0% -> 28%
where the time goes in v1:
time: 131 us; the launch traced here: 130 us
  Pallas kernels  61.8 us (47%)
  starting transfers between devices  25.7 us (20%)
  waiting for transfers between devices  25 us (19%)
  local copies, waits for them, and re-layouts  13.7 us (10%)
  other arithmetic  2.84 us (2%)
    pallas_call x2, Pallas kernels, _partial_logits(): pl.pallas_call(_logits_body, grid=(width // block,), in_specs=[_whole((ro...  14.8 us
    pallas_call x2, Pallas kernels, _feature_terms(): pl.pallas_call(functools.partial(_feature_body, last, order.shape[0] if l...  14.1 us
    pallas_call x2, Pallas kernels, _weight_grad(): pl.pallas_call(_weight_body, grid=(width // block,), in_specs=in_specs, o...  13.3 us
    ppermute x3, waiting for transfers between devices, per_device(): far = lax.ppermute(h, 'vocab', _xor(count, 1 << b))  12.8 us
    pallas_call x2, Pallas kernels, _exponentials(): pl.pallas_call(functools.partial(_exp_body, start, last), grid=(half // S...  12.7 us
    unnamed x24, local copies, waits for them, and re-layouts  8.73 us
    pallas_call x2, Pallas kernels, _logit_grad(): pl.pallas_call(functools.partial(_grad_body, start), grid=(half // STEP,)...  6.98 us
    ppermute x3, starting transfers between devices, per_device(): far = lax.ppermute(h, 'vocab', _xor(count, 1 << b))  6.63 us
  transfers between devices with their start and end apart: 17, of which 9 were waited for; matrix products, arithmetic and copies ran while one was open for 4% of the time, Pallas kernels for 28%

profile of v1, /device:TPU:0, one launch (start us, length us, event | category | flops | bytes accessed | tf_op | source)
XLA Modules:
  0.0 130.0 jit_solution(4214605475138606228)
XLA Ops:
  0.6 4.1 %collective-permute-start = (bf16[1,32,1024]{2,1,0:T(8,128)(2,1)}, bf16[1,32,1024]{2,1,0:T(8,128)(2,1)S(1)}, u32[]{:S(2)}, u32[]{:S(2)}) collective-permute-start(bf16[1,32,1024]{2,1,0:T(8,128)(2,1)} %bitcast.53), channel_id=1, source_target_pairs={{0,8},{2,10},{4,12},{6,14},{8,0},{10,2},{12,4},{14,6},{1,9},{3,11}... | collective-permute-start | bytes 196616 | tf_op jit(solution)/shard_map/ppermute | solution.py:372
  4.7 3.9 %collective-permute-done = bf16[1,32,1024]{2,1,0:T(8,128)(2,1)S(1)} collective-permute-done((bf16[1,32,1024]{2,1,0:T(8,128)(2,1)}, bf16[1,32,1024]{2,1,0:T(8,128)(2,1)S(1)}, u32[]{:S(2)}, u32[]{:S(2)}) %collective-permute-start) | collective-permute-done | bytes 65568 | tf_op jit(solution)/shard_map/ppermute | solution.py:372
  10.2 4.3 %collective-permute-done.1 = bf16[2,32,1024]{2,1,0:T(8,128)(2,1)S(1)} collective-permute-done((bf16[2,32,1024]{2,1,0:T(8,128)(2,1)S(1)}, bf16[2,32,1024]{2,1,0:T(8,128)(2,1)S(1)}, u32[]{:S(2)}, u32[]{:S(2)}) %collective-permute-start.1) | collective-permute-done | bytes 131104 | tf_op jit(solution)/shard_map/ppermute | solution.py:372
  14.6 1.8 %collective-permute-start.2 = (bf16[4,32,1024]{2,1,0:T(8,128)(2,1)S(1)}, bf16[4,32,1024]{2,1,0:T(8,128)(2,1)S(1)}, u32[]{:S(2)}, u32[]{:S(2)}) collective-permute-start(bf16[4,32,1024]{2,1,0:T(8,128)(2,1)S(1)} %bitcast.48), channel_id=1, source_target_pairs={{0,2},{2,0},{4,6},{6,4},{8,10},{10,8},{12,14},{14,12},{1,3},{3,1},... | collective-permute-start | bytes 786440 | tf_op jit(solution)/shard_map/ppermute | solution.py:372
  16.4 4.6 %collective-permute-done.2 = bf16[4,32,1024]{2,1,0:T(8,128)(2,1)S(1)} collective-permute-done((bf16[4,32,1024]{2,1,0:T(8,128)(2,1)S(1)}, bf16[4,32,1024]{2,1,0:T(8,128)(2,1)S(1)}, u32[]{:S(2)}, u32[]{:S(2)}) %collective-permute-start.2) | collective-permute-done | bytes 262176 | tf_op jit(solution)/shard_map/ppermute | solution.py:372
  21.2 7.5 %partial_logits.3 = (f32[128,5120]{1,0:T(8,128)S(1)}, f32[128,5120]{1,0:T(8,128)}) custom-call(bf16[256,1024]{1,0:T(8,128)(2,1)S(1)} %bitcast.43, bf16[1024,9728]{1,0:T(8,128)(2,1)} %refs_3_.1), custom_call_target="tpu_custom_call" | custom-call | flops 2684354560 | bytes 15728640 | tf_op jit(solution)/shard_map/partial_logits/pallas_call | solution.py:70
  30.1 7.3 %partial_logits.2 = (f32[128,4608]{1,0:T(8,128)S(1)}, f32[128,4608]{1,0:T(8,128)}) custom-call(bf16[256,1024]{1,0:T(8,128)(2,1)S(1)} %bitcast.44, bf16[1024,9728]{1,0:T(8,128)(2,1)} %refs_3_.1), custom_call_target="tpu_custom_call" | custom-call | flops 2415919104 | bytes 14155776 | tf_op jit(solution)/shard_map/partial_logits/pallas_call | solution.py:70
  37.9 1.8 %collective-permute-start.4 = (f32[1,2,4,128]{3,2,1,0:T(4,128)S(1)}, f32[1,2,4,128]{3,2,1,0:T(4,128)S(1)}, u32[]{:S(2)}, u32[]{:S(2)}) collective-permute-start(f32[1,2,4,128]{3,2,1,0:T(4,128)S(1)} %bitcast.49), channel_id=1, source_target_pairs={{0,2},{2,0},{4,6},{6,4},{8,10},{10,8},{12,14},{14,12},{1,3},{3,1},... | collective-permute-start | bytes 12296 | tf_op jit(solution)/shard_map/ppermute | solution.py:384
  39.7 1.9 %collective-permute-done.4 = f32[1,2,4,128]{3,2,1,0:T(4,128)S(1)} collective-permute-done((f32[1,2,4,128]{3,2,1,0:T(4,128)S(1)}, f32[1,2,4,128]{3,2,1,0:T(4,128)S(1)}, u32[]{:S(2)}, u32[]{:S(2)}) %collective-permute-start.4) | collective-permute-done | bytes 4128 | tf_op jit(solution)/shard_map/ppermute | solution.py:384
  42.5 2.8 %collective-permute-done.5 = f32[2,2,4,128]{3,2,1,0:T(4,128)S(1)} collective-permute-done((f32[2,2,4,128]{3,2,1,0:T(4,128)S(1)}, f32[2,2,4,128]{3,2,1,0:T(4,128)S(1)}, u32[]{:S(2)}, u32[]{:S(2)}) %collective-permute-start.5) | collective-permute-done | bytes 8224 | tf_op jit(solution)/shard_map/ppermute | solution.py:384
  45.3 3.2 %collective-permute-start.6 = (f32[4,2,4,128]{3,2,1,0:T(4,128)S(1)}, f32[4,2,4,128]{3,2,1,0:T(4,128)S(1)}, u32[]{:S(2)}, u32[]{:S(2)}) collective-permute-start(f32[4,2,4,128]{3,2,1,0:T(4,128)S(1)} %pad_maximum_fusion.2), channel_id=1, source_target_pairs={{0,8},{2,10},{4,12},{6,14},{8,0},{10,2},{12,4},{14,6},{1,9},{3,11}... | collective-permute-start | bytes 49160 | tf_op jit(solution)/shard_map/ppermute | solution.py:384
  55.0 1.7 %copy-done.3 = f32[128,5120]{1,0:T(8,128)S(1)} copy-done((f32[128,5120]{1,0:T(8,128)S(1)}, f32[128,5120]{1,0:T(8,128)}, u32[]{:S(2)}) %copy-start.3) | copy-done | bytes 2621464
  56.7 5.9 %exponentials.2 = (f32[128,5120]{1,0:T(8,128)S(1)}, f32[128,256]{1,0:T(8,128)S(1)}, f32[128,128]{1,0:T(8,128)S(1)}) custom-call(f32[128,5120]{1,0:T(8,128)S(1)} %copy-done.3, f32[128,5120]{1,0:T(8,128)} %collective-permute-done.7.refs_1_, s32[16,256]{1,0:T(8,128)S(1)} %sub.64.refs_2_.ids_ref), custom_call_target="tpu_custom_call" | custom-call | flops 5242880 | bytes 7864320 | tf_op jit(solution)/shard_map/exponentials/pallas_call | solution.py:172
  64.2 6.7 %exponentials.3 = (f32[128,4608]{1,0:T(8,128)S(1)}, f32[128,256]{1,0:T(8,128)S(1)}, f32[128,128]{1,0:T(8,128)S(1)}, f32[8,128]{1,0:T(8,128)S(1)}) custom-call(f32[128,4608]{1,0:T(8,128)S(1)} %get-tuple-element.15.refs_0_, f32[128,4608]{1,0:T(8,128)} %collective-permute-done.3.refs_1_, s32[16,256]{1,0:T(8,128)S(1)} %sub.64.refs_2_.ids_ref, ...), custom_call_target="tpu_custom_call" | custom-call | flops 4718592 | bytes 7077888 | tf_op jit(solution)/shard_map/exponentials/pallas_call | solution.py:172
  73.9 2.1 %collective-permute-done.8 = f32[4,128]{1,0:T(4,128)S(1)} collective-permute-done((f32[4,128]{1,0:T(4,128)S(1)}, f32[4,128]{1,0:T(4,128)S(1)}, u32[]{:S(2)}, u32[]{:S(2)}) %collective-permute-start.8) | collective-permute-done | bytes 2080 | tf_op jit(solution)/shard_map/ppermute | solution.py:398
  77.5 2.2 %collective-permute-done.9 = f32[4,128]{1,0:T(4,128)S(1)} collective-permute-done((f32[4,128]{1,0:T(4,128)S(1)}, f32[4,128]{1,0:T(4,128)S(1)}, u32[]{:S(2)}, u32[]{:S(2)}) %collective-permute-start.9) | collective-permute-done | bytes 2080 | tf_op jit(solution)/shard_map/ppermute | solution.py:398
  79.7 3.1 %collective-permute-start.10 = (f32[4,128]{1,0:T(4,128)S(1)}, f32[4,128]{1,0:T(4,128)S(1)}, u32[]{:S(2)}, u32[]{:S(2)}) collective-permute-start(f32[4,128]{1,0:T(4,128)S(1)} %pad_maximum_fusion.6), channel_id=1, source_target_pairs={{0,8},{2,10},{4,12},{6,14},{8,0},{10,2},{12,4},{14,6},{1,9},{3,11}... | collective-permute-start | bytes 6152 | tf_op jit(solution)/shard_map/ppermute | solution.py:398
  86.1 3.5 %logit_grad.3.refs_0_.own_ref = bf16[128,5120]{1,0:T(8,128)(2,1)S(1)} custom-call(f32[128,5120]{1,0:T(8,128)S(1)} %copy-done.1, f32[128,128]{1,0:T(8,128)S(1)} %get-tuple-element.20.refs_5_.stat_ref, f32[128,256]{1,0:T(8,128)S(1)} %get-tuple-element.23.picks_ref, s32[16,256]{1,0:T(8,128)S(1)} %sub.64.refs_2_.ids_ref, f32[16,256]{1,0:T(8,128)S(1)} %squeeze.2.refs_3_.lps_ref, ...), custom_call_target="tpu_custom_call" | custom-call | flops 5242880 | bytes 3932160 | tf_op jit(solution)/shard_map/logit_grad/pallas_call | solution.py:257
  89.7 3.5 %logit_grad.2.refs_1_.own_ref = bf16[128,4608]{1,0:T(8,128)(2,1)S(1)} custom-call(f32[128,4608]{1,0:T(8,128)S(1)} %copy-done.5, f32[128,128]{1,0:T(8,128)S(1)} %get-tuple-element.22.stat_ref, f32[128,256]{1,0:T(8,128)S(1)} %get-tuple-element.23.picks_ref, s32[16,256]{1,0:T(8,128)S(1)} %sub.64.refs_2_.ids_ref, f32[16,256]{1,0:T(8,128)S(1)} %squeeze.2.refs_3_.lps_ref, ...), custom_call_target="tpu_custom_call" | custom-call | flops 4718592 | bytes 3538944 | tf_op jit(solution)/shard_map/logit_grad/pallas_call | solution.py:257
  93.8 6.9 %feature_terms.2.refs_4_ = f32[256,1024]{1,0:T(8,128)S(1)} custom-call(bf16[128,5120]{1,0:T(8,128)(2,1)S(1)} %logit_grad.3.refs_0_.own_ref, bf16[128,5120]{1,0:T(8,128)(2,1)} %collective-permute-done.12.refs_1_.other_ref, bf16[1024,9728]{1,0:T(8,128)(2,1)} %refs_3_.1), custom_call_target="tpu_custom_call" | custom-call | flops 2684354560 | bytes 13107200 | tf_op jit(solution)/shard_map/feature_terms/pallas_call | solution.py:318
  100.7 7.2 %feature_terms.3 = (f32[128,1024]{1,0:T(8,128)S(1)}, bf16[128,1024]{1,0:T(8,128)(2,1)}) custom-call(s32[8]{0:T(128)S(1)} %xor_xor_fusion.refs_0_, bf16[128,4608]{1,0:T(8,128)(2,1)S(1)} %logit_grad.2.refs_1_.own_ref, bf16[128,4608]{1,0:T(8,128)(2,1)} %collective-permute-done.11.refs_2_.other_ref, bf16[1024,9728]{1,0:T(8,128)(2,1)} %refs_3_.1, ...), custom_call_target="tpu_custom_call" | custom-call | flops 2415919104 | bytes 11796480 | tf_op jit(solution)/shard_map/feature_terms/pallas_call | solution.py:318
  110.4 7.0 %weight_grad.2.refs_0_ = bf16[1024,9728]{1,0:T(8,128)(2,1)} custom-call(bf16[1024,256]{1,0:T(8,128)(2,1)S(1)} %bitcast.46, bf16[128,5120]{1,0:T(8,128)(2,1)S(1)} %logit_grad.3.refs_0_.own_ref, bf16[128,5120]{1,0:T(8,128)(2,1)} %collective-permute-done.12.refs_1_.other_ref), custom_call_target="tpu_custom_call" | custom-call | flops 2684354560 | bytes 13107200 | tf_op jit(solution)/shard_map/weight_grad/pallas_call | solution.py:347
  120.0 2.9 %collective-permute-start.16 = (bf16[32,1024]{1,0:T(8,128)(2,1)S(1)}, bf16[32,1024]{1,0:T(8,128)(2,1)S(1)}, u32[]{:S(2)}, u32[]{:S(2)}) collective-permute-start(bf16[32,1024]{1,0:T(8,128)(2,1)S(1)} %get-tuple-element.37), channel_id=1, source_target_pairs={{0,12},{2,14},{4,8},{6,10},{8,4},{10,6},{12,0},{14,2},{1,13},{3,15... | collective-permute-start | bytes 196616 | tf_op jit(solution)/shard_map/ppermute | solution.py:416
  123.0 6.3 %weight_grad.3 = bf16[1024,9728]{1,0:T(8,128)(2,1)} custom-call(bf16[1024,256]{1,0:T(8,128)(2,1)S(1)} %bitcast.47, bf16[128,4608]{1,0:T(8,128)(2,1)S(1)} %logit_grad.2.refs_1_.own_ref, bf16[128,4608]{1,0:T(8,128)(2,1)} %collective-permute-done.11.refs_2_.other_ref, bf16[1024,9728]{1,0:T(8,128)(2,1)} %weight_grad.2.refs_0_), custom_call_target="tpu_custom_call", output_to_operand_aliasing={{}: (3, {})} | custom-call | flops 2415919104 | bytes 11796480 | tf_op jit(solution)/shard_map/weight_grad/pallas_call | solution.py:347
  (80 shorter events, 27.0 us)
Async XLA Ops:
  0.6 8.0 %collective-permute-start = (bf16[1,32,1024]{2,1,0:T(8,128)(2,1)}, bf16[1,32,1024]{2,1,0:T(8,128)(2,1)S(1)}, u32[]{:S(2)}, u32[]{:S(2)}) collective-permute-start(bf16[1,32,1024]{2,1,0:T(8,128)(2,1)} %bitcast.53), channel_id=1, source_target_pairs={{0,8},{2,10},{4,12},{6,14},{8,0},{10,2},{12,4},{14,6},{1,9},{3,11}... | collective-permute-start | bytes 196616 | tf_op jit(solution)/shard_map/ppermute | solution.py:372
  9.5 5.0 %collective-permute-start.1 = (bf16[2,32,1024]{2,1,0:T(8,128)(2,1)S(1)}, bf16[2,32,1024]{2,1,0:T(8,128)(2,1)S(1)}, u32[]{:S(2)}, u32[]{:S(2)}) collective-permute-start(bf16[2,32,1024]{2,1,0:T(8,128)(2,1)S(1)} %maximum_bitcast_fusion), channel_id=1, source_target_pairs={{0,4},{2,6},{4,0},{6,2},{8,12},{10,14},{12,8},{14,10},{1,5},{3,7},... | collective-permute-start | bytes 393224 | tf_op jit(solution)/shard_map/ppermute | solution.py:372
  14.6 6.4 %collective-permute-start.2 = (bf16[4,32,1024]{2,1,0:T(8,128)(2,1)S(1)}, bf16[4,32,1024]{2,1,0:T(8,128)(2,1)S(1)}, u32[]{:S(2)}, u32[]{:S(2)}) collective-permute-start(bf16[4,32,1024]{2,1,0:T(8,128)(2,1)S(1)} %bitcast.48), channel_id=1, source_target_pairs={{0,2},{2,0},{4,6},{6,4},{8,10},{10,8},{12,14},{14,12},{1,3},{3,1},... | collective-permute-start | bytes 786440 | tf_op jit(solution)/shard_map/ppermute | solution.py:372
  30.1 7.8 %copy-start.8 = (s32[128,4]{0,1:T(4,128)S(1)}, s32[128,4]{0,1:T(4,128)}, u32[]{:S(2)}) copy-start(s32[128,4]{0,1:T(4,128)} %param.8) | copy-start | bytes 6148
  30.1 7.8 %copy-start.9 = (f32[128,4]{0,1:T(4,128)S(1)}, f32[128,4]{0,1:T(4,128)}, u32[]{:S(2)}) copy-start(f32[128,4]{0,1:T(4,128)} %param.9) | copy-start | bytes 6148
  30.1 24.9 %collective-permute-start.7 = (f32[128,5120]{1,0:T(8,128)}, f32[128,5120]{1,0:T(8,128)}, u32[]{:S(2)}, u32[]{:S(2)}) collective-permute-start(f32[128,5120]{1,0:T(8,128)} %get-tuple-element.18), channel_id=1, source_target_pairs={{0,1},{1,0},{2,3},{3,2},{4,5},{5,4},{6,7},{7,6},{8,9},{9,8},{10,11... | collective-permute-start | bytes 7864328 | tf_op jit(solution)/shard_map/ppermute | solution.py:392
  37.4 26.7 %collective-permute-start.3 = (f32[128,4608]{1,0:T(8,128)}, f32[128,4608]{1,0:T(8,128)}, u32[]{:S(2)}, u32[]{:S(2)}) collective-permute-start(f32[128,4608]{1,0:T(8,128)} %get-tuple-element.16), channel_id=1, source_target_pairs={{0,1},{1,0},{2,3},{3,2},{4,5},{5,4},{6,7},{7,6},{8,9},{9,8},{10,11... | collective-permute-start | bytes 7077896 | tf_op jit(solution)/shard_map/ppermute | solution.py:392
  37.9 3.7 %collective-permute-start.4 = (f32[1,2,4,128]{3,2,1,0:T(4,128)S(1)}, f32[1,2,4,128]{3,2,1,0:T(4,128)S(1)}, u32[]{:S(2)}, u32[]{:S(2)}) collective-permute-start(f32[1,2,4,128]{3,2,1,0:T(4,128)S(1)} %bitcast.49), channel_id=1, source_target_pairs={{0,2},{2,0},{4,6},{6,4},{8,10},{10,8},{12,14},{14,12},{1,3},{3,1},... | collective-permute-start | bytes 12296 | tf_op jit(solution)/shard_map/ppermute | solution.py:384
  41.6 3.7 %collective-permute-start.5 = (f32[2,2,4,128]{3,2,1,0:T(4,128)S(1)}, f32[2,2,4,128]{3,2,1,0:T(4,128)S(1)}, u32[]{:S(2)}, u32[]{:S(2)}) collective-permute-start(f32[2,2,4,128]{3,2,1,0:T(4,128)S(1)} %pad_maximum_fusion.3), channel_id=1, source_target_pairs={{0,4},{2,6},{4,0},{6,2},{8,12},{10,14},{12,8},{14,10},{1,5},{3,7},... | collective-permute-start | bytes 24584 | tf_op jit(solution)/shard_map/ppermute | solution.py:384
  45.3 5.0 %collective-permute-start.6 = (f32[4,2,4,128]{3,2,1,0:T(4,128)S(1)}, f32[4,2,4,128]{3,2,1,0:T(4,128)S(1)}, u32[]{:S(2)}, u32[]{:S(2)}) collective-permute-start(f32[4,2,4,128]{3,2,1,0:T(4,128)S(1)} %pad_maximum_fusion.2), channel_id=1, source_target_pairs={{0,8},{2,10},{4,12},{6,14},{8,0},{10,2},{12,4},{14,6},{1,9},{3,11}... | collective-permute-start | bytes 49160 | tf_op jit(solution)/shard_map/ppermute | solution.py:384
  64.2 18.6 %copy-start.10 = (f32[128]{0:T(128)S(1)}, f32[128]{0:T(128)}, u32[]{:S(2)}) copy-start(f32[128]{0:T(128)} %param.11) | copy-start | bytes 1540
  64.2 18.6 %copy-start.11 = (s32[128]{0:T(128)S(1)}, s32[128]{0:T(128)}, u32[]{:S(2)}) copy-start(s32[128]{0:T(128)} %param.10) | copy-start | bytes 1540
  72.4 3.6 %collective-permute-start.8 = (f32[4,128]{1,0:T(4,128)S(1)}, f32[4,128]{1,0:T(4,128)S(1)}, u32[]{:S(2)}, u32[]{:S(2)}) collective-permute-start(f32[4,128]{1,0:T(4,128)S(1)} %slice.93), channel_id=1, source_target_pairs={{0,2},{2,0},{4,6},{6,4},{8,10},{10,8},{12,14},{14,12},{1,3},{3,1},... | collective-permute-start | bytes 6152 | tf_op jit(solution)/shard_map/ppermute | solution.py:398
  76.0 3.7 %collective-permute-start.9 = (f32[4,128]{1,0:T(4,128)S(1)}, f32[4,128]{1,0:T(4,128)S(1)}, u32[]{:S(2)}, u32[]{:S(2)}) collective-permute-start(f32[4,128]{1,0:T(4,128)S(1)} %pad_maximum_fusion.5), channel_id=1, source_target_pairs={{0,4},{2,6},{4,0},{6,2},{8,12},{10,14},{12,8},{14,10},{1,5},{3,7},... | collective-permute-start | bytes 6152 | tf_op jit(solution)/shard_map/ppermute | solution.py:398
  79.7 4.7 %collective-permute-start.10 = (f32[4,128]{1,0:T(4,128)S(1)}, f32[4,128]{1,0:T(4,128)S(1)}, u32[]{:S(2)}, u32[]{:S(2)}) collective-permute-start(f32[4,128]{1,0:T(4,128)S(1)} %pad_maximum_fusion.6), channel_id=1, source_target_pairs={{0,8},{2,10},{4,12},{6,14},{8,0},{10,2},{12,4},{14,6},{1,9},{3,11}... | collective-permute-start | bytes 6152 | tf_op jit(solution)/shard_map/ppermute | solution.py:398
  84.4 1.7 %copy-start.1 = (f32[128,5120]{1,0:T(8,128)S(1)}, f32[128,5120]{1,0:T(8,128)}, u32[]{:S(2)}) copy-start(f32[128,5120]{1,0:T(8,128)} %copy-done) | copy-start | bytes 7864324
  86.1 3.6 %copy-start.5 = (f32[128,4608]{1,0:T(8,128)S(1)}, f32[128,4608]{1,0:T(8,128)}, u32[]{:S(2)}) copy-start(f32[128,4608]{1,0:T(8,128)} %copy-done.4) | copy-start | bytes 7077892
  89.6 4.1 %collective-permute-start.12 = (bf16[128,5120]{1,0:T(8,128)(2,1)S(1)}, bf16[128,5120]{1,0:T(8,128)(2,1)}, u32[]{:S(2)}, u32[]{:S(2)}) collective-permute-start(bf16[128,5120]{1,0:T(8,128)(2,1)S(1)} %logit_grad.3.refs_0_.own_ref), channel_id=1, source_target_pairs={{0,1},{1,0},{2,3},{3,2},{4,5},{5,4},{6,7},{7,6},{8,9},{9,8},{10,11... | collective-permute-start | bytes 3932168 | tf_op jit(solution)/shard_map/ppermute | solution.py:405
  93.2 7.5 %collective-permute-start.11 = (bf16[128,4608]{1,0:T(8,128)(2,1)S(1)}, bf16[128,4608]{1,0:T(8,128)(2,1)}, u32[]{:S(2)}, u32[]{:S(2)}) collective-permute-start(bf16[128,4608]{1,0:T(8,128)(2,1)S(1)} %logit_grad.2.refs_1_.own_ref), channel_id=1, source_target_pairs={{0,1},{1,0},{2,3},{3,2},{4,5},{5,4},{6,7},{7,6},{8,9},{9,8},{10,11... | collective-permute-start | bytes 3538952 | tf_op jit(solution)/shard_map/ppermute | solution.py:405
  108.7 8.7 %collective-permute-start.13 = (bf16[128,1024]{1,0:T(8,128)(2,1)}, bf16[128,1024]{1,0:T(8,128)(2,1)}, u32[]{:S(2)}, u32[]{:S(2)}) collective-permute-start(bf16[128,1024]{1,0:T(8,128)(2,1)} %get-tuple-element.27), channel_id=1, source_target_pairs={{0,2},{2,0},{4,6},{6,4},{8,10},{10,8},{12,14},{14,12},{1,3},{3,1},... | collective-permute-start | bytes 786440 | tf_op jit(solution)/shard_map/ppermute | solution.py:412
  110.4 7.0 %copy-start.7 = (f32[128,1024]{1,0:T(8,128)S(1)}, f32[128,1024]{1,0:T(8,128)}, u32[]{:S(2)}) copy-start(f32[128,1024]{1,0:T(8,128)} %copy-done.6) | copy-start | bytes 1572868
  118.5 10.8 %collective-permute-start.14 = (bf16[32,1024]{1,0:T(8,128)(2,1)S(1)}, bf16[32,1024]{1,0:T(8,128)(2,1)S(1)}, u32[]{:S(2)}, u32[]{:S(2)}) collective-permute-start(bf16[32,1024]{1,0:T(8,128)(2,1)S(1)} %get-tuple-element.36), channel_id=1, source_target_pairs={{0,4},{2,6},{4,0},{6,2},{8,12},{10,14},{12,8},{14,10},{1,5},{3,7},... | collective-permute-start | bytes 196616 | tf_op jit(solution)/shard_map/ppermute | solution.py:416
  120.0 9.2 %collective-permute-start.16 = (bf16[32,1024]{1,0:T(8,128)(2,1)S(1)}, bf16[32,1024]{1,0:T(8,128)(2,1)S(1)}, u32[]{:S(2)}, u32[]{:S(2)}) collective-permute-start(bf16[32,1024]{1,0:T(8,128)(2,1)S(1)} %get-tuple-element.37), channel_id=1, source_target_pairs={{0,12},{2,14},{4,8},{6,10},{8,4},{10,6},{12,0},{14,2},{1,13},{3,15... | collective-permute-start | bytes 196616 | tf_op jit(solution)/shard_map/ppermute | solution.py:416
  122.9 6.4 %collective-permute-start.15 = (bf16[32,1024]{1,0:T(8,128)(2,1)S(1)}, bf16[32,1024]{1,0:T(8,128)(2,1)S(1)}, u32[]{:S(2)}, u32[]{:S(2)}) collective-permute-start(bf16[32,1024]{1,0:T(8,128)(2,1)S(1)} %get-tuple-element.38), channel_id=1, source_target_pairs={{0,8},{2,10},{4,12},{6,14},{8,0},{10,2},{12,4},{14,6},{1,9},{3,11}... | collective-permute-start | bytes 196616 | tf_op jit(solution)/shard_map/ppermute | solution.py:416
  (5 other events, 7.0 us)

commit v2 on v0

v2 whole, which is shorter than its diff:
```python
import functools

import jax
import jax.numpy as jnp
from jax import lax
from jax.experimental import pallas as pl
from jax.experimental.pallas import tpu as pltpu
from jax.sharding import PartitionSpec as P

VMEM_LIMIT = 14 * 1024 * 1024
TILE = 8
STEP = 16
NT = (((1,), (1,)), ((), ()))
F32 = jnp.float32
BF16 = jnp.bfloat16
LOCAL = pl.BlockSpec(memory_space=pltpu.VMEM)
WRITES = 4


def _local(x):
    return pltpu.with_memory_space_constraint(x, pltpu.VMEM)


def _cost(flops, nbytes):
    return pl.CostEstimate(flops=int(flops), bytes_accessed=int(nbytes), transcendentals=0)


def _call(body, name, args, out_shape, cost, specs=None, out_specs=None, scratch=(), aliases=None):
    specs = specs or [LOCAL] * len(args)
    args = [_local(x) if s is LOCAL else x for x, s in zip(args, specs)]
    return pl.pallas_call(
        body,
        in_specs=specs,
        out_specs=out_specs or [LOCAL] * len(out_shape),
        out_shape=out_shape,
        scratch_shapes=list(scratch),
        input_output_aliases=aliases or {},
        compiler_params=pltpu.CompilerParams(vmem_limit_bytes=VMEM_LIMIT),
        cost_estimate=cost,
        name=name,
    )(*args)


def _split(width, count):
    unit = 256 if width % 256 == 0 else 128
    units = width // unit
    ends = [units * (i + 1) // count for i in range(count)]
    starts = [0] + ends[:-1]
    return [(a * unit, (b - a) * unit) for a, b in zip(starts, ends)]


def _blocks(width, block):
    return [(a, min(block, width - a)) for a in range(0, width, block)]


def _xor(n, s):
    return [(i, i ^ s) for i in range(n)]


def _logits_body(start, h_ref, w_ref, own_ref, send_ref):
    half = own_ref.shape[0]
    for at, size in _blocks(own_ref.shape[1], 1280):
        part = jnp.dot(h_ref[...], w_ref[:, start + at : start + at + size], preferred_element_type=F32)
        own_ref[:, at : at + size] = part[:half]
        send_ref[:, at : at + size] = part[half:]


def _partial_logits(h, w, chunk):
    start, width = chunk
    rows, depth = h.shape
    out = pltpu.VMEM((rows // 2, width), F32)
    return _call(
        functools.partial(_logits_body, start),
        "partial_logits",
        [h, w],
        [out, out],
        _cost(2 * rows * depth * width, 2 * depth * width + 4 * rows * width),
    )


def _exp_body(start, width, index, count, terms, *refs):
    first, last = index == 0, index == count - 1
    refs = list(refs)
    own_ref, recv_ref = refs.pop(0), refs.pop(0)
    if first:
        packed_ref = refs.pop(0)
    else:
        ids_ref, lps_ref, picks_in = refs.pop(0), refs.pop(0), refs.pop(0)
    before = [refs.pop(0) for _ in range(index)] if last else []
    e_ref, picks_ref, stat_ref = refs.pop(0), refs.pop(0), refs.pop(0)
    half = own_ref.shape[0]
    if first:
        ids_ref, lps_ref = refs.pop(0), refs.pop(0)
        pad = jnp.full((128 - terms, half), -1.0, F32)
        ids_ref[...] = jnp.concatenate([packed_ref[0], pad], axis=0).T.astype(jnp.int32)
        lps_ref[...] = jnp.concatenate([packed_ref[1], pad], axis=0).T
    if last:
        tot_ref, hold = refs
    lane = lax.broadcasted_iota(jnp.int32, (TILE, 128), 1)
    ways = 4

    def tile(t, carry):
        rows = pl.ds(pl.multiple_of(t * TILE, TILE), TILE)
        ids = ids_ref[rows, :]
        rel = ids - start
        key = rel >> 7
        slot = rel & 127
        acc = [jnp.zeros((TILE, 128), F32)] * ways
        top = [jnp.full((TILE, 128), -jnp.inf, F32)] * ways
        for c in range(width // 128):
            cols = slice(c * 128, (c + 1) * 128)
            w = c % ways
            logit = own_ref[rows, cols] + recv_ref[rows, cols]
            e_ref[rows, cols] = logit
            top[w] = jnp.maximum(top[w], logit)
            got = jnp.take_along_axis(logit, slot, axis=1, mode="promise_in_bounds")
            acc[w] = jnp.where(key == c, got, acc[w])
        top = functools.reduce(jnp.maximum, top)
        top = jnp.max(top, axis=1, keepdims=True)
        total = [jnp.zeros((TILE, 128), F32)] * ways
        for c in range(width // 128):
            cols = slice(c * 128, (c + 1) * 128)
            e = jnp.exp(e_ref[rows, cols] - top)
            e_ref[rows, cols] = e
            total[c % ways] += e
        total = jnp.sum(sum(total), axis=1, keepdims=True)
        picked = sum(acc)
        if not first:
            picked = picked + picks_in[rows, :]
        picks_ref[rows, :] = picked
        stat_ref[rows, :] = jnp.where(lane == 0, top, total)
        if last:
            tops, totals = [top], [total]
            for ref in before:
                tops.append(ref[rows, 0:1])
                totals.append(ref[rows, 1:2])
            both = functools.reduce(jnp.maximum, tops)
            total = sum(s * jnp.exp(m - both) for m, s in zip(tops, totals))
            inside = (ids >= 0) & (ids < start + width)
            weight = jnp.where(inside, jnp.exp(picked - both), 0.0)
            mixed = jnp.sum(weight * (picked - both - lps_ref[rows, :] + 1.0), axis=1, keepdims=True)
            plain = jnp.sum(weight, axis=1, keepdims=True)
            hold[rows, :] = jnp.where(
                lane == 0, both, jnp.where(lane == 1, total, jnp.where(lane == 2, mixed, plain))
            )
        return carry

    lax.fori_loop(0, half // TILE, tile, 0, unroll=2)
    if last:
        tot_ref[...] = hold[...].T[:TILE, :]


def _exponentials(own, recv, chunks, index, terms, packed=None, rows=None, picks=None, before=()):
    start, width = chunks[index]
    half = own.shape[0]
    first, last = index == 0, index == len(chunks) - 1
    table = pltpu.VMEM((half, 128), F32)
    args = [own, recv] + ([packed] if first else [*rows, picks]) + (list(before) if last else [])
    out = [pltpu.VMEM((half, width), F32), table, table]
    scratch = []
    if first:
        out += [pltpu.VMEM((half, 128), jnp.int32), table]
    if last:
        out.append(pltpu.VMEM((TILE, half), F32))
        scratch = [pltpu.VMEM((half, 128), F32)]
    return _call(
        functools.partial(_exp_body, start, width, index, len(chunks), terms),
        "exponentials",
        args,
        out,
        _cost(8 * half * width, 12 * half * width),
        scratch=scratch,
    )


def _join_stats(a, b):
    top = jnp.maximum(a[0], b[0])
    da, db = a[0] - top, b[0] - top
    fa, fb = jnp.exp(da), jnp.exp(db)
    return jnp.stack(
        [
            top,
            a[1] * fa + b[1] * fb,
            (a[2] + da * a[3]) * fa + (b[2] + db * b[3]) * fb,
            a[3] * fa + b[3] * fb,
        ]
    )


def _grad_body(chunks, terms, *refs):
    count = len(chunks)
    e_refs, stat_refs = refs[:count], refs[count : 2 * count]
    picks_ref, ids_ref, lps_ref, tot_ref, g_ref, hold = refs[2 * count :]
    half = tot_ref.shape[1]
    lanes = TILE * terms
    hold[...] = jnp.concatenate([tot_ref[...], jnp.zeros((128 - TILE, half), F32)], axis=0).T
    lane_row = lax.broadcasted_iota(jnp.int32, (TILE, lanes), 1) // terms
    mask = lane_row == lax.broadcasted_iota(jnp.int32, (TILE, lanes), 0)
    place = lax.broadcasted_iota(jnp.int32, (256, lanes), 0)
    begin = chunks[0][0]
    width = sum(w for _, w in chunks)
    parts = (width + 255) // 256

    def flat(x):
        return jnp.concatenate([x[:, :terms]] * TILE, axis=1)

    def tile(t):
        rows = pl.ds(pl.multiple_of(t * TILE, TILE), TILE)
        tot = hold[rows, :]
        top, total, mixed, plain, scale = (tot[:, i : i + 1] for i in range(5))
        log_sum = jnp.log(total)
        lse = top + log_sum
        sum_grad = scale * jnp.exp(-log_sum) * (mixed - log_sum * plain)
        coefs = [sum_grad * jnp.exp(ref[rows, 0:1] - lse) for ref in stat_refs]
        rel = ids_ref[rows, :] - begin
        inside = (rel >= 0) & (rel < width)
        support = picks_ref[rows, :] - lse
        grad = scale * jnp.exp(support) * (support - lps_ref[rows, :] + 1.0)
        grad = jnp.where(inside, grad, 0.0)
        high = grad.astype(BF16).astype(F32)
        key = jnp.where(mask, flat(jnp.where(inside, rel >> 8, -1)), -1)
        col = jnp.where(mask, flat(rel & 255), 0)
        col = jnp.sum(col, axis=0, keepdims=True)
        high, low = flat(high), flat(grad - high)
        lhs = jnp.concatenate(
            [
                jnp.concatenate([jnp.where(key == c, high, 0.0), jnp.where(key == c, low, 0.0)], axis=1)
                for c in range(parts)
            ],
            axis=0,
        ).astype(BF16)
        hot = (place == jnp.broadcast_to(col, (256, lanes))).astype(F32).astype(BF16)
        rhs = jnp.concatenate([hot, hot], axis=1)
        return rows, coefs, lax.dot_general(lhs, rhs, NT, preferred_element_type=F32)

    def step(i, carry):
        pair = [tile(i * (STEP // TILE) + t) for t in range(STEP // TILE)]
        out_rows = pl.ds(pl.multiple_of(i * STEP, STEP), STEP)
        for q, (start, w) in enumerate(chunks):
            for at, size in _blocks(w, 128):
                col = start - begin + at
                c, off = col // 256, col % 256
                out = [
                    s[c * TILE : (c + 1) * TILE, off : off + size] - e_refs[q][rows, at : at + size] * coefs[q]
                    for rows, coefs, s in pair
                ]
                g_ref[out_rows, col : col + size] = jnp.concatenate(out, axis=0).astype(BF16)
        return carry

    lax.fori_loop(0, half // STEP, step, 0)


def _logit_grad(es, stats, picks, ids, lps, tot, chunks, terms):
    half = es[0].shape[0]
    width = sum(w for _, w in chunks)
    return _call(
        functools.partial(_grad_body, chunks, terms),
        "logit_grad",
        [*es, *stats, picks, ids, lps, tot],
        [pltpu.VMEM((half, width), BF16)],
        _cost(8 * half * width, 6 * half * width),
        scratch=[pltpu.VMEM((half, 128), F32)],
    )[0]


def _feature_body(start, count, *refs):
    if count:
        own_ref, other_ref, w_ref, before_ref, order_ref, keep_ref, send_ref, acc = refs
    else:
        own_ref, other_ref, w_ref, acc = refs
    width = own_ref.shape[1]
    grads = jnp.concatenate([own_ref[...], other_ref[...]], axis=0)
    part = lax.dot_general(grads, w_ref[:, start : start + width], NT, preferred_element_type=F32)
    if not count:
        acc[...] = part
        return
    acc[...] = part + before_ref[...]
    rows = acc.shape[0] // count
    near, far = [], []
    for d in range(count):
        at = pl.multiple_of(order_ref[d] * rows, rows)
        (far if d % 2 else near).append(acc[pl.ds(at, rows), :])
    keep_ref[...] = jnp.concatenate(near, axis=0)
    send_ref[...] = jnp.concatenate(far, axis=0).astype(BF16)


def _feature_terms(own, other, w, start, before=None, order=None):
    half, width = own.shape
    depth = w.shape[0]
    args = [own, other, w]
    specs = [LOCAL] * 3
    scratch = []
    out = [pltpu.VMEM((2 * half, depth), F32)]
    if before is not None:
        args += [before, order]
        specs += [LOCAL, pl.BlockSpec(memory_space=pltpu.SMEM)]
        scratch = out
        out = [pltpu.VMEM((half, depth), F32), pltpu.VMEM((half, depth), BF16)]
    return _call(
        functools.partial(_feature_body, start, 0 if before is None else order.shape[0]),
        "feature_terms",
        args,
        out,
        _cost(4 * half * depth * width, 2 * depth * width + 4 * half * width),
        specs=specs,
        scratch=scratch,
    )


def _weight_body(start, block, ht_ref, own_ref, other_ref, *refs):
    out_ref, ring, sems = refs[-3:]
    copies = []
    for i, (at, size) in enumerate(_blocks(own_ref.shape[1], block)):
        slot = i % WRITES
        if i >= WRITES:
            copies[i - WRITES].wait()
        cols = slice(at, at + size)
        grads = jnp.concatenate([own_ref[:, cols], other_ref[:, cols]], axis=0)
        ring[slot, :, :size] = jnp.dot(ht_ref[...], grads, preferred_element_type=F32).astype(BF16)
        copy = pltpu.make_async_copy(
            ring.at[slot, :, pl.ds(0, size)], out_ref.at[:, pl.ds(start + at, size)], sems.at[slot]
        )
        copy.start()
        copies.append(copy)
    for copy in copies[-WRITES:]:
        copy.wait()


def _weight_grad(ht, own, other, start, width_all, before=None):
    depth, rows = ht.shape
    width = own.shape[1]
    block = 512
    args = [ht, own, other]
    specs = [LOCAL] * 3
    aliases = {}
    if before is not None:
        args.append(before)
        specs.append(pl.BlockSpec(memory_space=pl.ANY))
        aliases = {3: 0}
    return _call(
        functools.partial(_weight_body, start, block),
        "weight_grad",
        args,
        [jax.ShapeDtypeStruct((depth, width_all), BF16)],
        _cost(2 * rows * depth * width, 2 * depth * width + 2 * rows * width),
        specs=specs,
        out_specs=[pl.BlockSpec(memory_space=pl.ANY)],
        scratch=[pltpu.VMEM((WRITES, depth, block), BF16), pltpu.SemaphoreType.DMA((WRITES,))],
        aliases=aliases,
    )[0]


def per_device(hidden, head_weight, teacher_ids, teacher_logprobs, valid, row_weight):
    count = lax.axis_size("vocab")
    bits = count.bit_length() - 1
    r = lax.axis_index("row")
    v = lax.axis_index("vocab")
    width = head_weight.shape[1]
    half, own_terms = teacher_ids.shape
    terms = own_terms * count
    swap = [(0, 1), (1, 0)]
    chunks = _split(width, 4)
    groups = [[0, 1], [2, 3]]
    weights = _local(head_weight)

    h = hidden[None]
    packed = jnp.stack([teacher_ids.T.astype(F32), teacher_logprobs.T])
    for b in reversed(range(bits)):
        far = lax.ppermute(h, "vocab", _xor(count, 1 << b))
        far_packed = lax.ppermute(packed, "vocab", _xor(count, 1 << b))
        far, far_packed = lax.optimization_barrier((far, far_packed))
        bit = (v >> b) & 1
        first = bit == r if b == bits - 1 else bit == 0
        h = jnp.stack([jnp.where(first, h, far), jnp.where(first, far, h)], axis=1)
        h = h.reshape((-1,) + hidden.shape)
        packed = jnp.concatenate([packed, far_packed], axis=1)
    h = h.reshape(-1, hidden.shape[1])
    packed = packed - jnp.array([1.0, 0.0], F32)[:, None, None] * (v * width).astype(F32)
    h, packed = lax.optimization_barrier((h, packed))
    ht = h.T

    parts = []
    for chunk in chunks:
        own, send = _partial_logits(h, weights, chunk)
        parts.append((own, lax.ppermute(send, "row", swap)))
    es, stats = [], []
    picks = rows = None
    for i, (own, recv) in enumerate(parts):
        e, picks, stat, *rest = _exponentials(
            own, recv, chunks, i, terms, packed=packed, rows=rows, picks=picks, before=stats
        )
        if i == 0:
            rows = rest
        es.append(e)
        stats.append(stat)
    joined = rest[0][:4]
    ids, lps = rows

    for b in range(bits):
        joined = _join_stats(joined, lax.ppermute(joined, "vocab", _xor(count, 1 << b)))
    scale = row_weight * valid.astype(F32)
    tot = jnp.concatenate([joined, scale[None], jnp.zeros((3, half), F32)], axis=0)

    grads = []
    for group in groups:
        own = _logit_grad(
            [es[q] for q in group], [stats[q] for q in group], picks, ids, lps, tot, [chunks[q] for q in group], terms
        )
        grads.append((own, lax.ppermute(own, "row", swap)))

    order = (jnp.arange(count, dtype=jnp.int32) ^ v) ^ (r * (count // 2))
    starts = [chunks[group[0]][0] for group in groups]
    (before,) = _feature_terms(*grads[0], weights, starts[0])
    keep, send = _feature_terms(*grads[1], weights, starts[1], before, order)

    keep = keep + lax.ppermute(send, "vocab", _xor(count, 1)).astype(F32)
    keep = keep.reshape((count // 2,) + hidden.shape)
    total = keep[0]
    for d in range(1, count // 2):
        far = lax.ppermute(keep[d].astype(BF16), "vocab", _xor(count, 2 * d))
        total = total + far.astype(F32)
    hidden_grad = total.astype(BF16)

    weight_grad = _weight_grad(ht, *grads[0], starts[0], width)
    weight_grad = _weight_grad(ht, *grads[1], starts[1], width, weight_grad)
    return hidden_grad, weight_grad


def solution(mesh):
    return jax.shard_map(
        per_device,
        mesh=mesh,
        in_specs=(
            P(("grp", "vocab"), "row"),
            P("row", "vocab"),
            P(("grp", "row"), "vocab"),
            P(("grp", "row"), "vocab"),
            P(("grp", "row")),
            P(("grp", "row")),
        ),
        out_specs=(P(("grp", "vocab"), "row"), P(("grp", "row"), "vocab")),
        check_vma=False,
    )
```

time: 497 us -> 112 us (0.23)
  local copies, waits for them, and re-layouts: 198 us -> 19 us
  blocking collectives: 142 us -> 0 us
  Pallas kernels: 0 us -> 44 us
  matrix products: 41.4 us -> 0 us
  waiting for transfers between devices: 59.4 us -> 23.5 us
  other arithmetic: 37.9 us -> 4.94 us
  starting transfers between devices: 0.34 us -> 18.9 us
  between operations: 13.9 us -> 0.93 us
    gather x5 -> x0, local copies, waits for them, and re-layouts: 163 us -> none  [per_device(): jnp.take_along_axis(logits, safe_ids, axis=1)]
    all_gather x3 -> x0, blocking collectives: 87.4 us -> none  [the longest x1 35.4 us: per_device(): rows_all = lax.all_gather(hidden, 'vocab', axis=0, tiled=True)]
    pallas_call x0 -> x14, Pallas kernels: none -> 44 us  [_call(): pl.pallas_call(body, in_specs=specs, out_specs=out_specs or [LOCAL] * len...]
    dot_general x3 -> x0, matrix products: 41.4 us -> none  [the longest x1 17.6 us: per_device(): jnp.dot(mine, lax.all_gather(head_weight, 'row', axis=0, tiled=True), pre...]
    psum x1 -> x0, blocking collectives: 33 us -> none  [per_device(): summed, support_raw = lax.psum((local_sum, picked), 'vocab')]
    all_gather x3 -> x0, waiting for transfers between devices: 30.9 us -> none  [the longest x1 19.3 us: per_device(): lax.all_gather(head_weight, 'row', axis=0, tiled=True)]
    reduce_scatter x1 -> x0, waiting for transfers between devices: 27.7 us -> none  [per_device(): lax.psum_scatter(feature_terms, 'vocab', scatter_dimension=0, tiled=True)]
    unnamed x4 -> x0, other arithmetic: 24.8 us -> none
  transfers between devices with their start and end apart: 4 -> 19, of which waited for: 3 -> 8; matrix products, arithmetic and copies ran while one was open for 8% -> 2% of each run, Pallas kernels for 0% -> 26%
where the time goes in v2:
time: 112 us; the launch traced here: 111 us
  Pallas kernels  44 us (39%)
  waiting for transfers between devices  23.5 us (21%)
  local copies, waits for them, and re-layouts  19 us (17%)
  starting transfers between devices  18.9 us (17%)
  other arithmetic  4.94 us (4%)
    pallas_call x14, Pallas kernels, _call(): pl.pallas_call(body, in_specs=specs, out_specs=out_specs or [LOCAL] * len...  44 us
    unnamed x28, local copies, waits for them, and re-layouts  18.7 us
    ppermute x3, waiting for transfers between devices, per_device(): far_packed = lax.ppermute(packed, 'vocab', _xor(count, 1 << b))  12.1 us
    ppermute x3, waiting for transfers between devices, per_device(): lax.ppermute(joined, 'vocab', _xor(count, 1 << b))  8.23 us
    ppermute x3, starting transfers between devices, per_device(): far = lax.ppermute(h, 'vocab', _xor(count, 1 << b))  7.33 us
    ppermute x3, starting transfers between devices, per_device(): far = lax.ppermute(keep[d].astype(BF16), 'vocab', _xor(count, 2 * d))  3.55 us
    ppermute x3, starting transfers between devices, per_device(): lax.ppermute(joined, 'vocab', _xor(count, 1 << b))  3.54 us
    ppermute x4, waiting for transfers between devices, per_device(): parts.append((own, lax.ppermute(send, 'row', swap)))  2.67 us
  transfers between devices with their start and end apart: 19, of which 8 were waited for; matrix products, arithmetic and copies ran while one was open for 2% of the time, Pallas kernels for 26%

profile of v2, /device:TPU:0, one launch (start us, length us, event | category | flops | bytes accessed | tf_op | source)
XLA Modules:
  0.0 111.2 jit_solution(3981350138655486524)
XLA Ops:
  0.7 4.1 %collective-permute-start = (bf16[1,32,1024]{2,1,0:T(8,128)(2,1)}, bf16[1,32,1024]{2,1,0:T(8,128)(2,1)S(1)}, u32[]{:S(2)}, u32[]{:S(2)}) collective-permute-start(bf16[1,32,1024]{2,1,0:T(8,128)(2,1)} %bitcast.45), channel_id=1, source_target_pairs={{0,8},{2,10},{4,12},{6,14},{8,0},{10,2},{12,4},{14,6},{1,9},{3,11}... | collective-permute-start | bytes 196616 | tf_op jit(solution)/shard_map/ppermute | solution.py:369
  6.1 4.5 %collective-permute-done.1 = f32[2,4,128]{2,1,0:T(4,128)S(1)} collective-permute-done((f32[2,4,128]{2,1,0:T(4,128)S(1)}, f32[2,4,128]{2,1,0:T(4,128)S(1)}, u32[]{:S(2)}, u32[]{:S(2)}) %collective-permute-start.1) | collective-permute-done | bytes 4128 | tf_op jit(solution)/shard_map/ppermute | solution.py:370
  11.5 1.6 %collective-permute-start.2 = (bf16[2,32,1024]{2,1,0:T(8,128)(2,1)S(1)}, bf16[2,32,1024]{2,1,0:T(8,128)(2,1)S(1)}, u32[]{:S(2)}, u32[]{:S(2)}) collective-permute-start(bf16[2,32,1024]{2,1,0:T(8,128)(2,1)S(1)} %maximum_bitcast_fusion), channel_id=1, source_target_pairs={{0,4},{2,6},{4,0},{6,2},{8,12},{10,14},{12,8},{14,10},{1,5},{3,7},... | collective-permute-start | bytes 393224 | tf_op jit(solution)/shard_map/ppermute | solution.py:369
  14.3 3.2 %collective-permute-done.3 = f32[2,8,128]{2,1,0:T(8,128)S(1)} collective-permute-done((f32[2,8,128]{2,1,0:T(8,128)S(1)}, f32[2,8,128]{2,1,0:T(8,128)S(1)}, u32[]{:S(2)}, u32[]{:S(2)}) %collective-permute-start.3) | collective-permute-done | bytes 8224 | tf_op jit(solution)/shard_map/ppermute | solution.py:370
  17.6 1.6 %collective-permute-start.4 = (bf16[4,32,1024]{2,1,0:T(8,128)(2,1)S(1)}, bf16[4,32,1024]{2,1,0:T(8,128)(2,1)S(1)}, u32[]{:S(2)}, u32[]{:S(2)}) collective-permute-start(bf16[4,32,1024]{2,1,0:T(8,128)(2,1)S(1)} %bitcast.44), channel_id=1, source_target_pairs={{0,2},{2,0},{4,6},{6,4},{8,10},{10,8},{12,14},{14,12},{1,3},{3,1},... | collective-permute-start | bytes 786440 | tf_op jit(solution)/shard_map/ppermute | solution.py:369
  19.7 4.4 %collective-permute-done.5 = f32[2,16,128]{2,1,0:T(8,128)S(1)} collective-permute-done((f32[2,16,128]{2,1,0:T(8,128)S(1)}, f32[2,16,128]{2,1,0:T(8,128)S(1)}, u32[]{:S(2)}, u32[]{:S(2)}) %collective-permute-start.5) | collective-permute-done | bytes 16416 | tf_op jit(solution)/shard_map/ppermute | solution.py:370
  24.4 6.7 %copy-done = bf16[1024,9728]{1,0:T(8,128)(2,1)S(1)} copy-done((bf16[1024,9728]{1,0:T(8,128)(2,1)S(1)}, bf16[1024,9728]{1,0:T(8,128)(2,1)}, u32[]{:S(2)}) %copy-start) | copy-done | bytes 19922968
  38.1 2.7 %collective-permute-done.7.refs_1_ = f32[128,2304]{1,0:T(8,128)S(1)} collective-permute-done((f32[128,2304]{1,0:T(8,128)S(1)}, f32[128,2304]{1,0:T(8,128)S(1)}, u32[]{:S(2)}, u32[]{:S(2)}) %collective-permute-start.7) | collective-permute-done | bytes 1179680 | tf_op jit(solution)/shard_map/ppermute | solution.py:385
  40.8 1.8 %exponentials.4 = (f32[128,2304]{1,0:T(8,128)S(1)}, f32[128,128]{1,0:T(8,128)S(1)}, f32[128,128]{1,0:T(8,128)S(1)}, s32[128,128]{1,0:T(8,128)S(1)}, f32[128,128]{1,0:T(8,128)S(1)}) custom-call(f32[128,2304]{1,0:T(8,128)S(1)} %get-tuple-element.44.refs_0_, f32[128,2304]{1,0:T(8,128)S(1)} %collective-permute-done.7.refs_1_, ...), custom_call_target="tpu_custom_call" | custom-call | flops 2359296 | bytes 3538944 | tf_op jit(solution)/shard_map/exponentials/pallas_call | solution.py:31
  42.6 1.7 %exponentials.5 = (f32[128,2560]{1,0:T(8,128)S(1)}, f32[128,128]{1,0:T(8,128)S(1)}, f32[128,128]{1,0:T(8,128)S(1)}) custom-call(f32[128,2560]{1,0:T(8,128)S(1)} %get-tuple-element.49.refs_0_, f32[128,2560]{1,0:T(8,128)S(1)} %collective-permute-done.8.refs_1_, s32[128,128]{1,0:T(8,128)S(1)} %get-tuple-element.47.refs_2_.refs_5_, ...), custom_call_target="tpu_custom_call" | custom-call | flops 2621440 | bytes 3932160 | tf_op jit(solution)/shard_map/exponentials/pallas_call | solution.py:31
  45.4 1.7 %exponentials.6 = (f32[128,2304]{1,0:T(8,128)S(1)}, f32[128,128]{1,0:T(8,128)S(1)}, f32[128,128]{1,0:T(8,128)S(1)}) custom-call(f32[128,2304]{1,0:T(8,128)S(1)} %get-tuple-element.42.refs_0_, f32[128,2304]{1,0:T(8,128)S(1)} %collective-permute-done.6.refs_1_, s32[128,128]{1,0:T(8,128)S(1)} %get-tuple-element.47.refs_2_.refs_5_, ...), custom_call_target="tpu_custom_call" | custom-call | flops 2359296 | bytes 3538944 | tf_op jit(solution)/shard_map/exponentials/pallas_call | solution.py:31
  48.2 2.8 %exponentials.7 = (f32[128,2560]{1,0:T(8,128)S(1)}, f32[128,128]{1,0:T(8,128)S(1)}, f32[128,128]{1,0:T(8,128)S(1)}, f32[8,128]{1,0:T(8,128)S(1)}) custom-call(f32[128,2560]{1,0:T(8,128)S(1)} %get-tuple-element.54.refs_0_, f32[128,2560]{1,0:T(8,128)S(1)} %collective-permute-done.9.refs_1_, s32[128,128]{1,0:T(8,128)S(1)} %get-tuple-element.47.refs_2_.refs_5_, ...), custom_call_target="tpu_custom_call" | custom-call | flops 2621440 | bytes 3932160 | tf_op jit(solution)/shard_map/exponentials/pallas_call | solution.py:31
  53.6 2.1 %collective-permute-done.10 = f32[4,128]{1,0:T(4,128)S(1)} collective-permute-done((f32[4,128]{1,0:T(4,128)S(1)}, f32[4,128]{1,0:T(4,128)S(1)}, u32[]{:S(2)}, u32[]{:S(2)}) %collective-permute-start.10) | collective-permute-done | bytes 2080 | tf_op jit(solution)/shard_map/ppermute | solution.py:400
  56.5 2.9 %collective-permute-done.11 = f32[4,128]{1,0:T(4,128)S(1)} collective-permute-done((f32[4,128]{1,0:T(4,128)S(1)}, f32[4,128]{1,0:T(4,128)S(1)}, u32[]{:S(2)}, u32[]{:S(2)}) %collective-permute-start.11) | collective-permute-done | bytes 2080 | tf_op jit(solution)/shard_map/ppermute | solution.py:400
  60.7 3.3 %collective-permute-done.12 = f32[4,128]{1,0:T(4,128)S(1)} collective-permute-done((f32[4,128]{1,0:T(4,128)S(1)}, f32[4,128]{1,0:T(4,128)S(1)}, u32[]{:S(2)}, u32[]{:S(2)}) %collective-permute-start.12) | collective-permute-done | bytes 2080 | tf_op jit(solution)/shard_map/ppermute | solution.py:400
  65.3 4.2 %logit_grad.3.refs_0_.own_ref = bf16[128,4864]{1,0:T(8,128)(2,1)S(1)} custom-call(f32[128,2304]{1,0:T(8,128)S(1)} %get-tuple-element.64.refs_0_, f32[128,2560]{1,0:T(8,128)S(1)} %copy-done.3, f32[128,128]{1,0:T(8,128)S(1)} %get-tuple-element.57.refs_5_.refs_2_, f32[128,128]{1,0:T(8,128)S(1)} %get-tuple-element.58.refs_6_.refs_3_, ...), custom_call_target="tpu_custom_call" | custom-call | flops 4980736 | bytes 3735552 | tf_op jit(solution)/shard_map/logit_grad/pallas_call | solution.py:31
  69.7 4.4 %logit_grad.2.refs_0_.own_ref = bf16[128,4864]{1,0:T(8,128)(2,1)S(1)} custom-call(f32[128,2304]{1,0:T(8,128)S(1)} %copy-done.7, f32[128,2560]{1,0:T(8,128)S(1)} %copy-done.5, f32[128,128]{1,0:T(8,128)S(1)} %get-tuple-element.59.refs_7_.refs_2_, f32[128,128]{1,0:T(8,128)S(1)} %get-tuple-element.61.refs_3_, f32[128,128]{1,0:T(8,128)S(1)} %get-tuple-element.62.refs_4_, ...), custom_call_target="tpu_custom_call" | custom-call | flops 4980736 | bytes 3735552 | tf_op jit(solution)/shard_map/logit_grad/pallas_call | solution.py:31
  74.7 6.7 %copy-done.1 = bf16[1024,9728]{1,0:T(8,128)(2,1)S(1)} copy-done((bf16[1024,9728]{1,0:T(8,128)(2,1)S(1)}, bf16[1024,9728]{1,0:T(8,128)(2,1)}, u32[]{:S(2)}) %copy-start.1) | copy-done | bytes 19922968
  81.3 4.0 %feature_terms.2.refs_3_ = f32[256,1024]{1,0:T(8,128)S(1)} custom-call(bf16[128,4864]{1,0:T(8,128)(2,1)S(1)} %logit_grad.3.refs_0_.own_ref, bf16[128,4864]{1,0:T(8,128)(2,1)} %collective-permute-done.14.refs_1_.other_ref, bf16[1024,9728]{1,0:T(8,128)(2,1)S(1)} %copy-done.1), custom_call_target="tpu_custom_call" | custom-call | flops 2550136832 | bytes 12451840 | tf_op jit(solution)/shard_map/feature_terms/pallas_call | solution.py:31
  85.4 4.8 %feature_terms.3 = (f32[128,1024]{1,0:T(8,128)S(1)}, bf16[128,1024]{1,0:T(8,128)(2,1)}) custom-call(bf16[128,4864]{1,0:T(8,128)(2,1)S(1)} %logit_grad.2.refs_0_.own_ref, bf16[128,4864]{1,0:T(8,128)(2,1)} %collective-permute-done.13.refs_1_.other_ref, bf16[1024,9728]{1,0:T(8,128)(2,1)S(1)} %copy-done.1, f32[256,1024]{1,0:T(8,128)S(1)} %feature_terms.2.refs_3_, ...), custom_call_target="tpu_custom_call" | custom-call | flops 2550136832 | bytes 12451840 | tf_op jit(solution)/shard_map/feature_terms/pallas_call | solution.py:31
  91.0 1.5 %collective-permute-start.15 = (bf16[128,1024]{1,0:T(8,128)(2,1)}, bf16[128,1024]{1,0:T(8,128)(2,1)}, u32[]{:S(2)}, u32[]{:S(2)}) collective-permute-start(bf16[128,1024]{1,0:T(8,128)(2,1)} %get-tuple-element.67), channel_id=1, source_target_pairs={{0,2},{2,0},{4,6},{6,4},{8,10},{10,8},{12,14},{14,12},{1,3},{3,1},... | collective-permute-start | bytes 786440 | tf_op jit(solution)/shard_map/ppermute | solution.py:416
  92.8 6.3 %weight_grad.2.refs_0_ = bf16[1024,9728]{1,0:T(8,128)(2,1)} custom-call(bf16[1024,256]{1,0:T(8,128)(2,1)S(1)} %bitcast.42, bf16[128,4864]{1,0:T(8,128)(2,1)S(1)} %logit_grad.3.refs_0_.own_ref, bf16[128,4864]{1,0:T(8,128)(2,1)} %collective-permute-done.14.refs_1_.other_ref), custom_call_target="tpu_custom_call" | custom-call | flops 2550136832 | bytes 12451840 | tf_op jit(solution)/shard_map/weight_grad/pallas_call | solution.py:31
  101.4 1.9 %collective-permute-start.18 = (bf16[32,1024]{1,0:T(8,128)(2,1)S(1)}, bf16[32,1024]{1,0:T(8,128)(2,1)S(1)}, u32[]{:S(2)}, u32[]{:S(2)}) collective-permute-start(bf16[32,1024]{1,0:T(8,128)(2,1)S(1)} %get-tuple-element.77), channel_id=1, source_target_pairs={{0,12},{2,14},{4,8},{6,10},{8,4},{10,6},{12,0},{14,2},{1,13},{3,15... | collective-permute-start | bytes 196616 | tf_op jit(solution)/shard_map/ppermute | solution.py:420
  104.2 6.3 %weight_grad.3 = bf16[1024,9728]{1,0:T(8,128)(2,1)} custom-call(bf16[1024,256]{1,0:T(8,128)(2,1)S(1)} %bitcast.43, bf16[128,4864]{1,0:T(8,128)(2,1)S(1)} %logit_grad.2.refs_0_.own_ref, bf16[128,4864]{1,0:T(8,128)(2,1)} %collective-permute-done.13.refs_1_.other_ref, bf16[1024,9728]{1,0:T(8,128)(2,1)} %weight_grad.2.refs_0_), custom_call_target="tpu_custom_call", output_to_operand_aliasing={{}: (3, {})} | custom-call | flops 2550136832 | bytes 12451840 | tf_op jit(solution)/shard_map/weight_grad/pallas_call | solution.py:31
  (85 shorter events, 24.9 us)
Async XLA Ops:
  0.6 19.1 %copy-start.13 = (f32[2]{0:T(128)S(1)}, f32[2]{0:T(128)}, u32[]{:S(2)}) copy-start(f32[2]{0:T(128)} %constant.22.clone) | copy-start | bytes 28
  0.6 18.5 %copy-start.10 = (f32[128,4]{0,1:T(4,128)S(1)}, f32[128,4]{0,1:T(4,128)}, u32[]{:S(2)}) copy-start(f32[128,4]{0,1:T(4,128)} %param.10) | copy-start | bytes 6148
  0.7 10.0 %collective-permute-start = (bf16[1,32,1024]{2,1,0:T(8,128)(2,1)}, bf16[1,32,1024]{2,1,0:T(8,128)(2,1)S(1)}, u32[]{:S(2)}, u32[]{:S(2)}) collective-permute-start(bf16[1,32,1024]{2,1,0:T(8,128)(2,1)} %bitcast.45), channel_id=1, source_target_pairs={{0,8},{2,10},{4,12},{6,14},{8,0},{10,2},{12,4},{14,6},{1,9},{3,11}... | collective-permute-start | bytes 196616 | tf_op jit(solution)/shard_map/ppermute | solution.py:369
  6.1 4.5 %collective-permute-start.1 = (f32[2,4,128]{2,1,0:T(4,128)S(1)}, f32[2,4,128]{2,1,0:T(4,128)S(1)}, u32[]{:S(2)}, u32[]{:S(2)}) collective-permute-start(f32[2,4,128]{2,1,0:T(4,128)S(1)} %pad_maximum_fusion.4), channel_id=1, source_target_pairs={{0,8},{2,10},{4,12},{6,14},{8,0},{10,2},{12,4},{14,6},{1,9},{3,11}... | collective-permute-start | bytes 12296 | tf_op jit(solution)/shard_map/ppermute | solution.py:370
  11.5 6.0 %collective-permute-start.2 = (bf16[2,32,1024]{2,1,0:T(8,128)(2,1)S(1)}, bf16[2,32,1024]{2,1,0:T(8,128)(2,1)S(1)}, u32[]{:S(2)}, u32[]{:S(2)}) collective-permute-start(bf16[2,32,1024]{2,1,0:T(8,128)(2,1)S(1)} %maximum_bitcast_fusion), channel_id=1, source_target_pairs={{0,4},{2,6},{4,0},{6,2},{8,12},{10,14},{12,8},{14,10},{1,5},{3,7},... | collective-permute-start | bytes 393224 | tf_op jit(solution)/shard_map/ppermute | solution.py:369
  13.8 3.7 %collective-permute-start.3 = (f32[2,8,128]{2,1,0:T(8,128)S(1)}, f32[2,8,128]{2,1,0:T(8,128)S(1)}, u32[]{:S(2)}, u32[]{:S(2)}) collective-permute-start(f32[2,8,128]{2,1,0:T(8,128)S(1)} %pad_maximum_fusion.3), channel_id=1, source_target_pairs={{0,4},{2,6},{4,0},{6,2},{8,12},{10,14},{12,8},{14,10},{1,5},{3,7},... | collective-permute-start | bytes 24584 | tf_op jit(solution)/shard_map/ppermute | solution.py:370
  17.6 6.6 %collective-permute-start.4 = (bf16[4,32,1024]{2,1,0:T(8,128)(2,1)S(1)}, bf16[4,32,1024]{2,1,0:T(8,128)(2,1)S(1)}, u32[]{:S(2)}, u32[]{:S(2)}) collective-permute-start(bf16[4,32,1024]{2,1,0:T(8,128)(2,1)S(1)} %bitcast.44), channel_id=1, source_target_pairs={{0,2},{2,0},{4,6},{6,4},{8,10},{10,8},{12,14},{14,12},{1,3},{3,1},... | collective-permute-start | bytes 786440 | tf_op jit(solution)/shard_map/ppermute | solution.py:369
  19.2 5.0 %collective-permute-start.5 = (f32[2,16,128]{2,1,0:T(8,128)S(1)}, f32[2,16,128]{2,1,0:T(8,128)S(1)}, u32[]{:S(2)}, u32[]{:S(2)}) collective-permute-start(f32[2,16,128]{2,1,0:T(8,128)S(1)} %pad_maximum_fusion.2), channel_id=1, source_target_pairs={{0,2},{2,0},{4,6},{6,4},{8,10},{10,8},{12,14},{14,12},{1,3},{3,1},... | collective-permute-start | bytes 49160 | tf_op jit(solution)/shard_map/ppermute | solution.py:370
  34.1 14.0 %collective-permute-start.9 = (f32[128,2560]{1,0:T(8,128)S(1)}, f32[128,2560]{1,0:T(8,128)S(1)}, u32[]{:S(2)}, u32[]{:S(2)}) collective-permute-start(f32[128,2560]{1,0:T(8,128)S(1)} %get-tuple-element.55), channel_id=1, source_target_pairs={{0,1},{1,0},{2,3},{3,2},{4,5},{5,4},{6,7},{7,6},{8,9},{9,8},{10,11... | collective-permute-start | bytes 3932168 | tf_op jit(solution)/shard_map/ppermute | solution.py:385
  34.2 8.4 %collective-permute-start.8 = (f32[128,2560]{1,0:T(8,128)S(1)}, f32[128,2560]{1,0:T(8,128)S(1)}, u32[]{:S(2)}, u32[]{:S(2)}) collective-permute-start(f32[128,2560]{1,0:T(8,128)S(1)} %get-tuple-element.50), channel_id=1, source_target_pairs={{0,1},{1,0},{2,3},{3,2},{4,5},{5,4},{6,7},{7,6},{8,9},{9,8},{10,11... | collective-permute-start | bytes 3932168 | tf_op jit(solution)/shard_map/ppermute | solution.py:385
  36.1 4.7 %collective-permute-start.7 = (f32[128,2304]{1,0:T(8,128)S(1)}, f32[128,2304]{1,0:T(8,128)S(1)}, u32[]{:S(2)}, u32[]{:S(2)}) collective-permute-start(f32[128,2304]{1,0:T(8,128)S(1)} %get-tuple-element.45), channel_id=1, source_target_pairs={{0,1},{1,0},{2,3},{3,2},{4,5},{5,4},{6,7},{7,6},{8,9},{9,8},{10,11... | collective-permute-start | bytes 3538952 | tf_op jit(solution)/shard_map/ppermute | solution.py:385
  37.6 7.8 %collective-permute-start.6 = (f32[128,2304]{1,0:T(8,128)S(1)}, f32[128,2304]{1,0:T(8,128)S(1)}, u32[]{:S(2)}, u32[]{:S(2)}) collective-permute-start(f32[128,2304]{1,0:T(8,128)S(1)} %get-tuple-element.43), channel_id=1, source_target_pairs={{0,1},{1,0},{2,3},{3,2},{4,5},{5,4},{6,7},{7,6},{8,9},{9,8},{10,11... | collective-permute-start | bytes 3538952 | tf_op jit(solution)/shard_map/ppermute | solution.py:385
  48.2 12.5 %copy-start.11 = (f32[128]{0:T(128)S(1)}, f32[128]{0:T(128)}, u32[]{:S(2)}) copy-start(f32[128]{0:T(128)} %param.12) | copy-start | bytes 1540
  48.2 12.5 %copy-start.12 = (s32[128]{0:T(128)S(1)}, s32[128]{0:T(128)}, u32[]{:S(2)}) copy-start(s32[128]{0:T(128)} %param.11) | copy-start | bytes 1540
  52.1 3.6 %collective-permute-start.10 = (f32[4,128]{1,0:T(4,128)S(1)}, f32[4,128]{1,0:T(4,128)S(1)}, u32[]{:S(2)}, u32[]{:S(2)}) collective-permute-start(f32[4,128]{1,0:T(4,128)S(1)} %slice.83), channel_id=1, source_target_pairs={{0,2},{2,0},{4,6},{6,4},{8,10},{10,8},{12,14},{14,12},{1,3},{3,1},... | collective-permute-start | bytes 6152 | tf_op jit(solution)/shard_map/ppermute | solution.py:400
  55.7 3.7 %collective-permute-start.11 = (f32[4,128]{1,0:T(4,128)S(1)}, f32[4,128]{1,0:T(4,128)S(1)}, u32[]{:S(2)}, u32[]{:S(2)}) collective-permute-start(f32[4,128]{1,0:T(4,128)S(1)} %pad_maximum_fusion.5), channel_id=1, source_target_pairs={{0,4},{2,6},{4,0},{6,2},{8,12},{10,14},{12,8},{14,10},{1,5},{3,7},... | collective-permute-start | bytes 6152 | tf_op jit(solution)/shard_map/ppermute | solution.py:400
  59.4 4.5 %collective-permute-start.12 = (f32[4,128]{1,0:T(4,128)S(1)}, f32[4,128]{1,0:T(4,128)S(1)}, u32[]{:S(2)}, u32[]{:S(2)}) collective-permute-start(f32[4,128]{1,0:T(4,128)S(1)} %pad_maximum_fusion.6), channel_id=1, source_target_pairs={{0,8},{2,10},{4,12},{6,14},{8,0},{10,2},{12,4},{14,6},{1,9},{3,11}... | collective-permute-start | bytes 6152 | tf_op jit(solution)/shard_map/ppermute | solution.py:400
  69.6 5.1 %collective-permute-start.14 = (bf16[128,4864]{1,0:T(8,128)(2,1)S(1)}, bf16[128,4864]{1,0:T(8,128)(2,1)}, u32[]{:S(2)}, u32[]{:S(2)}) collective-permute-start(bf16[128,4864]{1,0:T(8,128)(2,1)S(1)} %logit_grad.3.refs_0_.own_ref), channel_id=1, source_target_pairs={{0,1},{1,0},{2,3},{3,2},{4,5},{5,4},{6,7},{7,6},{8,9},{9,8},{10,11... | collective-permute-start | bytes 3735560 | tf_op jit(solution)/shard_map/ppermute | solution.py:409
  74.1 11.3 %collective-permute-start.13 = (bf16[128,4864]{1,0:T(8,128)(2,1)S(1)}, bf16[128,4864]{1,0:T(8,128)(2,1)}, u32[]{:S(2)}, u32[]{:S(2)}) collective-permute-start(bf16[128,4864]{1,0:T(8,128)(2,1)S(1)} %logit_grad.2.refs_0_.own_ref), channel_id=1, source_target_pairs={{0,1},{1,0},{2,3},{3,2},{4,5},{5,4},{6,7},{7,6},{8,9},{9,8},{10,11... | collective-permute-start | bytes 3735560 | tf_op jit(solution)/shard_map/ppermute | solution.py:409
  91.0 8.6 %collective-permute-start.15 = (bf16[128,1024]{1,0:T(8,128)(2,1)}, bf16[128,1024]{1,0:T(8,128)(2,1)}, u32[]{:S(2)}, u32[]{:S(2)}) collective-permute-start(bf16[128,1024]{1,0:T(8,128)(2,1)} %get-tuple-element.67), channel_id=1, source_target_pairs={{0,2},{2,0},{4,6},{6,4},{8,10},{10,8},{12,14},{14,12},{1,3},{3,1},... | collective-permute-start | bytes 786440 | tf_op jit(solution)/shard_map/ppermute | solution.py:416
  92.8 6.8 %copy-start.9 = (f32[128,1024]{1,0:T(8,128)S(1)}, f32[128,1024]{1,0:T(8,128)}, u32[]{:S(2)}) copy-start(f32[128,1024]{1,0:T(8,128)} %copy-done.8) | copy-start | bytes 1572868
  100.7 9.8 %collective-permute-start.16 = (bf16[32,1024]{1,0:T(8,128)(2,1)S(1)}, bf16[32,1024]{1,0:T(8,128)(2,1)S(1)}, u32[]{:S(2)}, u32[]{:S(2)}) collective-permute-start(bf16[32,1024]{1,0:T(8,128)(2,1)S(1)} %get-tuple-element.76), channel_id=1, source_target_pairs={{0,4},{2,6},{4,0},{6,2},{8,12},{10,14},{12,8},{14,10},{1,5},{3,7},... | collective-permute-start | bytes 196616 | tf_op jit(solution)/shard_map/ppermute | solution.py:420
  101.4 9.1 %collective-permute-start.18 = (bf16[32,1024]{1,0:T(8,128)(2,1)S(1)}, bf16[32,1024]{1,0:T(8,128)(2,1)S(1)}, u32[]{:S(2)}, u32[]{:S(2)}) collective-permute-start(bf16[32,1024]{1,0:T(8,128)(2,1)S(1)} %get-tuple-element.77), channel_id=1, source_target_pairs={{0,12},{2,14},{4,8},{6,10},{8,4},{10,6},{12,0},{14,2},{1,13},{3,15... | collective-permute-start | bytes 196616 | tf_op jit(solution)/shard_map/ppermute | solution.py:420
  103.4 7.1 %collective-permute-start.17 = (bf16[32,1024]{1,0:T(8,128)(2,1)S(1)}, bf16[32,1024]{1,0:T(8,128)(2,1)S(1)}, u32[]{:S(2)}, u32[]{:S(2)}) collective-permute-start(bf16[32,1024]{1,0:T(8,128)(2,1)S(1)} %get-tuple-element.78), channel_id=1, source_target_pairs={{0,8},{2,10},{4,12},{6,14},{8,0},{10,2},{12,4},{14,6},{1,9},{3,11}... | collective-permute-start | bytes 196616 | tf_op jit(solution)/shard_map/ppermute | solution.py:420
  (9 other events, 27.4 us)

commit v3 on v2

--- a/solution.py
+++ b/solution.py
@@ -78,7 +78,7 @@
     )
 
 
-def _exp_body(start, width, index, count, terms, *refs):
+def _exp_body(start, width, index, count, terms, kept, *refs):
     first, last = index == 0, index == count - 1
     refs = list(refs)
     own_ref, recv_ref = refs.pop(0), refs.pop(0)
@@ -87,6 +87,7 @@
     else:
         ids_ref, lps_ref, picks_in = refs.pop(0), refs.pop(0), refs.pop(0)
     before = [refs.pop(0) for _ in range(index)] if last else []
+    del refs[:kept]
     e_ref, picks_ref, stat_ref = refs.pop(0), refs.pop(0), refs.pop(0)
     half = own_ref.shape[0]
     if first:
@@ -95,14 +96,14 @@
         ids_ref[...] = jnp.concatenate([packed_ref[0], pad], axis=0).T.astype(jnp.int32)
         lps_ref[...] = jnp.concatenate([packed_ref[1], pad], axis=0).T
     if last:
-        tot_ref, hold = refs
-    lane = lax.broadcasted_iota(jnp.int32, (TILE, 128), 1)
+        tot_ref = refs.pop(0)
+    hold = refs.pop(0)
+    lane = lax.broadcasted_iota(jnp.int32, (half, 128), 1)
     ways = 4
 
-    def tile(t, carry):
+    def pick(t, carry):
         rows = pl.ds(pl.multiple_of(t * TILE, TILE), TILE)
-        ids = ids_ref[rows, :]
-        rel = ids - start
+        rel = ids_ref[rows, :] - start
         key = rel >> 7
         slot = rel & 127
         acc = [jnp.zeros((TILE, 128), F32)] * ways
@@ -115,113 +116,154 @@
             top[w] = jnp.maximum(top[w], logit)
             got = jnp.take_along_axis(logit, slot, axis=1, mode="promise_in_bounds")
             acc[w] = jnp.where(key == c, got, acc[w])
-        top = functools.reduce(jnp.maximum, top)
-        top = jnp.max(top, axis=1, keepdims=True)
+        hold[rows, :] = functools.reduce(jnp.maximum, top)
+        picked = sum(acc)
+        picks_ref[rows, :] = picked if first else picked + picks_in[rows, :]
+        return carry
+
+    def power(t, carry):
+        rows = pl.ds(pl.multiple_of(t * TILE, TILE), TILE)
+        top = stat_ref[rows, :]
         total = [jnp.zeros((TILE, 128), F32)] * ways
         for c in range(width // 128):
             cols = slice(c * 128, (c + 1) * 128)
             e = jnp.exp(e_ref[rows, cols] - top)
             e_ref[rows, cols] = e
             total[c % ways] += e
-        total = jnp.sum(sum(total), axis=1, keepdims=True)
-        picked = sum(acc)
-        if not first:
-            picked = picked + picks_in[rows, :]
-        picks_ref[rows, :] = picked
-        stat_ref[rows, :] = jnp.where(lane == 0, top, total)
-        if last:
-            tops, totals = [top], [total]
-            for ref in before:
-                tops.append(ref[rows, 0:1])
-                totals.append(ref[rows, 1:2])
-            both = functools.reduce(jnp.maximum, tops)
-            total = sum(s * jnp.exp(m - both) for m, s in zip(tops, totals))
-            inside = (ids >= 0) & (ids < start + width)
-            weight = jnp.where(inside, jnp.exp(picked - both), 0.0)
-            mixed = jnp.sum(weight * (picked - both - lps_ref[rows, :] + 1.0), axis=1, keepdims=True)
-            plain = jnp.sum(weight, axis=1, keepdims=True)
-            hold[rows, :] = jnp.where(
-                lane == 0, both, jnp.where(lane == 1, total, jnp.where(lane == 2, mixed, plain))
-            )
+        hold[rows, :] = sum(total)
         return carry
 
-    lax.fori_loop(0, half // TILE, tile, 0, unroll=2)
+    lax.fori_loop(0, half // TILE, pick, 0, unroll=2)
+    stat_ref[...] = jnp.broadcast_to(jnp.max(hold[...], axis=1, keepdims=True), (half, 128))
+    lax.fori_loop(0, half // TILE, power, 0, unroll=2)
+    top = stat_ref[...]
+    total = jnp.sum(hold[...], axis=1, keepdims=True)
+    stat_ref[...] = jnp.where(lane == 0, top, total)
     if last:
-        tot_ref[...] = hold[...].T[:TILE, :]
-
-
-def _exponentials(own, recv, chunks, index, terms, packed=None, rows=None, picks=None, before=()):
+        tops, totals = [top[:, 0:1]], [total]
+        for ref in before:
+            tops.append(ref[:, 0:1])
+            totals.append(ref[:, 1:2])
+        both = functools.reduce(jnp.maximum, tops)
+        total = sum(s * jnp.exp(m - both) for m, s in zip(tops, totals))
+        ids = ids_ref[...]
+        inside = (ids >= 0) & (ids < start + width)
+        picked = picks_ref[...] - both
+        weight = jnp.where(inside, jnp.exp(picked), 0.0)
+        mixed = jnp.sum(weight * (picked - lps_ref[...] + 1.0), axis=1, keepdims=True)
+        plain = jnp.sum(weight, axis=1, keepdims=True)
+        table = jnp.where(lane == 0, both, jnp.where(lane == 1, total, jnp.where(lane == 2, mixed, plain)))
+        tot_ref[...] = table.T[:TILE, :]
+
+
+def _exponentials(own, recv, chunks, index, terms, packed=None, rows=None, picks=None, before=(), kept=()):
     start, width = chunks[index]
     half = own.shape[0]
     first, last = index == 0, index == len(chunks) - 1
     table = pltpu.VMEM((half, 128), F32)
-    args = [own, recv] + ([packed] if first else [*rows, picks]) + (list(before) if last else [])
+    args = [own, recv] + ([packed] if first else [*rows, picks]) + (list(before) if last else []) + list(kept)
     out = [pltpu.VMEM((half, width), F32), table, table]
-    scratch = []
     if first:
         out += [pltpu.VMEM((half, 128), jnp.int32), table]
     if last:
         out.append(pltpu.VMEM((TILE, half), F32))
-        scratch = [pltpu.VMEM((half, 128), F32)]
-    return _call(
-        functools.partial(_exp_body, start, width, index, len(chunks), terms),
+    return _call(
+        functools.partial(_exp_body, start, width, index, len(chunks), terms, len(kept)),
         "exponentials",
         args,
         out,
         _cost(8 * half * width, 12 * half * width),
-        scratch=scratch,
+        scratch=[pltpu.VMEM((half, 128), F32)],
     )
 
 
-def _join_stats(a, b):
-    top = jnp.maximum(a[0], b[0])
-    da, db = a[0] - top, b[0] - top
+def _join_body(a_ref, b_ref, *refs):
+    a, b = a_ref[...], b_ref[...]
+    top = jnp.maximum(a[0:1], b[0:1])
+    da, db = a[0:1] - top, b[0:1] - top
     fa, fb = jnp.exp(da), jnp.exp(db)
-    return jnp.stack(
-        [
-            top,
-            a[1] * fa + b[1] * fb,
-            (a[2] + da * a[3]) * fa + (b[2] + db * b[3]) * fb,
-            a[3] * fa + b[3] * fb,
-        ]
-    )
+    total = a[1:2] * fa + b[1:2] * fb
+    mixed = (a[2:3] + da * a[3:4]) * fa + (b[2:3] + db * b[3:4]) * fb
+    plain = a[3:4] * fa + b[3:4] * fb
+    refs[-1][...] = jnp.concatenate([top, total, mixed, plain, a[4:]], axis=0)
+
+
+def _join_stats(a, b, kept):
+    return _call(
+        _join_body, "join_stats", [a, b, *kept], [pltpu.VMEM(a.shape, F32)], _cost(10 * a.size, 12 * a.size)
+    )[0]
+
+
+def _fetch_body(start, w_ref, out_ref, sems):
+    depth = w_ref.shape[0]
+    step = depth // sems.shape[0]
+    copies = [
+        pltpu.make_async_copy(
+            w_ref.at[pl.ds(i * step, step), pl.ds(start, out_ref.shape[1])],
+            out_ref.at[pl.ds(i * step, step), :],
+            sems.at[i],
+        )
+        for i in range(sems.shape[0])
+    ]
+    for copy in copies:
+        copy.start()
+    for copy in copies:
+        copy.wait()
+
+
+def _fetch(w, start, width):
+    depth = w.shape[0]
+    return _call(
+        functools.partial(_fetch_body, start),
+        "fetch_weight",
+        [pltpu.with_memory_space_constraint(w, pltpu.HBM)],
+        [pltpu.VMEM((depth, width), BF16)],
+        _cost(0, 2 * depth * width),
+        specs=[pl.BlockSpec(memory_space=pltpu.HBM)],
+        scratch=[pltpu.SemaphoreType.DMA((4,))],
+    )[0]
 
 
 def _grad_body(chunks, terms, *refs):
     count = len(chunks)
     e_refs, stat_refs = refs[:count], refs[count : 2 * count]
-    picks_ref, ids_ref, lps_ref, tot_ref, g_ref, hold = refs[2 * count :]
+    picks_ref, ids_ref, lps_ref, tot_ref = refs[2 * count : 2 * count + 4]
+    g_ref, coef_ref, high_ref, low_ref = refs[-4:]
     half = tot_ref.shape[1]
     lanes = TILE * terms
-    hold[...] = jnp.concatenate([tot_ref[...], jnp.zeros((128 - TILE, half), F32)], axis=0).T
+    begin = chunks[0][0]
+    width = sum(w for _, w in chunks)
+    parts = (width + 255) // 256
+
+    tot = jnp.concatenate([tot_ref[...], jnp.zeros((128 - TILE, half), F32)], axis=0).T
+    top, total, mixed, plain, scale = (tot[:, i : i + 1] for i in range(5))
+    log_sum = jnp.log(total)
+    lse = top + log_sum
+    sum_grad = scale * jnp.exp(-log_sum) * (mixed - log_sum * plain)
+    for q, ref in enumerate(stat_refs):
+        coef_ref[q] = jnp.broadcast_to(sum_grad * jnp.exp(ref[:, 0:1] - lse), (half, 128))
+    rel = ids_ref[...] - begin
+    inside = (rel >= 0) & (rel < width)
+    support = picks_ref[...] - lse
+    grad = scale * jnp.exp(support) * (support - lps_ref[...] + 1.0)
+    grad = jnp.where(inside, grad, 0.0)
+    high = grad.astype(BF16).astype(F32)
+    high_ref[...] = high
+    low_ref[...] = grad - high
+
     lane_row = lax.broadcasted_iota(jnp.int32, (TILE, lanes), 1) // terms
     mask = lane_row == lax.broadcasted_iota(jnp.int32, (TILE, lanes), 0)
     place = lax.broadcasted_iota(jnp.int32, (256, lanes), 0)
-    begin = chunks[0][0]
-    width = sum(w for _, w in chunks)
-    parts = (width + 255) // 256
 
     def flat(x):
         return jnp.concatenate([x[:, :terms]] * TILE, axis=1)
 
     def tile(t):
         rows = pl.ds(pl.multiple_of(t * TILE, TILE), TILE)
-        tot = hold[rows, :]
-        top, total, mixed, plain, scale = (tot[:, i : i + 1] for i in range(5))
-        log_sum = jnp.log(total)
-        lse = top + log_sum
-        sum_grad = scale * jnp.exp(-log_sum) * (mixed - log_sum * plain)
-        coefs = [sum_grad * jnp.exp(ref[rows, 0:1] - lse) for ref in stat_refs]
-        rel = ids_ref[rows, :] - begin
-        inside = (rel >= 0) & (rel < width)
-        support = picks_ref[rows, :] - lse
-        grad = scale * jnp.exp(support) * (support - lps_ref[rows, :] + 1.0)
-        grad = jnp.where(inside, grad, 0.0)
-        high = grad.astype(BF16).astype(F32)
-        key = jnp.where(mask, flat(jnp.where(inside, rel >> 8, -1)), -1)
-        col = jnp.where(mask, flat(rel & 255), 0)
-        col = jnp.sum(col, axis=0, keepdims=True)
-        high, low = flat(high), flat(grad - high)
+        rel = flat(ids_ref[rows, :]) - begin
+        key = jnp.where(mask, rel >> 8, -1)
+        col = jnp.sum(jnp.where(mask, rel & 255, 0), axis=0, keepdims=True)
+        high, low = flat(high_ref[rows, :]), flat(low_ref[rows, :])
         lhs = jnp.concatenate(
             [
                 jnp.concatenate([jnp.where(key == c, high, 0.0), jnp.where(key == c, low, 0.0)], axis=1)
@@ -231,46 +273,47 @@
         ).astype(BF16)
         hot = (place == jnp.broadcast_to(col, (256, lanes))).astype(F32).astype(BF16)
         rhs = jnp.concatenate([hot, hot], axis=1)
-        return rows, coefs, lax.dot_general(lhs, rhs, NT, preferred_element_type=F32)
+        return rows, lax.dot_general(lhs, rhs, NT, preferred_element_type=F32)
 
     def step(i, carry):
         pair = [tile(i * (STEP // TILE) + t) for t in range(STEP // TILE)]
         out_rows = pl.ds(pl.multiple_of(i * STEP, STEP), STEP)
         for q, (start, w) in enumerate(chunks):
+            coefs = [coef_ref[q, rows, :] for rows, _ in pair]
             for at, size in _blocks(w, 128):
                 col = start - begin + at
                 c, off = col // 256, col % 256
                 out = [
-                    s[c * TILE : (c + 1) * TILE, off : off + size] - e_refs[q][rows, at : at + size] * coefs[q]
-                    for rows, coefs, s in pair
+                    s[c * TILE : (c + 1) * TILE, off : off + size] - e_refs[q][rows, at : at + size] * coef
+                    for (rows, s), coef in zip(pair, coefs)
                 ]
                 g_ref[out_rows, col : col + size] = jnp.concatenate(out, axis=0).astype(BF16)
         return carry
 
-    lax.fori_loop(0, half // STEP, step, 0)
-
-
-def _logit_grad(es, stats, picks, ids, lps, tot, chunks, terms):
+    lax.fori_loop(0, half // STEP, step, 0, unroll=2)
+
+
+def _logit_grad(es, stats, picks, ids, lps, tot, chunks, terms, kept):
     half = es[0].shape[0]
     width = sum(w for _, w in chunks)
+    table = pltpu.VMEM((half, 128), F32)
     return _call(
         functools.partial(_grad_body, chunks, terms),
         "logit_grad",
-        [*es, *stats, picks, ids, lps, tot],
+        [*es, *stats, picks, ids, lps, tot, *kept],
         [pltpu.VMEM((half, width), BF16)],
         _cost(8 * half * width, 6 * half * width),
-        scratch=[pltpu.VMEM((half, 128), F32)],
+        scratch=[pltpu.VMEM((len(chunks), half, 128), F32), table, table],
     )[0]
 
 
-def _feature_body(start, count, *refs):
+def _feature_body(count, *refs):
     if count:
         own_ref, other_ref, w_ref, before_ref, order_ref, keep_ref, send_ref, acc = refs
     else:
         own_ref, other_ref, w_ref, acc = refs
-    width = own_ref.shape[1]
     grads = jnp.concatenate([own_ref[...], other_ref[...]], axis=0)
-    part = lax.dot_general(grads, w_ref[:, start : start + width], NT, preferred_element_type=F32)
+    part = lax.dot_general(grads, w_ref[...], NT, preferred_element_type=F32)
     if not count:
         acc[...] = part
         return
@@ -284,7 +327,7 @@
     send_ref[...] = jnp.concatenate(far, axis=0).astype(BF16)
 
 
-def _feature_terms(own, other, w, start, before=None, order=None):
+def _feature_terms(own, other, w, before=None, order=None):
     half, width = own.shape
     depth = w.shape[0]
     args = [own, other, w]
@@ -297,7 +340,7 @@
         scratch = out
         out = [pltpu.VMEM((half, depth), F32), pltpu.VMEM((half, depth), BF16)]
     return _call(
-        functools.partial(_feature_body, start, 0 if before is None else order.shape[0]),
+        functools.partial(_feature_body, 0 if before is None else order.shape[0]),
         "feature_terms",
         args,
         out,
@@ -361,14 +404,23 @@
     swap = [(0, 1), (1, 0)]
     chunks = _split(width, 4)
     groups = [[0, 1], [2, 3]]
-    weights = _local(head_weight)
+    starts = [chunks[group[0]][0] for group in groups]
+    widths = [sum(chunks[q][1] for q in group) for group in groups]
 
     h = hidden[None]
     packed = jnp.stack([teacher_ids.T.astype(F32), teacher_logprobs.T])
+    weights = []
     for b in reversed(range(bits)):
         far = lax.ppermute(h, "vocab", _xor(count, 1 << b))
         far_packed = lax.ppermute(packed, "vocab", _xor(count, 1 << b))
-        far, far_packed = lax.optimization_barrier((far, far_packed))
+        if b < 2:
+            g = len(weights)
+            _, source = lax.optimization_barrier((h, head_weight))
+            part = _fetch(source, starts[g], widths[g])
+            far, far_packed, part = lax.optimization_barrier((far, far_packed, part))
+            weights.append(part)
+        else:
+            far, far_packed = lax.optimization_barrier((far, far_packed))
         bit = (v >> b) & 1
         first = bit == r if b == bits - 1 else bit == 0
         h = jnp.stack([jnp.where(first, h, far), jnp.where(first, far, h)], axis=1)
@@ -380,38 +432,46 @@
     ht = h.T
 
     parts = []
-    for chunk in chunks:
-        own, send = _partial_logits(h, weights, chunk)
+    for i, (start, size) in enumerate(chunks):
+        g = 0 if i in groups[0] else 1
+        own, send = _partial_logits(h, weights[g], (start - starts[g], size))
         parts.append((own, lax.ppermute(send, "row", swap)))
     es, stats = [], []
     picks = rows = None
     for i, (own, recv) in enumerate(parts):
         e, picks, stat, *rest = _exponentials(
-            own, recv, chunks, i, terms, packed=packed, rows=rows, picks=picks, before=stats
+            own, recv, chunks, i, terms, packed=packed, rows=rows, picks=picks, before=stats, kept=[*weights, *es]
         )
         if i == 0:
             rows = rest
         es.append(e)
         stats.append(stat)
-    joined = rest[0][:4]
     ids, lps = rows
 
+    scale = row_weight * valid.astype(F32)
+    joined = jnp.concatenate([rest[0][:4], scale[None], jnp.zeros((3, half), F32)], axis=0)
     for b in range(bits):
-        joined = _join_stats(joined, lax.ppermute(joined, "vocab", _xor(count, 1 << b)))
-    scale = row_weight * valid.astype(F32)
-    tot = jnp.concatenate([joined, scale[None], jnp.zeros((3, half), F32)], axis=0)
+        far = lax.ppermute(joined, "vocab", _xor(count, 1 << b))
+        joined = _join_stats(joined, far, [*weights, *es, *stats, picks, ids, lps])
 
     grads = []
     for group in groups:
         own = _logit_grad(
-            [es[q] for q in group], [stats[q] for q in group], picks, ids, lps, tot, [chunks[q] for q in group], terms
+            [es[q] for q in group],
+            [stats[q] for q in group],
+            picks,
+            ids,
+            lps,
+            joined,
+            [chunks[q] for q in group],
+            terms,
+            weights,
         )
         grads.append((own, lax.ppermute(own, "row", swap)))
 
     order = (jnp.arange(count, dtype=jnp.int32) ^ v) ^ (r * (count // 2))
-    starts = [chunks[group[0]][0] for group in groups]
-    (before,) = _feature_terms(*grads[0], weights, starts[0])
-    keep, send = _feature_terms(*grads[1], weights, starts[1], before, order)
+    (before,) = _feature_terms(*grads[0], weights[0])
+    keep, send = _feature_terms(*grads[1], weights[1], before, order)
 
     keep = keep + lax.ppermute(send, "vocab", _xor(count, 1)).astype(F32)
     keep = keep.reshape((count // 2,) + hidden.shape)

time: 112 us -> 102 us (0.911)
  waiting for transfers between devices: 23.5 us -> 14.5 us
  local copies, waits for them, and re-layouts: 19 us -> 13.9 us
  Pallas kernels: 44 us -> 48.9 us
    ppermute x3, waiting for transfers between devices: 12.1 us -> 4.81 us  [per_device(): far_packed = lax.ppermute(packed, 'vocab', _xor(count, 1 << b))]
    unnamed x28, local copies, waits for them, and re-layouts: 18.7 us -> 12.8 us
    pallas_call x14 -> x19, Pallas kernels: 44 us -> 48.9 us  [_call(): pl.pallas_call(body, in_specs=specs, out_specs=out_specs or [LOCAL] * len...]
    ppermute x4, waiting for transfers between devices: 2.67 us -> 1.15 us  [per_device(): parts.append((own, lax.ppermute(send, 'row', swap)))]
  transfers between devices with their start and end apart: 19 -> 19, of which waited for: 8 -> 6; matrix products, arithmetic and copies ran while one was open for 2% -> 3% of each run, Pallas kernels for 26% -> 37%
where the time goes in v3:
time: 102 us; the launch traced here: 101 us
  Pallas kernels  48.9 us (48%)
  starting transfers between devices  18.1 us (18%)
  waiting for transfers between devices  14.5 us (14%)
  local copies, waits for them, and re-layouts  13.9 us (14%)
  other arithmetic  4.94 us (5%)
    pallas_call x19, Pallas kernels, _call(): pl.pallas_call(body, in_specs=specs, out_specs=out_specs or [LOCAL] * len...  48.9 us
    unnamed x28, local copies, waits for them, and re-layouts  12.8 us
    ppermute x3, waiting for transfers between devices, per_device(): far = lax.ppermute(joined, 'vocab', _xor(count, 1 << b))  8.56 us
    ppermute x3, starting transfers between devices, per_device(): far = lax.ppermute(h, 'vocab', _xor(count, 1 << b))  7.33 us
    ppermute x3, waiting for transfers between devices, per_device(): far_packed = lax.ppermute(packed, 'vocab', _xor(count, 1 << b))  4.81 us
    ppermute x3, starting transfers between devices, per_device(): far = lax.ppermute(keep[d].astype(BF16), 'vocab', _xor(count, 2 * d))  3.55 us
    ppermute x3, starting transfers between devices, per_device(): far = lax.ppermute(joined, 'vocab', _xor(count, 1 << b))  3.3 us
  transfers between devices with their start and end apart: 19, of which 6 were waited for; matrix products, arithmetic and copies ran while one was open for 3% of the time, Pallas kernels for 37%

profile of v3, /device:TPU:0, one launch (start us, length us, event | category | flops | bytes accessed | tf_op | source)
XLA Modules:
  0.0 101.4 jit_solution(10721237435245622292)
XLA Ops:
  0.6 4.1 %collective-permute-start = (bf16[1,32,1024]{2,1,0:T(8,128)(2,1)}, bf16[1,32,1024]{2,1,0:T(8,128)(2,1)S(1)}, u32[]{:S(2)}, u32[]{:S(2)}) collective-permute-start(bf16[1,32,1024]{2,1,0:T(8,128)(2,1)} %bitcast.47), channel_id=1, source_target_pairs={{0,8},{2,10},{4,12},{6,14},{8,0},{10,2},{12,4},{14,6},{1,9},{3,11}... | collective-permute-start | bytes 196616 | tf_op jit(solution)/shard_map/ppermute | solution.py:414
  6.1 4.5 %collective-permute-done.1 = f32[2,4,128]{2,1,0:T(4,128)S(1)} collective-permute-done((f32[2,4,128]{2,1,0:T(4,128)S(1)}, f32[2,4,128]{2,1,0:T(4,128)S(1)}, u32[]{:S(2)}, u32[]{:S(2)}) %collective-permute-start.1) | collective-permute-done | bytes 4128 | tf_op jit(solution)/shard_map/ppermute | solution.py:415
  11.5 1.6 %collective-permute-start.2 = (bf16[2,32,1024]{2,1,0:T(8,128)(2,1)S(1)}, bf16[2,32,1024]{2,1,0:T(8,128)(2,1)S(1)}, u32[]{:S(2)}, u32[]{:S(2)}) collective-permute-start(bf16[2,32,1024]{2,1,0:T(8,128)(2,1)S(1)} %maximum_bitcast_fusion), channel_id=1, source_target_pairs={{0,4},{2,6},{4,0},{6,2},{8,12},{10,14},{12,8},{14,10},{1,5},{3,7},... | collective-permute-start | bytes 393224 | tf_op jit(solution)/shard_map/ppermute | solution.py:414
  14.3 4.0 %fetch_weight.2.w_ref.refs_3_.refs_5_.refs_8_.refs_0_.refs_2_ = bf16[1024,4864]{1,0:T(8,128)(2,1)S(1)} custom-call(bf16[1024,9728]{1,0:T(8,128)(2,1)} %w_ref.1), custom_call_target="tpu_custom_call" | custom-call | bytes 9961472 | tf_op jit(solution)/shard_map/fetch_weight/pallas_call | solution.py:31
  18.3 3.9 %copy-done = bf16[1024,4864]{1,0:T(8,128)(2,1)} copy-done((bf16[1024,4864]{1,0:T(8,128)(2,1)}, bf16[1024,4864]{1,0:T(8,128)(2,1)S(1)}, u32[]{:S(2)}) %copy-start) | copy-done | bytes 9961496
  22.3 1.6 %collective-permute-start.4 = (bf16[4,32,1024]{2,1,0:T(8,128)(2,1)S(1)}, bf16[4,32,1024]{2,1,0:T(8,128)(2,1)S(1)}, u32[]{:S(2)}, u32[]{:S(2)}) collective-permute-start(bf16[4,32,1024]{2,1,0:T(8,128)(2,1)S(1)} %bitcast.46), channel_id=1, source_target_pairs={{0,2},{2,0},{4,6},{6,4},{8,10},{10,8},{12,14},{14,12},{1,3},{3,1},... | collective-permute-start | bytes 786440 | tf_op jit(solution)/shard_map/ppermute | solution.py:414
  24.5 4.1 %fetch_weight.3.w_ref.refs_4_.refs_6_.refs_9_.refs_1_.refs_2_ = bf16[1024,4864]{1,0:T(8,128)(2,1)S(1)} custom-call(bf16[1024,9728]{1,0:T(8,128)(2,1)} %w_ref.1), custom_call_target="tpu_custom_call" | custom-call | bytes 9961472 | tf_op jit(solution)/shard_map/fetch_weight/pallas_call | solution.py:31
  29.1 1.5 %partial_logits.7 = (f32[128,2560]{1,0:T(8,128)S(1)}, f32[128,2560]{1,0:T(8,128)S(1)}) custom-call(bf16[256,1024]{1,0:T(8,128)(2,1)S(1)} %bitcast.39, bf16[1024,4864]{1,0:T(8,128)(2,1)S(1)} %fetch_weight.3.w_ref.refs_4_.refs_6_.refs_9_.refs_1_.refs_2_), custom_call_target="tpu_custom_call" | custom-call | flops 1342177280 | bytes 7864320 | tf_op jit(solution)/shard_map/partial_logits/pallas_call | solution.py:31
  30.8 3.2 %slice-done.2 = s8[4194304]{0:T(1024)(128)(4,1)S(1)} async-done(((s8[9961472]{0:T(1024)(128)(4,1)}), s8[4194304]{0:T(1024)(128)(4,1)S(1)}, s32[]{:S(2)}) %slice-start.2) | async-done | bytes 4194328
  40.2 1.6 %exponentials.4 = (f32[128,2304]{1,0:T(8,128)S(1)}, f32[128,128]{1,0:T(8,128)S(1)}, f32[128,128]{1,0:T(8,128)S(1)}, s32[128,128]{1,0:T(8,128)S(1)}, f32[128,128]{1,0:T(8,128)S(1)}) custom-call(f32[128,2304]{1,0:T(8,128)S(1)} %get-tuple-element.52.refs_0_, f32[128,2304]{1,0:T(8,128)S(1)} %collective-permute-done.7.refs_1_, ...), custom_call_target="tpu_custom_call" | custom-call | flops 2359296 | bytes 3538944 | tf_op jit(solution)/shard_map/exponentials/pallas_call | solution.py:31
  44.9 1.9 %exponentials.7 = (f32[128,2560]{1,0:T(8,128)S(1)}, f32[128,128]{1,0:T(8,128)S(1)}, f32[128,128]{1,0:T(8,128)S(1)}, f32[8,128]{1,0:T(8,128)S(1)}) custom-call(f32[128,2560]{1,0:T(8,128)S(1)} %get-tuple-element.64.refs_0_, f32[128,2560]{1,0:T(8,128)S(1)} %collective-permute-done.9.refs_1_, s32[128,128]{1,0:T(8,128)S(1)} %get-tuple-element.55.refs_2_.refs_11_.refs_5_, ...), custom_call_target="tpu_custom_call" | custom-call | flops 2621440 | bytes 3932160 | tf_op jit(solution)/shard_map/exponentials/pallas_call | solution.py:31
  48.3 2.1 %collective-permute-done.10.b_ref = f32[8,128]{1,0:T(8,128)S(1)} collective-permute-done((f32[8,128]{1,0:T(8,128)S(1)}, f32[8,128]{1,0:T(8,128)S(1)}, u32[]{:S(2)}, u32[]{:S(2)}) %collective-permute-start.10) | collective-permute-done | bytes 4128 | tf_op jit(solution)/shard_map/ppermute | solution.py:454
  50.4 1.6 %collective-permute-start.11 = (f32[8,128]{1,0:T(8,128)S(1)}, f32[8,128]{1,0:T(8,128)S(1)}, u32[]{:S(2)}, u32[]{:S(2)}) collective-permute-start(f32[8,128]{1,0:T(8,128)S(1)} %join_stats.3.a_ref), channel_id=1, source_target_pairs={{0,4},{2,6},{4,0},{6,2},{8,12},{10,14},{12,8},{14,10},{1,5},{3,7},... | collective-permute-start | bytes 12296 | tf_op jit(solution)/shard_map/ppermute | solution.py:454
  52.1 2.1 %collective-permute-done.11.b_ref = f32[8,128]{1,0:T(8,128)S(1)} collective-permute-done((f32[8,128]{1,0:T(8,128)S(1)}, f32[8,128]{1,0:T(8,128)S(1)}, u32[]{:S(2)}, u32[]{:S(2)}) %collective-permute-start.11) | collective-permute-done | bytes 4128 | tf_op jit(solution)/shard_map/ppermute | solution.py:454
  54.3 4.4 %collective-permute-done.12.b_ref = f32[8,128]{1,0:T(8,128)S(1)} collective-permute-done((f32[8,128]{1,0:T(8,128)S(1)}, f32[8,128]{1,0:T(8,128)S(1)}, u32[]{:S(2)}, u32[]{:S(2)}) %collective-permute-start.12) | collective-permute-done | bytes 4128 | tf_op jit(solution)/shard_map/ppermute | solution.py:454
  58.7 2.8 %logit_grad.3.refs_0_.own_ref = bf16[128,4864]{1,0:T(8,128)(2,1)S(1)} custom-call(f32[128,2304]{1,0:T(8,128)S(1)} %get-tuple-element.60.refs_7_.refs_10_.refs_2_.refs_0_, f32[128,2560]{1,0:T(8,128)S(1)} %get-tuple-element.62.refs_8_.refs_11_.refs_3_.refs_1_, f32[128,128]{1,0:T(8,128)S(1)} %get-tuple-element.67.refs_5_.refs_6_.refs_2_, ...), custom_call_target="tpu_custom_call" | custom-call | flops 4980736 | bytes 3735552 | tf_op jit(solution)/shard_map/logit_grad/pallas_call | solution.py:31
  61.6 4.0 %logit_grad.2.refs_0_.own_ref = bf16[128,4864]{1,0:T(8,128)(2,1)} custom-call(f32[128,2304]{1,0:T(8,128)S(1)} %get-tuple-element.63.refs_12_.refs_4_.refs_0_, f32[128,2560]{1,0:T(8,128)S(1)} %get-tuple-element.70.refs_5_.refs_1_, f32[128,128]{1,0:T(8,128)S(1)} %get-tuple-element.69.refs_7_.refs_8_.refs_2_, f32[128,128]{1,0:T(8,128)S(1)} %get-tuple-element.71.refs_9_.refs_3_, ...), custom_call_target="tpu_custom_call" | custom-call | flops 4980736 | bytes 3735552 | tf_op jit(solution)/shard_map/logit_grad/pallas_call | solution.py:31
  66.2 3.8 %copy-done.1 = bf16[1024,4864]{1,0:T(8,128)(2,1)S(1)} copy-done((bf16[1024,4864]{1,0:T(8,128)(2,1)S(1)}, bf16[1024,4864]{1,0:T(8,128)(2,1)}, u32[]{:S(2)}) %copy-start.1) | copy-done | bytes 9961496
  70.0 4.2 %feature_terms.2.refs_3_ = f32[256,1024]{1,0:T(8,128)S(1)} custom-call(bf16[128,4864]{1,0:T(8,128)(2,1)S(1)} %logit_grad.3.refs_0_.own_ref, bf16[128,4864]{1,0:T(8,128)(2,1)} %collective-permute-done.14.refs_1_.other_ref, bf16[1024,4864]{1,0:T(8,128)(2,1)S(1)} %copy-done.1), custom_call_target="tpu_custom_call" | custom-call | flops 2550136832 | bytes 12451840 | tf_op jit(solution)/shard_map/feature_terms/pallas_call | solution.py:31
  74.2 4.8 %feature_terms.3 = (f32[128,1024]{1,0:T(8,128)S(1)}, bf16[128,1024]{1,0:T(8,128)(2,1)}) custom-call(bf16[128,4864]{1,0:T(8,128)(2,1)} %logit_grad.2.refs_0_.own_ref, bf16[128,4864]{1,0:T(8,128)(2,1)S(1)} %collective-permute-done.13.refs_1_.other_ref, bf16[1024,4864]{1,0:T(8,128)(2,1)S(1)} %copy-done.3, f32[256,1024]{1,0:T(8,128)S(1)} %feature_terms.2.refs_3_, ...), custom_call_target="tpu_custom_call" | custom-call | flops 2550136832 | bytes 12451840 | tf_op jit(solution)/shard_map/feature_terms/pallas_call | solution.py:31
  83.4 6.3 %weight_grad.2.refs_0_ = bf16[1024,9728]{1,0:T(8,128)(2,1)} custom-call(bf16[1024,256]{1,0:T(8,128)(2,1)S(1)} %bitcast.44, bf16[128,4864]{1,0:T(8,128)(2,1)S(1)} %logit_grad.3.refs_0_.own_ref, bf16[128,4864]{1,0:T(8,128)(2,1)} %collective-permute-done.14.refs_1_.other_ref), custom_call_target="tpu_custom_call" | custom-call | flops 2550136832 | bytes 12451840 | tf_op jit(solution)/shard_map/weight_grad/pallas_call | solution.py:31
  90.9 1.6 %collective-permute-start.16 = (bf16[32,1024]{1,0:T(8,128)(2,1)S(1)}, bf16[32,1024]{1,0:T(8,128)(2,1)S(1)}, u32[]{:S(2)}, u32[]{:S(2)}) collective-permute-start(bf16[32,1024]{1,0:T(8,128)(2,1)S(1)} %get-tuple-element.80), channel_id=1, source_target_pairs={{0,4},{2,6},{4,0},{6,2},{8,12},{10,14},{12,8},{14,10},{1,5},{3,7},... | collective-permute-start | bytes 196616 | tf_op jit(solution)/shard_map/ppermute | solution.py:480
  92.8 1.6 %collective-permute-start.17 = (bf16[32,1024]{1,0:T(8,128)(2,1)S(1)}, bf16[32,1024]{1,0:T(8,128)(2,1)S(1)}, u32[]{:S(2)}, u32[]{:S(2)}) collective-permute-start(bf16[32,1024]{1,0:T(8,128)(2,1)S(1)} %get-tuple-element.82), channel_id=1, source_target_pairs={{0,8},{2,10},{4,12},{6,14},{8,0},{10,2},{12,4},{14,6},{1,9},{3,11}... | collective-permute-start | bytes 196616 | tf_op jit(solution)/shard_map/ppermute | solution.py:480
  94.4 6.3 %weight_grad.3 = bf16[1024,9728]{1,0:T(8,128)(2,1)} custom-call(bf16[1024,256]{1,0:T(8,128)(2,1)S(1)} %bitcast.45, bf16[128,4864]{1,0:T(8,128)(2,1)} %logit_grad.2.refs_0_.own_ref, bf16[128,4864]{1,0:T(8,128)(2,1)S(1)} %collective-permute-done.13.refs_1_.other_ref, bf16[1024,9728]{1,0:T(8,128)(2,1)} %weight_grad.2.refs_0_), custom_call_target="tpu_custom_call", output_to_operand_aliasing={{}: (3, {})} | custom-call | flops 2550136832 | bytes 12451840 | tf_op jit(solution)/shard_map/weight_grad/pallas_call | solution.py:31
  (85 shorter events, 22.7 us)
Async XLA Ops:
  0.6 10.0 %collective-permute-start = (bf16[1,32,1024]{2,1,0:T(8,128)(2,1)}, bf16[1,32,1024]{2,1,0:T(8,128)(2,1)S(1)}, u32[]{:S(2)}, u32[]{:S(2)}) collective-permute-start(bf16[1,32,1024]{2,1,0:T(8,128)(2,1)} %bitcast.47), channel_id=1, source_target_pairs={{0,8},{2,10},{4,12},{6,14},{8,0},{10,2},{12,4},{14,6},{1,9},{3,11}... | collective-permute-start | bytes 196616 | tf_op jit(solution)/shard_map/ppermute | solution.py:414
  6.1 4.5 %collective-permute-start.1 = (f32[2,4,128]{2,1,0:T(4,128)S(1)}, f32[2,4,128]{2,1,0:T(4,128)S(1)}, u32[]{:S(2)}, u32[]{:S(2)}) collective-permute-start(f32[2,4,128]{2,1,0:T(4,128)S(1)} %pad_maximum_fusion.4), channel_id=1, source_target_pairs={{0,8},{2,10},{4,12},{6,14},{8,0},{10,2},{12,4},{14,6},{1,9},{3,11}... | collective-permute-start | bytes 12296 | tf_op jit(solution)/shard_map/ppermute | solution.py:415
  11.5 10.7 %collective-permute-start.2 = (bf16[2,32,1024]{2,1,0:T(8,128)(2,1)S(1)}, bf16[2,32,1024]{2,1,0:T(8,128)(2,1)S(1)}, u32[]{:S(2)}, u32[]{:S(2)}) collective-permute-start(bf16[2,32,1024]{2,1,0:T(8,128)(2,1)S(1)} %maximum_bitcast_fusion), channel_id=1, source_target_pairs={{0,4},{2,6},{4,0},{6,2},{8,12},{10,14},{12,8},{14,10},{1,5},{3,7},... | collective-permute-start | bytes 393224 | tf_op jit(solution)/shard_map/ppermute | solution.py:414
  13.8 8.4 %collective-permute-start.3 = (f32[2,8,128]{2,1,0:T(8,128)S(1)}, f32[2,8,128]{2,1,0:T(8,128)S(1)}, u32[]{:S(2)}, u32[]{:S(2)}) collective-permute-start(f32[2,8,128]{2,1,0:T(8,128)S(1)} %pad_maximum_fusion.3), channel_id=1, source_target_pairs={{0,4},{2,6},{4,0},{6,2},{8,12},{10,14},{12,8},{14,10},{1,5},{3,7},... | collective-permute-start | bytes 24584 | tf_op jit(solution)/shard_map/ppermute | solution.py:415
  14.3 9.6 %copy-start.7 = (f32[128,4]{0,1:T(4,128)S(1)}, f32[128,4]{0,1:T(4,128)}, u32[]{:S(2)}) copy-start(f32[128,4]{0,1:T(4,128)} %param.10) | copy-start | bytes 6148
  14.3 10.2 %copy-start.10 = (f32[2]{0:T(128)S(1)}, f32[2]{0:T(128)}, u32[]{:S(2)}) copy-start(f32[2]{0:T(128)} %constant.22.clone) | copy-start | bytes 28
  22.2 8.5 %slice-start = ((s8[9961472]{0:T(1024)(128)(4,1)}), s8[1572864]{0:T(1024)(128)(4,1)S(1)}, s32[]{:S(2)}) async-start(s8[9961472]{0:T(1024)(128)(4,1)} %bitcast.37), calls=%async_computation | async-start | bytes 3145728
  22.3 6.6 %collective-permute-start.4 = (bf16[4,32,1024]{2,1,0:T(8,128)(2,1)S(1)}, bf16[4,32,1024]{2,1,0:T(8,128)(2,1)S(1)}, u32[]{:S(2)}, u32[]{:S(2)}) collective-permute-start(bf16[4,32,1024]{2,1,0:T(8,128)(2,1)S(1)} %bitcast.46), channel_id=1, source_target_pairs={{0,2},{2,0},{4,6},{6,4},{8,10},{10,8},{12,14},{14,12},{1,3},{3,1},... | collective-permute-start | bytes 786440 | tf_op jit(solution)/shard_map/ppermute | solution.py:414
  23.9 5.0 %collective-permute-start.5 = (f32[2,16,128]{2,1,0:T(8,128)S(1)}, f32[2,16,128]{2,1,0:T(8,128)S(1)}, u32[]{:S(2)}, u32[]{:S(2)}) collective-permute-start(f32[2,16,128]{2,1,0:T(8,128)S(1)} %pad_maximum_fusion.2), channel_id=1, source_target_pairs={{0,2},{2,0},{4,6},{6,4},{8,10},{10,8},{12,14},{14,12},{1,3},{3,1},... | collective-permute-start | bytes 49160 | tf_op jit(solution)/shard_map/ppermute | solution.py:415
  24.5 9.5 %slice-start.2 = ((s8[9961472]{0:T(1024)(128)(4,1)}), s8[4194304]{0:T(1024)(128)(4,1)S(1)}, s32[]{:S(2)}) async-start(s8[9961472]{0:T(1024)(128)(4,1)} %bitcast.37), calls=%async_computation.2 | async-start | bytes 8388608
  28.6 33.1 %copy-start.2 = (bf16[1024,4864]{1,0:T(8,128)(2,1)}, bf16[1024,4864]{1,0:T(8,128)(2,1)S(1)}, u32[]{:S(2)}) copy-start(bf16[1024,4864]{1,0:T(8,128)(2,1)S(1)} %fetch_weight.3.w_ref.refs_4_.refs_6_.refs_9_.refs_1_.refs_2_) | copy-start | bytes 29884420
  30.7 14.2 %collective-permute-start.9 = (f32[128,2560]{1,0:T(8,128)S(1)}, f32[128,2560]{1,0:T(8,128)S(1)}, u32[]{:S(2)}, u32[]{:S(2)}) collective-permute-start(f32[128,2560]{1,0:T(8,128)S(1)} %get-tuple-element.65), channel_id=1, source_target_pairs={{0,1},{1,0},{2,3},{3,2},{4,5},{5,4},{6,7},{7,6},{8,9},{9,8},{10,11... | collective-permute-start | bytes 3932168 | tf_op jit(solution)/shard_map/ppermute | solution.py:438
  35.5 6.4 %collective-permute-start.8 = (f32[128,2560]{1,0:T(8,128)S(1)}, f32[128,2560]{1,0:T(8,128)S(1)}, u32[]{:S(2)}, u32[]{:S(2)}) collective-permute-start(f32[128,2560]{1,0:T(8,128)S(1)} %get-tuple-element.58), channel_id=1, source_target_pairs={{0,1},{1,0},{2,3},{3,2},{4,5},{5,4},{6,7},{7,6},{8,9},{9,8},{10,11... | collective-permute-start | bytes 3932168 | tf_op jit(solution)/shard_map/ppermute | solution.py:438
  37.0 3.3 %collective-permute-start.7 = (f32[128,2304]{1,0:T(8,128)S(1)}, f32[128,2304]{1,0:T(8,128)S(1)}, u32[]{:S(2)}, u32[]{:S(2)}) collective-permute-start(f32[128,2304]{1,0:T(8,128)S(1)} %get-tuple-element.53), channel_id=1, source_target_pairs={{0,1},{1,0},{2,3},{3,2},{4,5},{5,4},{6,7},{7,6},{8,9},{9,8},{10,11... | collective-permute-start | bytes 3538952 | tf_op jit(solution)/shard_map/ppermute | solution.py:438
  38.9 4.4 %collective-permute-start.6 = (f32[128,2304]{1,0:T(8,128)S(1)}, f32[128,2304]{1,0:T(8,128)S(1)}, u32[]{:S(2)}, u32[]{:S(2)}) collective-permute-start(f32[128,2304]{1,0:T(8,128)S(1)} %get-tuple-element.50), channel_id=1, source_target_pairs={{0,1},{1,0},{2,3},{3,2},{4,5},{5,4},{6,7},{7,6},{8,9},{9,8},{10,11... | collective-permute-start | bytes 3538952 | tf_op jit(solution)/shard_map/ppermute | solution.py:438
  46.8 3.6 %collective-permute-start.10 = (f32[8,128]{1,0:T(8,128)S(1)}, f32[8,128]{1,0:T(8,128)S(1)}, u32[]{:S(2)}, u32[]{:S(2)}) collective-permute-start(f32[8,128]{1,0:T(8,128)S(1)} %maximum_maximum_fusion.a_ref), channel_id=1, source_target_pairs={{0,2},{2,0},{4,6},{6,4},{8,10},{10,8},{12,14},{14,12},{1,3},{3,1},... | collective-permute-start | bytes 12296 | tf_op jit(solution)/shard_map/ppermute | solution.py:454
  50.4 3.7 %collective-permute-start.11 = (f32[8,128]{1,0:T(8,128)S(1)}, f32[8,128]{1,0:T(8,128)S(1)}, u32[]{:S(2)}, u32[]{:S(2)}) collective-permute-start(f32[8,128]{1,0:T(8,128)S(1)} %join_stats.3.a_ref), channel_id=1, source_target_pairs={{0,4},{2,6},{4,0},{6,2},{8,12},{10,14},{12,8},{14,10},{1,5},{3,7},... | collective-permute-start | bytes 12296 | tf_op jit(solution)/shard_map/ppermute | solution.py:454
  54.1 4.6 %collective-permute-start.12 = (f32[8,128]{1,0:T(8,128)S(1)}, f32[8,128]{1,0:T(8,128)S(1)}, u32[]{:S(2)}, u32[]{:S(2)}) collective-permute-start(f32[8,128]{1,0:T(8,128)S(1)} %join_stats.4.a_ref), channel_id=1, source_target_pairs={{0,8},{2,10},{4,12},{6,14},{8,0},{10,2},{12,4},{14,6},{1,9},{3,11}... | collective-permute-start | bytes 12296 | tf_op jit(solution)/shard_map/ppermute | solution.py:454
  61.6 4.6 %collective-permute-start.14 = (bf16[128,4864]{1,0:T(8,128)(2,1)S(1)}, bf16[128,4864]{1,0:T(8,128)(2,1)}, u32[]{:S(2)}, u32[]{:S(2)}) collective-permute-start(bf16[128,4864]{1,0:T(8,128)(2,1)S(1)} %logit_grad.3.refs_0_.own_ref), channel_id=1, source_target_pairs={{0,1},{1,0},{2,3},{3,2},{4,5},{5,4},{6,7},{7,6},{8,9},{9,8},{10,11... | collective-permute-start | bytes 3735560 | tf_op jit(solution)/shard_map/ppermute | solution.py:470
  65.7 8.5 %collective-permute-start.13 = (bf16[128,4864]{1,0:T(8,128)(2,1)}, bf16[128,4864]{1,0:T(8,128)(2,1)S(1)}, u32[]{:S(2)}, u32[]{:S(2)}) collective-permute-start(bf16[128,4864]{1,0:T(8,128)(2,1)} %logit_grad.2.refs_0_.own_ref), channel_id=1, source_target_pairs={{0,1},{1,0},{2,3},{3,2},{4,5},{5,4},{6,7},{7,6},{8,9},{9,8},{10,11... | collective-permute-start | bytes 3735560 | tf_op jit(solution)/shard_map/ppermute | solution.py:470
  79.9 9.9 %collective-permute-start.15 = (bf16[128,1024]{1,0:T(8,128)(2,1)}, bf16[128,1024]{1,0:T(8,128)(2,1)}, u32[]{:S(2)}, u32[]{:S(2)}) collective-permute-start(bf16[128,1024]{1,0:T(8,128)(2,1)} %get-tuple-element.75), channel_id=1, source_target_pairs={{0,2},{2,0},{4,6},{6,4},{8,10},{10,8},{12,14},{14,12},{1,3},{3,1},... | collective-permute-start | bytes 786440 | tf_op jit(solution)/shard_map/ppermute | solution.py:476
  90.9 9.8 %collective-permute-start.16 = (bf16[32,1024]{1,0:T(8,128)(2,1)S(1)}, bf16[32,1024]{1,0:T(8,128)(2,1)S(1)}, u32[]{:S(2)}, u32[]{:S(2)}) collective-permute-start(bf16[32,1024]{1,0:T(8,128)(2,1)S(1)} %get-tuple-element.80), channel_id=1, source_target_pairs={{0,4},{2,6},{4,0},{6,2},{8,12},{10,14},{12,8},{14,10},{1,5},{3,7},... | collective-permute-start | bytes 196616 | tf_op jit(solution)/shard_map/ppermute | solution.py:480
  92.5 8.2 %collective-permute-start.18 = (bf16[32,1024]{1,0:T(8,128)(2,1)S(1)}, bf16[32,1024]{1,0:T(8,128)(2,1)S(1)}, u32[]{:S(2)}, u32[]{:S(2)}) collective-permute-start(bf16[32,1024]{1,0:T(8,128)(2,1)S(1)} %get-tuple-element.81), channel_id=1, source_target_pairs={{0,12},{2,14},{4,8},{6,10},{8,4},{10,6},{12,0},{14,2},{1,13},{3,15... | collective-permute-start | bytes 196616 | tf_op jit(solution)/shard_map/ppermute | solution.py:480
  92.8 7.9 %collective-permute-start.17 = (bf16[32,1024]{1,0:T(8,128)(2,1)S(1)}, bf16[32,1024]{1,0:T(8,128)(2,1)S(1)}, u32[]{:S(2)}, u32[]{:S(2)}) collective-permute-start(bf16[32,1024]{1,0:T(8,128)(2,1)S(1)} %get-tuple-element.82), channel_id=1, source_target_pairs={{0,8},{2,10},{4,12},{6,14},{8,0},{10,2},{12,4},{14,6},{1,9},{3,11}... | collective-permute-start | bytes 196616 | tf_op jit(solution)/shard_map/ppermute | solution.py:480
  (9 other events, 30.8 us)

commit v4 on v3

--- a/solution.py
+++ b/solution.py
@@ -7,13 +7,14 @@
 from jax.experimental.pallas import tpu as pltpu
 from jax.sharding import PartitionSpec as P
 
-VMEM_LIMIT = 14 * 1024 * 1024
+MIB = 1024 * 1024
 TILE = 8
 STEP = 16
 NT = (((1,), (1,)), ((), ()))
 F32 = jnp.float32
 BF16 = jnp.bfloat16
 LOCAL = pl.BlockSpec(memory_space=pltpu.VMEM)
+REMOTE = pl.BlockSpec(memory_space=pltpu.HBM)
 WRITES = 4
 
 
@@ -25,9 +26,12 @@
     return pl.CostEstimate(flops=int(flops), bytes_accessed=int(nbytes), transcendentals=0)
 
 
-def _call(body, name, args, out_shape, cost, specs=None, out_specs=None, scratch=(), aliases=None):
+def _call(body, name, args, out_shape, cost, specs=None, out_specs=None, scratch=(), aliases=None, limit=8):
     specs = specs or [LOCAL] * len(args)
-    args = [_local(x) if s is LOCAL else x for x, s in zip(args, specs)]
+    args = [
+        _local(x) if s is LOCAL else pltpu.with_memory_space_constraint(x, pltpu.HBM) if s is REMOTE else x
+        for x, s in zip(args, specs)
+    ]
     return pl.pallas_call(
         body,
         in_specs=specs,
@@ -35,7 +39,7 @@
         out_shape=out_shape,
         scratch_shapes=list(scratch),
         input_output_aliases=aliases or {},
-        compiler_params=pltpu.CompilerParams(vmem_limit_bytes=VMEM_LIMIT),
+        compiler_params=pltpu.CompilerParams(vmem_limit_bytes=limit * MIB),
         cost_estimate=cost,
         name=name,
     )(*args)
@@ -57,24 +61,74 @@
     return [(i, i ^ s) for i in range(n)]
 
 
-def _logits_body(start, h_ref, w_ref, own_ref, send_ref):
+def _copies(w_ref, start, out_ref, sems):
+    depth, width = out_ref.shape
+    step = depth // sems.shape[0]
+    return [
+        pltpu.make_async_copy(
+            w_ref.at[pl.ds(i * step, step), pl.ds(start, width)], out_ref.at[pl.ds(i * step, step), :], sems.at[i]
+        )
+        for i in range(sems.shape[0])
+    ]
+
+
+def _fetch_body(start, w_ref, out_ref, sems):
+    copies = _copies(w_ref, start, out_ref, sems)
+    for copy in copies:
+        copy.start()
+    for copy in copies:
+        copy.wait()
+
+
+def _fetch(w, start, width):
+    depth = w.shape[0]
+    return _call(
+        functools.partial(_fetch_body, start),
+        "fetch_weight",
+        [w],
+        [pltpu.VMEM((depth, width), BF16)],
+        _cost(0, 2 * depth * width),
+        specs=[REMOTE],
+        scratch=[pltpu.SemaphoreType.DMA((4,))],
+    )[0]
+
+
+def _logits_body(start, after, h_ref, w_ref, *refs):
+    if after is not None:
+        source_ref, own_ref, send_ref, next_ref, sems = refs
+        copies = _copies(source_ref, after, next_ref, sems)
+        for copy in copies:
+            copy.start()
+    else:
+        own_ref, send_ref = refs
     half = own_ref.shape[0]
     for at, size in _blocks(own_ref.shape[1], 1280):
         part = jnp.dot(h_ref[...], w_ref[:, start + at : start + at + size], preferred_element_type=F32)
         own_ref[:, at : at + size] = part[:half]
         send_ref[:, at : at + size] = part[half:]
-
-
-def _partial_logits(h, w, chunk):
+    if after is not None:
+        for copy in copies:
+            copy.wait()
+
+
+def _partial_logits(h, w, chunk, source=None, after=None):
     start, width = chunk
     rows, depth = h.shape
     out = pltpu.VMEM((rows // 2, width), F32)
-    return _call(
-        functools.partial(_logits_body, start),
+    args, specs, outs, scratch = [h, w], [LOCAL, LOCAL], [out, out], []
+    if after is not None:
+        args.append(source)
+        specs.append(REMOTE)
+        outs.append(pltpu.VMEM((depth, after[1]), BF16))
+        scratch = [pltpu.SemaphoreType.DMA((4,))]
+    return _call(
+        functools.partial(_logits_body, start, after and after[0]),
         "partial_logits",
-        [h, w],
-        [out, out],
+        args,
+        outs,
         _cost(2 * rows * depth * width, 2 * depth * width + 4 * rows * width),
+        specs=specs,
+        scratch=scratch,
     )
 
 
@@ -194,36 +248,6 @@
     )[0]
 
 
-def _fetch_body(start, w_ref, out_ref, sems):
-    depth = w_ref.shape[0]
-    step = depth // sems.shape[0]
-    copies = [
-        pltpu.make_async_copy(
-            w_ref.at[pl.ds(i * step, step), pl.ds(start, out_ref.shape[1])],
-            out_ref.at[pl.ds(i * step, step), :],
-            sems.at[i],
-        )
-        for i in range(sems.shape[0])
-    ]
-    for copy in copies:
-        copy.start()
-    for copy in copies:
-        copy.wait()
-
-
-def _fetch(w, start, width):
-    depth = w.shape[0]
-    return _call(
-        functools.partial(_fetch_body, start),
-        "fetch_weight",
-        [pltpu.with_memory_space_constraint(w, pltpu.HBM)],
-        [pltpu.VMEM((depth, width), BF16)],
-        _cost(0, 2 * depth * width),
-        specs=[pl.BlockSpec(memory_space=pltpu.HBM)],
-        scratch=[pltpu.SemaphoreType.DMA((4,))],
-    )[0]
-
-
 def _grad_body(chunks, terms, *refs):
     count = len(chunks)
     e_refs, stat_refs = refs[:count], refs[count : 2 * count]
@@ -293,31 +317,44 @@
     lax.fori_loop(0, half // STEP, step, 0, unroll=2)
 
 
-def _logit_grad(es, stats, picks, ids, lps, tot, chunks, terms, kept):
+def _logit_grad(es, stats, picks, ids, lps, tot, chunks, terms):
     half = es[0].shape[0]
     width = sum(w for _, w in chunks)
     table = pltpu.VMEM((half, 128), F32)
     return _call(
         functools.partial(_grad_body, chunks, terms),
         "logit_grad",
-        [*es, *stats, picks, ids, lps, tot, *kept],
+        [*es, *stats, picks, ids, lps, tot],
         [pltpu.VMEM((half, width), BF16)],
         _cost(8 * half * width, 6 * half * width),
         scratch=[pltpu.VMEM((len(chunks), half, 128), F32), table, table],
     )[0]
 
 
-def _feature_body(count, *refs):
+def _feature_body(start, block, count, *refs):
     if count:
-        own_ref, other_ref, w_ref, before_ref, order_ref, keep_ref, send_ref, acc = refs
+        own_ref, far_ref, w_ref, before_ref, order_ref, keep_ref, send_ref, acc, other, weights, sems = refs
     else:
-        own_ref, other_ref, w_ref, acc = refs
-    grads = jnp.concatenate([own_ref[...], other_ref[...]], axis=0)
-    part = lax.dot_general(grads, w_ref[...], NT, preferred_element_type=F32)
+        own_ref, far_ref, w_ref, acc, other, weights, sems = refs
+    blocks = _blocks(own_ref.shape[1], block)
+    copies = [pltpu.make_async_copy(far_ref, other, sems.at[len(blocks)])] + [
+        pltpu.make_async_copy(w_ref.at[:, pl.ds(start + at, size)], weights.at[:, pl.ds(at, size)], sems.at[i])
+        for i, (at, size) in enumerate(blocks)
+    ]
+    for copy in copies:
+        copy.start()
+    copies[0].wait()
+    for i, (at, size) in enumerate(blocks):
+        cols = slice(at, at + size)
+        grads = jnp.concatenate([own_ref[:, cols], other[:, cols]], axis=0)
+        copies[i + 1].wait()
+        part = lax.dot_general(grads, weights[:, cols], NT, preferred_element_type=F32)
+        if i:
+            acc[...] += part
+        else:
+            acc[...] = part + before_ref[...] if count else part
     if not count:
-        acc[...] = part
         return
-    acc[...] = part + before_ref[...]
     rows = acc.shape[0] // count
     near, far = [], []
     for d in range(count):
@@ -327,38 +364,47 @@
     send_ref[...] = jnp.concatenate(far, axis=0).astype(BF16)
 
 
-def _feature_terms(own, other, w, before=None, order=None):
+def _feature_terms(own, other, w, start, before=None, order=None):
     half, width = own.shape
     depth = w.shape[0]
+    block = 1024
     args = [own, other, w]
-    specs = [LOCAL] * 3
-    scratch = []
+    specs = [LOCAL, REMOTE, REMOTE]
+    scratch = [
+        pltpu.VMEM((half, width), BF16),
+        pltpu.VMEM((depth, width), BF16),
+        pltpu.SemaphoreType.DMA((len(_blocks(width, block)) + 1,)),
+    ]
     out = [pltpu.VMEM((2 * half, depth), F32)]
     if before is not None:
         args += [before, order]
         specs += [LOCAL, pl.BlockSpec(memory_space=pltpu.SMEM)]
-        scratch = out
+        scratch = out + scratch
         out = [pltpu.VMEM((half, depth), F32), pltpu.VMEM((half, depth), BF16)]
     return _call(
-        functools.partial(_feature_body, 0 if before is None else order.shape[0]),
+        functools.partial(_feature_body, start, block, 0 if before is None else order.shape[0]),
         "feature_terms",
         args,
         out,
         _cost(4 * half * depth * width, 2 * depth * width + 4 * half * width),
         specs=specs,
         scratch=scratch,
+        limit=20,
     )
 
 
-def _weight_body(start, block, ht_ref, own_ref, other_ref, *refs):
-    out_ref, ring, sems = refs[-3:]
+def _weight_body(start, block, ht_ref, own_ref, far_ref, *refs):
+    out_ref, ring, other, sems = refs[-4:]
+    fetch = pltpu.make_async_copy(far_ref, other, sems.at[WRITES])
+    fetch.start()
+    fetch.wait()
     copies = []
     for i, (at, size) in enumerate(_blocks(own_ref.shape[1], block)):
         slot = i % WRITES
         if i >= WRITES:
             copies[i - WRITES].wait()
         cols = slice(at, at + size)
-        grads = jnp.concatenate([own_ref[:, cols], other_ref[:, cols]], axis=0)
+        grads = jnp.concatenate([own_ref[:, cols], other[:, cols]], axis=0)
         ring[slot, :, :size] = jnp.dot(ht_ref[...], grads, preferred_element_type=F32).astype(BF16)
         copy = pltpu.make_async_copy(
             ring.at[slot, :, pl.ds(0, size)], out_ref.at[:, pl.ds(start + at, size)], sems.at[slot]
@@ -369,12 +415,12 @@
         copy.wait()
 
 
-def _weight_grad(ht, own, other, start, width_all, before=None):
+def _weight_grad(ht, own, other, start, width_all, before=None, kept=()):
     depth, rows = ht.shape
-    width = own.shape[1]
-    block = 512
+    half, width = own.shape
+    block = 1024
     args = [ht, own, other]
-    specs = [LOCAL] * 3
+    specs = [LOCAL, LOCAL, REMOTE]
     aliases = {}
     if before is not None:
         args.append(before)
@@ -383,13 +429,18 @@
     return _call(
         functools.partial(_weight_body, start, block),
         "weight_grad",
-        args,
+        [*args, *kept],
         [jax.ShapeDtypeStruct((depth, width_all), BF16)],
         _cost(2 * rows * depth * width, 2 * depth * width + 2 * rows * width),
-        specs=specs,
+        specs=specs + [LOCAL] * len(kept),
         out_specs=[pl.BlockSpec(memory_space=pl.ANY)],
-        scratch=[pltpu.VMEM((WRITES, depth, block), BF16), pltpu.SemaphoreType.DMA((WRITES,))],
+        scratch=[
+            pltpu.VMEM((WRITES, depth, block), BF16),
+            pltpu.VMEM((half, width), BF16),
+            pltpu.SemaphoreType.DMA((WRITES + 1,)),
+        ],
         aliases=aliases,
+        limit=16,
     )[0]
 
 
@@ -409,16 +460,13 @@
 
     h = hidden[None]
     packed = jnp.stack([teacher_ids.T.astype(F32), teacher_logprobs.T])
-    weights = []
     for b in reversed(range(bits)):
         far = lax.ppermute(h, "vocab", _xor(count, 1 << b))
         far_packed = lax.ppermute(packed, "vocab", _xor(count, 1 << b))
-        if b < 2:
-            g = len(weights)
+        if b == 0:
             _, source = lax.optimization_barrier((h, head_weight))
-            part = _fetch(source, starts[g], widths[g])
-            far, far_packed, part = lax.optimization_barrier((far, far_packed, part))
-            weights.append(part)
+            weights = _fetch(source, starts[0], widths[0])
+            far, far_packed, weights = lax.optimization_barrier((far, far_packed, weights))
         else:
             far, far_packed = lax.optimization_barrier((far, far_packed))
         bit = (v >> b) & 1
@@ -431,16 +479,20 @@
     h, packed = lax.optimization_barrier((h, packed))
     ht = h.T
 
-    parts = []
+    parts, ready = [], {}
     for i, (start, size) in enumerate(chunks):
-        g = 0 if i in groups[0] else 1
-        own, send = _partial_logits(h, weights[g], (start - starts[g], size))
+        if i in groups[0]:
+            own, send, ready[i] = _partial_logits(
+                h, weights, (start, size), head_weight, chunks[i + len(groups[0])]
+            )
+        else:
+            own, send = _partial_logits(h, ready[i - len(groups[0])], (0, size))
         parts.append((own, lax.ppermute(send, "row", swap)))
     es, stats = [], []
     picks = rows = None
     for i, (own, recv) in enumerate(parts):
         e, picks, stat, *rest = _exponentials(
-            own, recv, chunks, i, terms, packed=packed, rows=rows, picks=picks, before=stats, kept=[*weights, *es]
+            own, recv, chunks, i, terms, packed=packed, rows=rows, picks=picks, before=stats, kept=es
         )
         if i == 0:
             rows = rest
@@ -452,7 +504,7 @@
     joined = jnp.concatenate([rest[0][:4], scale[None], jnp.zeros((3, half), F32)], axis=0)
     for b in range(bits):
         far = lax.ppermute(joined, "vocab", _xor(count, 1 << b))
-        joined = _join_stats(joined, far, [*weights, *es, *stats, picks, ids, lps])
+        joined = _join_stats(joined, far, [*es, *stats, picks, ids, lps])
 
     grads = []
     for group in groups:
@@ -465,15 +517,16 @@
             joined,
             [chunks[q] for q in group],
             terms,
-            weights,
         )
         grads.append((own, lax.ppermute(own, "row", swap)))
 
     order = (jnp.arange(count, dtype=jnp.int32) ^ v) ^ (r * (count // 2))
-    (before,) = _feature_terms(*grads[0], weights[0])
-    keep, send = _feature_terms(*grads[1], weights[1], before, order)
-
-    keep = keep + lax.ppermute(send, "vocab", _xor(count, 1)).astype(F32)
+    (before,) = _feature_terms(*grads[0], head_weight, starts[0])
+    keep, send = _feature_terms(*grads[1], head_weight, starts[1], before, order)
+
+    far = lax.ppermute(send, "vocab", _xor(count, 1))
+    weight_grad = _weight_grad(ht, *grads[0], starts[0], width, kept=[keep])
+    keep = keep + far.astype(F32)
     keep = keep.reshape((count // 2,) + hidden.shape)
     total = keep[0]
     for d in range(1, count // 2):
@@ -481,7 +534,6 @@
         total = total + far.astype(F32)
     hidden_grad = total.astype(BF16)
 
-    weight_grad = _weight_grad(ht, *grads[0], starts[0], width)
     weight_grad = _weight_grad(ht, *grads[1], starts[1], width, weight_grad)
     return hidden_grad, weight_grad
 

time: 102 us -> 93.7 us (0.919)
  local copies, waits for them, and re-layouts: 13.9 us -> 2.18 us
  waiting for transfers between devices: 14.5 us -> 17.6 us
    unnamed x28 -> x12, local copies, waits for them, and re-layouts: 12.8 us -> 1.85 us
    ppermute x3, waiting for transfers between devices: 4.81 us -> 8.14 us  [per_device(): far_packed = lax.ppermute(packed, 'vocab', _xor(count, 1 << b))]
    pallas_call x19 -> x18, Pallas kernels: 48.9 us -> 48.8 us  [_call(): pl.pallas_call(body, in_specs=specs, out_specs=out_specs or [LOCAL] * len...]
  transfers between devices with their start and end apart: 19 -> 19, of which waited for: 6 -> 8; matrix products, arithmetic and copies ran while one was open for 3% -> 3% of each run, Pallas kernels for 37% -> 36%
where the time goes in v4:
time: 93.7 us; the launch traced here: 93.3 us
  Pallas kernels  48.8 us (52%)
  starting transfers between devices  18.9 us (20%)
  waiting for transfers between devices  17.6 us (19%)
  other arithmetic  4.94 us (5%)
  local copies, waits for them, and re-layouts  2.18 us (2%)
    pallas_call x18, Pallas kernels, _call(): pl.pallas_call(body, in_specs=specs, out_specs=out_specs or [LOCAL] * len...  48.8 us
    ppermute x3, waiting for transfers between devices, per_device(): far = lax.ppermute(joined, 'vocab', _xor(count, 1 << b))  8.31 us
    ppermute x3, waiting for transfers between devices, per_device(): far_packed = lax.ppermute(packed, 'vocab', _xor(count, 1 << b))  8.14 us
    ppermute x3, starting transfers between devices, per_device(): far = lax.ppermute(h, 'vocab', _xor(count, 1 << b))  7.33 us
    ppermute x3, starting transfers between devices, per_device(): far = lax.ppermute(joined, 'vocab', _xor(count, 1 << b))  3.56 us
    ppermute x3, starting transfers between devices, per_device(): far = lax.ppermute(keep[d].astype(BF16), 'vocab', _xor(count, 2 * d))  3.55 us
  transfers between devices with their start and end apart: 19, of which 8 were waited for; matrix products, arithmetic and copies ran while one was open for 3% of the time, Pallas kernels for 36%

profile of v4, /device:TPU:0, one launch (start us, length us, event | category | flops | bytes accessed | tf_op | source)
XLA Modules:
  0.0 93.3 jit_solution(16146051854150779135)
XLA Ops:
  0.7 4.1 %collective-permute-start = (bf16[1,32,1024]{2,1,0:T(8,128)(2,1)}, bf16[1,32,1024]{2,1,0:T(8,128)(2,1)S(1)}, u32[]{:S(2)}, u32[]{:S(2)}) collective-permute-start(bf16[1,32,1024]{2,1,0:T(8,128)(2,1)} %bitcast.45), channel_id=1, source_target_pairs={{0,8},{2,10},{4,12},{6,14},{8,0},{10,2},{12,4},{14,6},{1,9},{3,11}... | collective-permute-start | bytes 196616 | tf_op jit(solution)/shard_map/ppermute | solution.py:464
  6.1 4.5 %collective-permute-done.1 = f32[2,4,128]{2,1,0:T(4,128)S(1)} collective-permute-done((f32[2,4,128]{2,1,0:T(4,128)S(1)}, f32[2,4,128]{2,1,0:T(4,128)S(1)}, u32[]{:S(2)}, u32[]{:S(2)}) %collective-permute-start.1) | collective-permute-done | bytes 4128 | tf_op jit(solution)/shard_map/ppermute | solution.py:465
  11.5 1.6 %collective-permute-start.2 = (bf16[2,32,1024]{2,1,0:T(8,128)(2,1)S(1)}, bf16[2,32,1024]{2,1,0:T(8,128)(2,1)S(1)}, u32[]{:S(2)}, u32[]{:S(2)}) collective-permute-start(bf16[2,32,1024]{2,1,0:T(8,128)(2,1)S(1)} %maximum_bitcast_fusion), channel_id=1, source_target_pairs={{0,4},{2,6},{4,0},{6,2},{8,12},{10,14},{12,8},{14,10},{1,5},{3,7},... | collective-permute-start | bytes 393224 | tf_op jit(solution)/shard_map/ppermute | solution.py:464
  14.3 3.2 %collective-permute-done.3 = f32[2,8,128]{2,1,0:T(8,128)S(1)} collective-permute-done((f32[2,8,128]{2,1,0:T(8,128)S(1)}, f32[2,8,128]{2,1,0:T(8,128)S(1)}, u32[]{:S(2)}, u32[]{:S(2)}) %collective-permute-start.3) | collective-permute-done | bytes 8224 | tf_op jit(solution)/shard_map/ppermute | solution.py:465
  17.6 1.6 %collective-permute-start.4 = (bf16[4,32,1024]{2,1,0:T(8,128)(2,1)S(1)}, bf16[4,32,1024]{2,1,0:T(8,128)(2,1)S(1)}, u32[]{:S(2)}, u32[]{:S(2)}) collective-permute-start(bf16[4,32,1024]{2,1,0:T(8,128)(2,1)S(1)} %bitcast.44), channel_id=1, source_target_pairs={{0,2},{2,0},{4,6},{6,4},{8,10},{10,8},{12,14},{14,12},{1,3},{3,1},... | collective-permute-start | bytes 786440 | tf_op jit(solution)/shard_map/ppermute | solution.py:464
  19.7 3.9 %fetch_weight.1.w_ref = bf16[1024,4864]{1,0:T(8,128)(2,1)S(1)} custom-call(bf16[1024,9728]{1,0:T(8,128)(2,1)} %refs_2_.3), custom_call_target="tpu_custom_call" | custom-call | bytes 9961472 | tf_op jit(solution)/shard_map/fetch_weight/pallas_call | solution.py:35
  24.4 2.8 %partial_logits.6 = (f32[128,2560]{1,0:T(8,128)S(1)}, f32[128,2560]{1,0:T(8,128)S(1)}, bf16[1024,2560]{1,0:T(8,128)(2,1)S(1)}) custom-call(bf16[256,1024]{1,0:T(8,128)(2,1)S(1)} %bitcast.37, bf16[1024,4864]{1,0:T(8,128)(2,1)S(1)} %fetch_weight.1.w_ref, bf16[1024,9728]{1,0:T(8,128)(2,1)} %refs_2_.3), custom_call_target="tpu_custom_call" | custom-call | flops 1342177280 | bytes 7864320 | tf_op jit(solution)/shard_map/partial_logits/pallas_call | solution.py:35
  27.2 1.5 %partial_logits.7 = (f32[128,2560]{1,0:T(8,128)S(1)}, f32[128,2560]{1,0:T(8,128)S(1)}) custom-call(bf16[256,1024]{1,0:T(8,128)(2,1)S(1)} %bitcast.38, bf16[1024,2560]{1,0:T(8,128)(2,1)S(1)} %get-tuple-element.63.w_ref), custom_call_target="tpu_custom_call" | custom-call | flops 1342177280 | bytes 7864320 | tf_op jit(solution)/shard_map/partial_logits/pallas_call | solution.py:35
  29.3 3.1 %partial_logits.4 = (f32[128,2304]{1,0:T(8,128)S(1)}, f32[128,2304]{1,0:T(8,128)S(1)}, bf16[1024,2304]{1,0:T(8,128)(2,1)S(1)}) custom-call(bf16[256,1024]{1,0:T(8,128)(2,1)S(1)} %bitcast.39, bf16[1024,4864]{1,0:T(8,128)(2,1)S(1)} %fetch_weight.1.w_ref, bf16[1024,9728]{1,0:T(8,128)(2,1)} %refs_2_.3), custom_call_target="tpu_custom_call" | custom-call | flops 1207959552 | bytes 7077888 | tf_op jit(solution)/shard_map/partial_logits/pallas_call | solution.py:35
  35.4 1.6 %exponentials.4 = (f32[128,2304]{1,0:T(8,128)S(1)}, f32[128,128]{1,0:T(8,128)S(1)}, f32[128,128]{1,0:T(8,128)S(1)}, s32[128,128]{1,0:T(8,128)S(1)}, f32[128,128]{1,0:T(8,128)S(1)}) custom-call(f32[128,2304]{1,0:T(8,128)S(1)} %get-tuple-element.51.refs_0_, f32[128,2304]{1,0:T(8,128)S(1)} %collective-permute-done.7.refs_1_, ...), custom_call_target="tpu_custom_call" | custom-call | flops 2359296 | bytes 3538944 | tf_op jit(solution)/shard_map/exponentials/pallas_call | solution.py:35
  37.0 1.5 %exponentials.5 = (f32[128,2560]{1,0:T(8,128)S(1)}, f32[128,128]{1,0:T(8,128)S(1)}, f32[128,128]{1,0:T(8,128)S(1)}) custom-call(f32[128,2560]{1,0:T(8,128)S(1)} %get-tuple-element.56.refs_0_, f32[128,2560]{1,0:T(8,128)S(1)} %collective-permute-done.8.refs_1_, s32[128,128]{1,0:T(8,128)S(1)} %get-tuple-element.54.refs_2_.refs_9_.refs_5_, ...), custom_call_target="tpu_custom_call" | custom-call | flops 2621440 | bytes 3932160 | tf_op jit(solution)/shard_map/exponentials/pallas_call | solution.py:35
  40.0 1.9 %exponentials.7 = (f32[128,2560]{1,0:T(8,128)S(1)}, f32[128,128]{1,0:T(8,128)S(1)}, f32[128,128]{1,0:T(8,128)S(1)}, f32[8,128]{1,0:T(8,128)S(1)}) custom-call(f32[128,2560]{1,0:T(8,128)S(1)} %get-tuple-element.64.refs_0_, f32[128,2560]{1,0:T(8,128)S(1)} %collective-permute-done.9.refs_1_, s32[128,128]{1,0:T(8,128)S(1)} %get-tuple-element.54.refs_2_.refs_9_.refs_5_, ...), custom_call_target="tpu_custom_call" | custom-call | flops 2621440 | bytes 3932160 | tf_op jit(solution)/shard_map/exponentials/pallas_call | solution.py:35
  41.9 1.5 %collective-permute-start.10 = (f32[8,128]{1,0:T(8,128)S(1)}, f32[8,128]{1,0:T(8,128)S(1)}, u32[]{:S(2)}, u32[]{:S(2)}) collective-permute-start(f32[8,128]{1,0:T(8,128)S(1)} %maximum_maximum_fusion.a_ref), channel_id=1, source_target_pairs={{0,2},{2,0},{4,6},{6,4},{8,10},{10,8},{12,14},{14,12},{1,3},{3,1},... | collective-permute-start | bytes 12296 | tf_op jit(solution)/shard_map/ppermute | solution.py:506
  43.5 2.1 %collective-permute-done.10.b_ref = f32[8,128]{1,0:T(8,128)S(1)} collective-permute-done((f32[8,128]{1,0:T(8,128)S(1)}, f32[8,128]{1,0:T(8,128)S(1)}, u32[]{:S(2)}, u32[]{:S(2)}) %collective-permute-start.10) | collective-permute-done | bytes 4128 | tf_op jit(solution)/shard_map/ppermute | solution.py:506
  46.3 2.9 %collective-permute-done.11.b_ref = f32[8,128]{1,0:T(8,128)S(1)} collective-permute-done((f32[8,128]{1,0:T(8,128)S(1)}, f32[8,128]{1,0:T(8,128)S(1)}, u32[]{:S(2)}, u32[]{:S(2)}) %collective-permute-start.11) | collective-permute-done | bytes 4128 | tf_op jit(solution)/shard_map/ppermute | solution.py:506
  50.5 3.3 %collective-permute-done.12.b_ref = f32[8,128]{1,0:T(8,128)S(1)} collective-permute-done((f32[8,128]{1,0:T(8,128)S(1)}, f32[8,128]{1,0:T(8,128)S(1)}, u32[]{:S(2)}, u32[]{:S(2)}) %collective-permute-start.12) | collective-permute-done | bytes 4128 | tf_op jit(solution)/shard_map/ppermute | solution.py:506
  53.8 2.8 %logit_grad.3.refs_0_.own_ref = bf16[128,4864]{1,0:T(8,128)(2,1)S(1)} custom-call(f32[128,2304]{1,0:T(8,128)S(1)} %get-tuple-element.59.refs_5_.refs_8_.refs_0_, f32[128,2560]{1,0:T(8,128)S(1)} %get-tuple-element.61.refs_6_.refs_9_.refs_1_, f32[128,128]{1,0:T(8,128)S(1)} %get-tuple-element.67.refs_5_.refs_4_.refs_2_, ...), custom_call_target="tpu_custom_call" | custom-call | flops 4980736 | bytes 3735552 | tf_op jit(solution)/shard_map/logit_grad/pallas_call | solution.py:35
  56.7 3.0 %logit_grad.2.refs_0_.own_ref = bf16[128,4864]{1,0:T(8,128)(2,1)S(1)} custom-call(f32[128,2304]{1,0:T(8,128)S(1)} %get-tuple-element.62.refs_10_.refs_2_.refs_0_, f32[128,2560]{1,0:T(8,128)S(1)} %get-tuple-element.70.refs_3_.refs_1_, f32[128,128]{1,0:T(8,128)S(1)} %get-tuple-element.69.refs_7_.refs_6_.refs_2_, ...), custom_call_target="tpu_custom_call" | custom-call | flops 4980736 | bytes 3735552 | tf_op jit(solution)/shard_map/logit_grad/pallas_call | solution.py:35
  60.3 5.2 %feature_terms.2.refs_3_ = f32[256,1024]{1,0:T(8,128)S(1)} custom-call(bf16[128,4864]{1,0:T(8,128)(2,1)S(1)} %logit_grad.3.refs_0_.own_ref, bf16[128,4864]{1,0:T(8,128)(2,1)} %collective-permute-done.14.refs_1_.far_ref, bf16[1024,9728]{1,0:T(8,128)(2,1)} %refs_2_.3), custom_call_target="tpu_custom_call" | custom-call | flops 2550136832 | bytes 12451840 | tf_op jit(solution)/shard_map/feature_terms/pallas_call | solution.py:35
  65.6 6.6 %feature_terms.3 = (f32[128,1024]{1,0:T(8,128)S(1)}, bf16[128,1024]{1,0:T(8,128)(2,1)}) custom-call(bf16[128,4864]{1,0:T(8,128)(2,1)S(1)} %logit_grad.2.refs_0_.own_ref, bf16[128,4864]{1,0:T(8,128)(2,1)} %collective-permute-done.13.refs_1_.far_ref, bf16[1024,9728]{1,0:T(8,128)(2,1)} %refs_2_.3, f32[256,1024]{1,0:T(8,128)S(1)} %feature_terms.2.refs_3_, ...), custom_call_target="tpu_custom_call" | custom-call | flops 2550136832 | bytes 12451840 | tf_op jit(solution)/shard_map/feature_terms/pallas_call | solution.py:35
  73.0 1.5 %collective-permute-start.15 = (bf16[128,1024]{1,0:T(8,128)(2,1)}, bf16[128,1024]{1,0:T(8,128)(2,1)}, u32[]{:S(2)}, u32[]{:S(2)}) collective-permute-start(bf16[128,1024]{1,0:T(8,128)(2,1)} %get-tuple-element.75), channel_id=1, source_target_pairs={{0,2},{2,0},{4,6},{6,4},{8,10},{10,8},{12,14},{14,12},{1,3},{3,1},... | collective-permute-start | bytes 786440 | tf_op jit(solution)/shard_map/ppermute | solution.py:527
  75.8 6.0 %weight_grad.2.refs_0_ = bf16[1024,9728]{1,0:T(8,128)(2,1)} custom-call(bf16[1024,256]{1,0:T(8,128)(2,1)S(1)} %bitcast.42, bf16[128,4864]{1,0:T(8,128)(2,1)S(1)} %logit_grad.3.refs_0_.own_ref, bf16[128,4864]{1,0:T(8,128)(2,1)} %collective-permute-done.14.refs_1_.far_ref, f32[128,1024]{1,0:T(8,128)S(1)} %copy-done.1), custom_call_target="tpu_custom_call" | custom-call | flops 2550136832 | bytes 12451840 | tf_op jit(solution)/shard_map/weight_grad/pallas_call | solution.py:35
  83.6 1.8 %collective-permute-start.18 = (bf16[32,1024]{1,0:T(8,128)(2,1)S(1)}, bf16[32,1024]{1,0:T(8,128)(2,1)S(1)}, u32[]{:S(2)}, u32[]{:S(2)}) collective-permute-start(bf16[32,1024]{1,0:T(8,128)(2,1)S(1)} %get-tuple-element.81), channel_id=1, source_target_pairs={{0,12},{2,14},{4,8},{6,10},{8,4},{10,6},{12,0},{14,2},{1,13},{3,15... | collective-permute-start | bytes 196616 | tf_op jit(solution)/shard_map/ppermute | solution.py:533
  86.4 6.0 %weight_grad.3 = bf16[1024,9728]{1,0:T(8,128)(2,1)} custom-call(bf16[1024,256]{1,0:T(8,128)(2,1)S(1)} %bitcast.43, bf16[128,4864]{1,0:T(8,128)(2,1)S(1)} %logit_grad.2.refs_0_.own_ref, bf16[128,4864]{1,0:T(8,128)(2,1)} %collective-permute-done.13.refs_1_.far_ref, bf16[1024,9728]{1,0:T(8,128)(2,1)} %weight_grad.2.refs_0_), custom_call_target="tpu_custom_call", output_to_operand_aliasing={{}: (3, {})} | custom-call | flops 2550136832 | bytes 12451840 | tf_op jit(solution)/shard_map/weight_grad/pallas_call | solution.py:35
  (67 shorter events, 18.3 us)
Async XLA Ops:
  0.6 19.1 %copy-start.5 = (f32[2]{0:T(128)S(1)}, f32[2]{0:T(128)}, u32[]{:S(2)}) copy-start(f32[2]{0:T(128)} %constant.22.clone) | copy-start | bytes 28
  0.6 18.5 %copy-start.2 = (f32[128,4]{0,1:T(4,128)S(1)}, f32[128,4]{0,1:T(4,128)}, u32[]{:S(2)}) copy-start(f32[128,4]{0,1:T(4,128)} %param.10) | copy-start | bytes 6148
  0.7 10.0 %collective-permute-start = (bf16[1,32,1024]{2,1,0:T(8,128)(2,1)}, bf16[1,32,1024]{2,1,0:T(8,128)(2,1)S(1)}, u32[]{:S(2)}, u32[]{:S(2)}) collective-permute-start(bf16[1,32,1024]{2,1,0:T(8,128)(2,1)} %bitcast.45), channel_id=1, source_target_pairs={{0,8},{2,10},{4,12},{6,14},{8,0},{10,2},{12,4},{14,6},{1,9},{3,11}... | collective-permute-start | bytes 196616 | tf_op jit(solution)/shard_map/ppermute | solution.py:464
  6.1 4.5 %collective-permute-start.1 = (f32[2,4,128]{2,1,0:T(4,128)S(1)}, f32[2,4,128]{2,1,0:T(4,128)S(1)}, u32[]{:S(2)}, u32[]{:S(2)}) collective-permute-start(f32[2,4,128]{2,1,0:T(4,128)S(1)} %pad_maximum_fusion.4), channel_id=1, source_target_pairs={{0,8},{2,10},{4,12},{6,14},{8,0},{10,2},{12,4},{14,6},{1,9},{3,11}... | collective-permute-start | bytes 12296 | tf_op jit(solution)/shard_map/ppermute | solution.py:465
  11.5 6.0 %collective-permute-start.2 = (bf16[2,32,1024]{2,1,0:T(8,128)(2,1)S(1)}, bf16[2,32,1024]{2,1,0:T(8,128)(2,1)S(1)}, u32[]{:S(2)}, u32[]{:S(2)}) collective-permute-start(bf16[2,32,1024]{2,1,0:T(8,128)(2,1)S(1)} %maximum_bitcast_fusion), channel_id=1, source_target_pairs={{0,4},{2,6},{4,0},{6,2},{8,12},{10,14},{12,8},{14,10},{1,5},{3,7},... | collective-permute-start | bytes 393224 | tf_op jit(solution)/shard_map/ppermute | solution.py:464
  13.8 3.7 %collective-permute-start.3 = (f32[2,8,128]{2,1,0:T(8,128)S(1)}, f32[2,8,128]{2,1,0:T(8,128)S(1)}, u32[]{:S(2)}, u32[]{:S(2)}) collective-permute-start(f32[2,8,128]{2,1,0:T(8,128)S(1)} %pad_maximum_fusion.3), channel_id=1, source_target_pairs={{0,4},{2,6},{4,0},{6,2},{8,12},{10,14},{12,8},{14,10},{1,5},{3,7},... | collective-permute-start | bytes 24584 | tf_op jit(solution)/shard_map/ppermute | solution.py:465
  17.6 6.6 %collective-permute-start.4 = (bf16[4,32,1024]{2,1,0:T(8,128)(2,1)S(1)}, bf16[4,32,1024]{2,1,0:T(8,128)(2,1)S(1)}, u32[]{:S(2)}, u32[]{:S(2)}) collective-permute-start(bf16[4,32,1024]{2,1,0:T(8,128)(2,1)S(1)} %bitcast.44), channel_id=1, source_target_pairs={{0,2},{2,0},{4,6},{6,4},{8,10},{10,8},{12,14},{14,12},{1,3},{3,1},... | collective-permute-start | bytes 786440 | tf_op jit(solution)/shard_map/ppermute | solution.py:464
  19.2 5.0 %collective-permute-start.5 = (f32[2,16,128]{2,1,0:T(8,128)S(1)}, f32[2,16,128]{2,1,0:T(8,128)S(1)}, u32[]{:S(2)}, u32[]{:S(2)}) collective-permute-start(f32[2,16,128]{2,1,0:T(8,128)S(1)} %pad_maximum_fusion.2), channel_id=1, source_target_pairs={{0,2},{2,0},{4,6},{6,4},{8,10},{10,8},{12,14},{14,12},{1,3},{3,1},... | collective-permute-start | bytes 49160 | tf_op jit(solution)/shard_map/ppermute | solution.py:465
  28.7 11.3 %collective-permute-start.9 = (f32[128,2560]{1,0:T(8,128)S(1)}, f32[128,2560]{1,0:T(8,128)S(1)}, u32[]{:S(2)}, u32[]{:S(2)}) collective-permute-start(f32[128,2560]{1,0:T(8,128)S(1)} %get-tuple-element.65), channel_id=1, source_target_pairs={{0,1},{1,0},{2,3},{3,2},{4,5},{5,4},{6,7},{7,6},{8,9},{9,8},{10,11... | collective-permute-start | bytes 3932168 | tf_op jit(solution)/shard_map/ppermute | solution.py:490
  28.8 8.2 %collective-permute-start.8 = (f32[128,2560]{1,0:T(8,128)S(1)}, f32[128,2560]{1,0:T(8,128)S(1)}, u32[]{:S(2)}, u32[]{:S(2)}) collective-permute-start(f32[128,2560]{1,0:T(8,128)S(1)} %get-tuple-element.57), channel_id=1, source_target_pairs={{0,1},{1,0},{2,3},{3,2},{4,5},{5,4},{6,7},{7,6},{8,9},{9,8},{10,11... | collective-permute-start | bytes 3932168 | tf_op jit(solution)/shard_map/ppermute | solution.py:490
  32.4 3.0 %collective-permute-start.7 = (f32[128,2304]{1,0:T(8,128)S(1)}, f32[128,2304]{1,0:T(8,128)S(1)}, u32[]{:S(2)}, u32[]{:S(2)}) collective-permute-start(f32[128,2304]{1,0:T(8,128)S(1)} %get-tuple-element.52), channel_id=1, source_target_pairs={{0,1},{1,0},{2,3},{3,2},{4,5},{5,4},{6,7},{7,6},{8,9},{9,8},{10,11... | collective-permute-start | bytes 3538952 | tf_op jit(solution)/shard_map/ppermute | solution.py:490
  32.5 2.0 %copy-start.3 = (f32[128]{0:T(128)S(1)}, f32[128]{0:T(128)}, u32[]{:S(2)}) copy-start(f32[128]{0:T(128)} %param.12) | copy-start | bytes 1540
  32.5 2.0 %copy-start.4 = (s32[128]{0:T(128)S(1)}, s32[128]{0:T(128)}, u32[]{:S(2)}) copy-start(s32[128]{0:T(128)} %param.11) | copy-start | bytes 1540
  33.9 4.6 %collective-permute-start.6 = (f32[128,2304]{1,0:T(8,128)S(1)}, f32[128,2304]{1,0:T(8,128)S(1)}, u32[]{:S(2)}, u32[]{:S(2)}) collective-permute-start(f32[128,2304]{1,0:T(8,128)S(1)} %get-tuple-element.50), channel_id=1, source_target_pairs={{0,1},{1,0},{2,3},{3,2},{4,5},{5,4},{6,7},{7,6},{8,9},{9,8},{10,11... | collective-permute-start | bytes 3538952 | tf_op jit(solution)/shard_map/ppermute | solution.py:490
  41.9 3.6 %collective-permute-start.10 = (f32[8,128]{1,0:T(8,128)S(1)}, f32[8,128]{1,0:T(8,128)S(1)}, u32[]{:S(2)}, u32[]{:S(2)}) collective-permute-start(f32[8,128]{1,0:T(8,128)S(1)} %maximum_maximum_fusion.a_ref), channel_id=1, source_target_pairs={{0,2},{2,0},{4,6},{6,4},{8,10},{10,8},{12,14},{14,12},{1,3},{3,1},... | collective-permute-start | bytes 12296 | tf_op jit(solution)/shard_map/ppermute | solution.py:506
  45.6 3.7 %collective-permute-start.11 = (f32[8,128]{1,0:T(8,128)S(1)}, f32[8,128]{1,0:T(8,128)S(1)}, u32[]{:S(2)}, u32[]{:S(2)}) collective-permute-start(f32[8,128]{1,0:T(8,128)S(1)} %join_stats.3.a_ref), channel_id=1, source_target_pairs={{0,4},{2,6},{4,0},{6,2},{8,12},{10,14},{12,8},{14,10},{1,5},{3,7},... | collective-permute-start | bytes 12296 | tf_op jit(solution)/shard_map/ppermute | solution.py:506
  49.2 4.6 %collective-permute-start.12 = (f32[8,128]{1,0:T(8,128)S(1)}, f32[8,128]{1,0:T(8,128)S(1)}, u32[]{:S(2)}, u32[]{:S(2)}) collective-permute-start(f32[8,128]{1,0:T(8,128)S(1)} %join_stats.4.a_ref), channel_id=1, source_target_pairs={{0,8},{2,10},{4,12},{6,14},{8,0},{10,2},{12,4},{14,6},{1,9},{3,11}... | collective-permute-start | bytes 12296 | tf_op jit(solution)/shard_map/ppermute | solution.py:506
  56.7 3.7 %collective-permute-start.14 = (bf16[128,4864]{1,0:T(8,128)(2,1)S(1)}, bf16[128,4864]{1,0:T(8,128)(2,1)}, u32[]{:S(2)}, u32[]{:S(2)}) collective-permute-start(bf16[128,4864]{1,0:T(8,128)(2,1)S(1)} %logit_grad.3.refs_0_.own_ref), channel_id=1, source_target_pairs={{0,1},{1,0},{2,3},{3,2},{4,5},{5,4},{6,7},{7,6},{8,9},{9,8},{10,11... | collective-permute-start | bytes 3735560 | tf_op jit(solution)/shard_map/ppermute | solution.py:521
  59.8 5.8 %collective-permute-start.13 = (bf16[128,4864]{1,0:T(8,128)(2,1)S(1)}, bf16[128,4864]{1,0:T(8,128)(2,1)}, u32[]{:S(2)}, u32[]{:S(2)}) collective-permute-start(bf16[128,4864]{1,0:T(8,128)(2,1)S(1)} %logit_grad.2.refs_0_.own_ref), channel_id=1, source_target_pairs={{0,1},{1,0},{2,3},{3,2},{4,5},{5,4},{6,7},{7,6},{8,9},{9,8},{10,11... | collective-permute-start | bytes 3735560 | tf_op jit(solution)/shard_map/ppermute | solution.py:521
  73.0 8.8 %collective-permute-start.15 = (bf16[128,1024]{1,0:T(8,128)(2,1)}, bf16[128,1024]{1,0:T(8,128)(2,1)}, u32[]{:S(2)}, u32[]{:S(2)}) collective-permute-start(bf16[128,1024]{1,0:T(8,128)(2,1)} %get-tuple-element.75), channel_id=1, source_target_pairs={{0,2},{2,0},{4,6},{6,4},{8,10},{10,8},{12,14},{14,12},{1,3},{3,1},... | collective-permute-start | bytes 786440 | tf_op jit(solution)/shard_map/ppermute | solution.py:527
  74.8 1.0 %copy-start.1 = (f32[128,1024]{1,0:T(8,128)S(1)}, f32[128,1024]{1,0:T(8,128)}, u32[]{:S(2)}) copy-start(f32[128,1024]{1,0:T(8,128)} %copy-done) | copy-start | bytes 1572868
  82.8 9.5 %collective-permute-start.16 = (bf16[32,1024]{1,0:T(8,128)(2,1)S(1)}, bf16[32,1024]{1,0:T(8,128)(2,1)S(1)}, u32[]{:S(2)}, u32[]{:S(2)}) collective-permute-start(bf16[32,1024]{1,0:T(8,128)(2,1)S(1)} %get-tuple-element.80), channel_id=1, source_target_pairs={{0,4},{2,6},{4,0},{6,2},{8,12},{10,14},{12,8},{14,10},{1,5},{3,7},... | collective-permute-start | bytes 196616 | tf_op jit(solution)/shard_map/ppermute | solution.py:533
  83.6 8.8 %collective-permute-start.18 = (bf16[32,1024]{1,0:T(8,128)(2,1)S(1)}, bf16[32,1024]{1,0:T(8,128)(2,1)S(1)}, u32[]{:S(2)}, u32[]{:S(2)}) collective-permute-start(bf16[32,1024]{1,0:T(8,128)(2,1)S(1)} %get-tuple-element.81), channel_id=1, source_target_pairs={{0,12},{2,14},{4,8},{6,10},{8,4},{10,6},{12,0},{14,2},{1,13},{3,15... | collective-permute-start | bytes 196616 | tf_op jit(solution)/shard_map/ppermute | solution.py:533
  85.4 7.1 %collective-permute-start.17 = (bf16[32,1024]{1,0:T(8,128)(2,1)S(1)}, bf16[32,1024]{1,0:T(8,128)(2,1)S(1)}, u32[]{:S(2)}, u32[]{:S(2)}) collective-permute-start(bf16[32,1024]{1,0:T(8,128)(2,1)S(1)} %get-tuple-element.82), channel_id=1, source_target_pairs={{0,8},{2,10},{4,12},{6,14},{8,0},{10,2},{12,4},{14,6},{1,9},{3,11}... | collective-permute-start | bytes 196616 | tf_op jit(solution)/shard_map/ppermute | solution.py:533
  (1 other events, 0.8 us)

commit v5 on v4

--- a/solution.py
+++ b/solution.py
@@ -16,6 +16,9 @@
 LOCAL = pl.BlockSpec(memory_space=pltpu.VMEM)
 REMOTE = pl.BlockSpec(memory_space=pltpu.HBM)
 WRITES = 4
+GROUPS = 4
+BLOCK = 1024
+WIDE = 1280
 
 
 def _local(x):
@@ -26,8 +29,46 @@
     return pl.CostEstimate(flops=int(flops), bytes_accessed=int(nbytes), transcendentals=0)
 
 
-def _call(body, name, args, out_shape, cost, specs=None, out_specs=None, scratch=(), aliases=None, limit=8):
-    specs = specs or [LOCAL] * len(args)
+def _copies(w_ref, start, out_ref, sems):
+    depth, width = out_ref.shape
+    step = depth // GROUPS
+    return [
+        pltpu.make_async_copy(
+            w_ref.at[pl.ds(i * step, step), pl.ds(start, width)], out_ref.at[pl.ds(i * step, step), :], sems.at[i]
+        )
+        for i in range(GROUPS)
+    ]
+
+
+def _bringing(body, inputs, outputs, pieces):
+    def wrapped(*refs):
+        first = inputs + 1 + outputs
+        news = refs[first : first + len(pieces)]
+        sems = refs[-1]
+        copies = []
+        for i, ((start, _), ref) in enumerate(zip(pieces, news)):
+            copies += _copies(refs[inputs], start, ref, sems.at[i])
+        for copy in copies:
+            copy.start()
+        body(*refs[:inputs], *refs[inputs + 1 : first], *refs[first + len(pieces) : -1])
+        for copy in copies:
+            copy.wait()
+
+    return wrapped
+
+
+def _call(body, name, args, out_shape, cost, specs=None, out_specs=None, scratch=(), aliases=None, limit=8, bring=None):
+    args, out_shape, scratch = list(args), list(out_shape), list(scratch)
+    specs = list(specs or [LOCAL] * len(args))
+    out_specs = list(out_specs or [LOCAL] * len(out_shape))
+    if bring:
+        source, pieces = bring
+        body = _bringing(body, len(args), len(out_shape), pieces)
+        args.append(source)
+        specs.append(REMOTE)
+        out_shape += [pltpu.VMEM((source.shape[0], width), source.dtype) for _, width in pieces]
+        out_specs += [LOCAL] * len(pieces)
+        scratch.append(pltpu.SemaphoreType.DMA((len(pieces), GROUPS)))
     args = [
         _local(x) if s is LOCAL else pltpu.with_memory_space_constraint(x, pltpu.HBM) if s is REMOTE else x
         for x, s in zip(args, specs)
@@ -35,9 +76,9 @@
     return pl.pallas_call(
         body,
         in_specs=specs,
-        out_specs=out_specs or [LOCAL] * len(out_shape),
+        out_specs=out_specs,
         out_shape=out_shape,
-        scratch_shapes=list(scratch),
+        scratch_shapes=scratch,
         input_output_aliases=aliases or {},
         compiler_params=pltpu.CompilerParams(vmem_limit_bytes=limit * MIB),
         cost_estimate=cost,
@@ -61,74 +102,49 @@
     return [(i, i ^ s) for i in range(n)]
 
 
-def _copies(w_ref, start, out_ref, sems):
-    depth, width = out_ref.shape
-    step = depth // sems.shape[0]
-    return [
-        pltpu.make_async_copy(
-            w_ref.at[pl.ds(i * step, step), pl.ds(start, width)], out_ref.at[pl.ds(i * step, step), :], sems.at[i]
-        )
-        for i in range(sems.shape[0])
-    ]
-
-
-def _fetch_body(start, w_ref, out_ref, sems):
-    copies = _copies(w_ref, start, out_ref, sems)
-    for copy in copies:
+def _fetch(source, pieces):
+    size = sum(width for _, width in pieces)
+    return _call(lambda: None, "fetch_weight", [], [], _cost(0, 2 * source.shape[0] * size), bring=(source, pieces))
+
+
+def _logits_body(count, turn, h_ref, *refs):
+    w_refs = refs[:count]
+    own_ref, send_ref = refs[count : count + 2]
+    if turn:
+        out_ref, turned, sem = refs[count + 2 :]
+        turned[...] = h_ref[...].T
+        copy = pltpu.make_async_copy(turned, out_ref, sem.at[0])
         copy.start()
-    for copy in copies:
+    half = own_ref.shape[0]
+    begin = 0
+    for w_ref in w_refs:
+        for at, size in _blocks(w_ref.shape[1], 1280):
+            part = jnp.dot(h_ref[...], w_ref[:, at : at + size], preferred_element_type=F32)
+            own_ref[:, begin + at : begin + at + size] = part[:half]
+            send_ref[:, begin + at : begin + at + size] = part[half:]
+        begin += w_ref.shape[1]
+    if turn:
         copy.wait()
 
 
-def _fetch(w, start, width):
-    depth = w.shape[0]
+def _partial_logits(h, weights, turn=False, bring=None):
+    rows, depth = h.shape
+    width = sum(w.shape[1] for w in weights)
+    out = [pltpu.VMEM((rows // 2, width), F32)] * 2
+    out_specs, scratch = [LOCAL] * 2, []
+    if turn:
+        out.append(pltpu.HBM((depth, rows), BF16))
+        out_specs.append(REMOTE)
+        scratch = [pltpu.VMEM((depth, rows), BF16), pltpu.SemaphoreType.DMA((1,))]
     return _call(
-        functools.partial(_fetch_body, start),
-        "fetch_weight",
-        [w],
-        [pltpu.VMEM((depth, width), BF16)],
-        _cost(0, 2 * depth * width),
-        specs=[REMOTE],
-        scratch=[pltpu.SemaphoreType.DMA((4,))],
-    )[0]
-
-
-def _logits_body(start, after, h_ref, w_ref, *refs):
-    if after is not None:
-        source_ref, own_ref, send_ref, next_ref, sems = refs
-        copies = _copies(source_ref, after, next_ref, sems)
-        for copy in copies:
-            copy.start()
-    else:
-        own_ref, send_ref = refs
-    half = own_ref.shape[0]
-    for at, size in _blocks(own_ref.shape[1], 1280):
-        part = jnp.dot(h_ref[...], w_ref[:, start + at : start + at + size], preferred_element_type=F32)
-        own_ref[:, at : at + size] = part[:half]
-        send_ref[:, at : at + size] = part[half:]
-    if after is not None:
-        for copy in copies:
-            copy.wait()
-
-
-def _partial_logits(h, w, chunk, source=None, after=None):
-    start, width = chunk
-    rows, depth = h.shape
-    out = pltpu.VMEM((rows // 2, width), F32)
-    args, specs, outs, scratch = [h, w], [LOCAL, LOCAL], [out, out], []
-    if after is not None:
-        args.append(source)
-        specs.append(REMOTE)
-        outs.append(pltpu.VMEM((depth, after[1]), BF16))
-        scratch = [pltpu.SemaphoreType.DMA((4,))]
-    return _call(
-        functools.partial(_logits_body, start, after and after[0]),
+        functools.partial(_logits_body, len(weights), turn),
         "partial_logits",
-        args,
-        outs,
+        [h, *weights],
+        out,
         _cost(2 * rows * depth * width, 2 * depth * width + 4 * rows * width),
-        specs=specs,
+        out_specs=out_specs,
         scratch=scratch,
+        bring=bring,
     )
 
 
@@ -187,9 +203,9 @@
         hold[rows, :] = sum(total)
         return carry
 
-    lax.fori_loop(0, half // TILE, pick, 0, unroll=2)
+    lax.fori_loop(0, half // TILE, pick, 0, unroll=8)
     stat_ref[...] = jnp.broadcast_to(jnp.max(hold[...], axis=1, keepdims=True), (half, 128))
-    lax.fori_loop(0, half // TILE, power, 0, unroll=2)
+    lax.fori_loop(0, half // TILE, power, 0, unroll=8)
     top = stat_ref[...]
     total = jnp.sum(hold[...], axis=1, keepdims=True)
     stat_ref[...] = jnp.where(lane == 0, top, total)
@@ -314,7 +330,7 @@
                 g_ref[out_rows, col : col + size] = jnp.concatenate(out, axis=0).astype(BF16)
         return carry
 
-    lax.fori_loop(0, half // STEP, step, 0, unroll=2)
+    lax.fori_loop(0, half // STEP, step, 0, unroll=4)
 
 
 def _logit_grad(es, stats, picks, ids, lps, tot, chunks, terms):
@@ -328,26 +344,29 @@
         [pltpu.VMEM((half, width), BF16)],
         _cost(8 * half * width, 6 * half * width),
         scratch=[pltpu.VMEM((len(chunks), half, 128), F32), table, table],
-    )[0]
-
-
-def _feature_body(start, block, count, *refs):
+    )
+
+
+def _feature_body(start, count, own_ref, far_ref, w_ref, *refs):
     if count:
-        own_ref, far_ref, w_ref, before_ref, order_ref, keep_ref, send_ref, acc, other, weights, sems = refs
+        before_ref, order_ref, keep_ref, send_ref, acc, other, weights, keep, send, sems, w_sems = refs
     else:
-        own_ref, far_ref, w_ref, acc, other, weights, sems = refs
-    blocks = _blocks(own_ref.shape[1], block)
-    copies = [pltpu.make_async_copy(far_ref, other, sems.at[len(blocks)])] + [
-        pltpu.make_async_copy(w_ref.at[:, pl.ds(start + at, size)], weights.at[:, pl.ds(at, size)], sems.at[i])
-        for i, (at, size) in enumerate(blocks)
-    ]
-    for copy in copies:
-        copy.start()
-    copies[0].wait()
+        acc, other, weights, sems, w_sems = refs
+    blocks = _blocks(own_ref.shape[1], WIDE)
+    fetches, copies = [], []
+    for i, (at, size) in enumerate(blocks):
+        cols = pl.ds(at, size)
+        copies.append(pltpu.make_async_copy(far_ref.at[:, cols], other.at[:, cols], sems.at[i]))
+        fetches.append(
+            pltpu.make_async_copy(w_ref.at[:, pl.ds(start + at, size)], weights.at[:, cols], w_sems.at[i])
+        )
+        copies[i].start()
+        fetches[i].start()
     for i, (at, size) in enumerate(blocks):
         cols = slice(at, at + size)
+        copies[i].wait()
         grads = jnp.concatenate([own_ref[:, cols], other[:, cols]], axis=0)
-        copies[i + 1].wait()
+        fetches[i].wait()
         part = lax.dot_general(grads, weights[:, cols], NT, preferred_element_type=F32)
         if i:
             acc[...] += part
@@ -356,56 +375,61 @@
     if not count:
         return
     rows = acc.shape[0] // count
-    near, far = [], []
-    for d in range(count):
-        at = pl.multiple_of(order_ref[d] * rows, rows)
-        (far if d % 2 else near).append(acc[pl.ds(at, rows), :])
-    keep_ref[...] = jnp.concatenate(near, axis=0)
-    send_ref[...] = jnp.concatenate(far, axis=0).astype(BF16)
-
-
-def _feature_terms(own, other, w, start, before=None, order=None):
+    block = [acc[pl.ds(pl.multiple_of(order_ref[d] * rows, rows), rows), :] for d in range(count)]
+    send[...] = jnp.concatenate(block[1::2], axis=0).astype(BF16)
+    copies = [pltpu.make_async_copy(send, send_ref, sems.at[0]), pltpu.make_async_copy(keep, keep_ref, w_sems.at[0])]
+    copies[0].start()
+    keep[...] = jnp.concatenate(block[::2], axis=0)
+    copies[1].start()
+    for copy in copies:
+        copy.wait()
+
+
+def _feature_terms(own, other, source, start, before=None, order=None):
     half, width = own.shape
-    depth = w.shape[0]
-    block = 1024
-    args = [own, other, w]
+    depth = source.shape[0]
+    args = [own, other, source]
     specs = [LOCAL, REMOTE, REMOTE]
-    scratch = [
-        pltpu.VMEM((half, width), BF16),
-        pltpu.VMEM((depth, width), BF16),
-        pltpu.SemaphoreType.DMA((len(_blocks(width, block)) + 1,)),
-    ]
-    out = [pltpu.VMEM((2 * half, depth), F32)]
+    count = len(_blocks(width, WIDE))
+    scratch = [pltpu.VMEM((half, width), BF16), pltpu.VMEM((depth, width), BF16)]
+    out, out_specs = [pltpu.VMEM((2 * half, depth), F32)], [LOCAL]
     if before is not None:
         args += [before, order]
         specs += [LOCAL, pl.BlockSpec(memory_space=pltpu.SMEM)]
-        scratch = out + scratch
-        out = [pltpu.VMEM((half, depth), F32), pltpu.VMEM((half, depth), BF16)]
+        scratch = out + scratch + [pltpu.VMEM((half, depth), F32), pltpu.VMEM((half, depth), BF16)]
+        out, out_specs = [pltpu.HBM((half, depth), F32), pltpu.HBM((half, depth), BF16)], [REMOTE] * 2
     return _call(
-        functools.partial(_feature_body, start, block, 0 if before is None else order.shape[0]),
+        functools.partial(_feature_body, start, 0 if before is None else order.shape[0]),
         "feature_terms",
         args,
         out,
         _cost(4 * half * depth * width, 2 * depth * width + 4 * half * width),
         specs=specs,
-        scratch=scratch,
+        out_specs=out_specs,
+        scratch=scratch + [pltpu.SemaphoreType.DMA((count,)), pltpu.SemaphoreType.DMA((count,))],
         limit=20,
     )
 
 
-def _weight_body(start, block, ht_ref, own_ref, far_ref, *refs):
-    out_ref, ring, other, sems = refs[-4:]
-    fetch = pltpu.make_async_copy(far_ref, other, sems.at[WRITES])
-    fetch.start()
-    fetch.wait()
+def _weight_body(start, ht_ref, own_ref, far_ref, *refs):
+    out_ref, ring, ht, other, sems, fetched = refs[-6:]
+    blocks = _blocks(own_ref.shape[1], BLOCK)
+    fetches = [pltpu.make_async_copy(ht_ref, ht, fetched.at[0])] + [
+        pltpu.make_async_copy(far_ref.at[:, pl.ds(at, size)], other.at[:, pl.ds(at, size)], fetched.at[i + 1])
+        for i, (at, size) in enumerate(blocks)
+    ]
+    for fetch in fetches:
+        fetch.start()
+    fetches[0].wait()
     copies = []
-    for i, (at, size) in enumerate(_blocks(own_ref.shape[1], block)):
+    for i, (at, size) in enumerate(blocks):
         slot = i % WRITES
         if i >= WRITES:
             copies[i - WRITES].wait()
         cols = slice(at, at + size)
+        fetches[i + 1].wait()
         grads = jnp.concatenate([own_ref[:, cols], other[:, cols]], axis=0)
-        ring[slot, :, :size] = jnp.dot(ht_ref[...], grads, preferred_element_type=F32).astype(BF16)
+        ring[slot, :, :size] = jnp.dot(ht[...], grads, preferred_element_type=F32).astype(BF16)
         copy = pltpu.make_async_copy(
             ring.at[slot, :, pl.ds(0, size)], out_ref.at[:, pl.ds(start + at, size)], sems.at[slot]
         )
@@ -415,29 +439,30 @@
         copy.wait()
 
 
-def _weight_grad(ht, own, other, start, width_all, before=None, kept=()):
+def _weight_grad(ht, own, other, start, width_all, before=None):
     depth, rows = ht.shape
     half, width = own.shape
-    block = 1024
     args = [ht, own, other]
-    specs = [LOCAL, LOCAL, REMOTE]
+    specs = [REMOTE, LOCAL, REMOTE]
     aliases = {}
     if before is not None:
         args.append(before)
         specs.append(pl.BlockSpec(memory_space=pl.ANY))
         aliases = {3: 0}
     return _call(
-        functools.partial(_weight_body, start, block),
+        functools.partial(_weight_body, start),
         "weight_grad",
-        [*args, *kept],
+        args,
         [jax.ShapeDtypeStruct((depth, width_all), BF16)],
         _cost(2 * rows * depth * width, 2 * depth * width + 2 * rows * width),
-        specs=specs + [LOCAL] * len(kept),
+        specs=specs,
         out_specs=[pl.BlockSpec(memory_space=pl.ANY)],
         scratch=[
-            pltpu.VMEM((WRITES, depth, block), BF16),
+            pltpu.VMEM((WRITES, depth, BLOCK), BF16),
+            pltpu.VMEM((depth, rows), BF16),
             pltpu.VMEM((half, width), BF16),
-            pltpu.SemaphoreType.DMA((WRITES + 1,)),
+            pltpu.SemaphoreType.DMA((WRITES,)),
+            pltpu.SemaphoreType.DMA((len(_blocks(width, BLOCK)) + 1,)),
         ],
         aliases=aliases,
         limit=16,
@@ -455,40 +480,52 @@
     swap = [(0, 1), (1, 0)]
     chunks = _split(width, 4)
     groups = [[0, 1], [2, 3]]
-    starts = [chunks[group[0]][0] for group in groups]
-    widths = [sum(chunks[q][1] for q in group) for group in groups]
+    halves = [(sum(chunks[q][0] for q in group[:1]), sum(chunks[q][1] for q in group)) for group in groups]
 
     h = hidden[None]
-    packed = jnp.stack([teacher_ids.T.astype(F32), teacher_logprobs.T])
+    packed = None
     for b in reversed(range(bits)):
-        far = lax.ppermute(h, "vocab", _xor(count, 1 << b))
-        far_packed = lax.ppermute(packed, "vocab", _xor(count, 1 << b))
-        if b == 0:
-            _, source = lax.optimization_barrier((h, head_weight))
-            weights = _fetch(source, starts[0], widths[0])
-            far, far_packed, weights = lax.optimization_barrier((far, far_packed, weights))
+        perm = _xor(count, 1 << b)
+        far = lax.ppermute(h, "vocab", perm)
+        if packed is None:
+            raw = (teacher_ids.T, teacher_logprobs.T)
+            far_raw = tuple(lax.ppermute(x, "vocab", perm) for x in raw)
+            far, far_raw = lax.optimization_barrier((far, far_raw))
+            packed = jnp.stack([jnp.concatenate([x, y], axis=0).astype(F32) for x, y in zip(raw, far_raw)])
         else:
-            far, far_packed = lax.optimization_barrier((far, far_packed))
+            far_packed = lax.ppermute(packed, "vocab", perm)
+            if b == 0:
+                _, source = lax.optimization_barrier((h, head_weight))
+                fetched = _fetch(source, [chunks[q] for q in groups[0]])
+                far, far_packed, fetched = lax.optimization_barrier((far, far_packed, fetched))
+            else:
+                far, far_packed = lax.optimization_barrier((far, far_packed))
+            packed = jnp.concatenate([packed, far_packed], axis=1)
         bit = (v >> b) & 1
         first = bit == r if b == bits - 1 else bit == 0
         h = jnp.stack([jnp.where(first, h, far), jnp.where(first, far, h)], axis=1)
         h = h.reshape((-1,) + hidden.shape)
-        packed = jnp.concatenate([packed, far_packed], axis=1)
     h = h.reshape(-1, hidden.shape[1])
     packed = packed - jnp.array([1.0, 0.0], F32)[:, None, None] * (v * width).astype(F32)
     h, packed = lax.optimization_barrier((h, packed))
-    ht = h.T
-
-    parts, ready = [], {}
-    for i, (start, size) in enumerate(chunks):
+
+    def bring(*pieces):
+        return head_weight, list(pieces)
+
+    def swapped(x):
+        return lax.ppermute(x, "row", swap)
+
+    es, stats, parts, news = [], [], [], []
+    for i in range(len(chunks)):
         if i in groups[0]:
-            own, send, ready[i] = _partial_logits(
-                h, weights, (start, size), head_weight, chunks[i + len(groups[0])]
-            )
+            turn = i == 0
+            own, send, *rest = _partial_logits(h, fetched[i : i + 1], turn, bring(chunks[i + len(groups[0])]))
+            news.append(rest[-1])
+            if turn:
+                ht = rest[0]
         else:
-            own, send = _partial_logits(h, ready[i - len(groups[0])], (0, size))
-        parts.append((own, lax.ppermute(send, "row", swap)))
-    es, stats = [], []
+            own, send = _partial_logits(h, [news[i - len(groups[0])]])
+        parts.append((own, swapped(send)))
     picks = rows = None
     for i, (own, recv) in enumerate(parts):
         e, picks, stat, *rest = _exponentials(
@@ -508,7 +545,7 @@
 
     grads = []
     for group in groups:
-        own = _logit_grad(
+        (own,) = _logit_grad(
             [es[q] for q in group],
             [stats[q] for q in group],
             picks,
@@ -518,14 +555,15 @@
             [chunks[q] for q in group],
             terms,
         )
-        grads.append((own, lax.ppermute(own, "row", swap)))
+        grads.append((own, swapped(own)))
 
     order = (jnp.arange(count, dtype=jnp.int32) ^ v) ^ (r * (count // 2))
+    starts = [start for start, _ in halves]
     (before,) = _feature_terms(*grads[0], head_weight, starts[0])
     keep, send = _feature_terms(*grads[1], head_weight, starts[1], before, order)
 
     far = lax.ppermute(send, "vocab", _xor(count, 1))
-    weight_grad = _weight_grad(ht, *grads[0], starts[0], width, kept=[keep])
+    weight_grad = _weight_grad(ht, *grads[0], starts[0], width)
     keep = keep + far.astype(F32)
     keep = keep.reshape((count // 2,) + hidden.shape)
     total = keep[0]

time: 93.7 us -> 88.8 us (0.948)
  starting transfers between devices: 18.9 us -> 23.7 us
  waiting for transfers between devices: 17.6 us -> 14.5 us
  Pallas kernels: 48.8 us -> 45.9 us
  local copies, waits for them, and re-layouts: 2.18 us -> 0.16 us
  other arithmetic: 4.94 us -> 3.31 us
    pallas_call x18, Pallas kernels: 48.8 us -> 45.9 us  [_call(): pl.pallas_call(body, in_specs=specs, out_specs=out_specs, out_shape=out_s...]
    ppermute x12 -> x13, starting transfers between devices: 10.2 us -> 13.1 us  [the longest x3 7.58 us: per_device(): far = lax.ppermute(h, 'vocab', perm)]
    ppermute x12 -> x13, waiting for transfers between devices: 9.04 us -> 6.68 us  [the longest x2 4.02 us: per_device(): far_packed = lax.ppermute(packed, 'vocab', perm)]
    unnamed x12 -> x8, local copies, waits for them, and re-layouts: 1.85 us -> 0.02 us
    another operation x3, other arithmetic: 2.39 us -> 0.77 us  [the longest x2 0.7 us: per_device(): jnp.stack([jnp.concatenate([x, y], axis=0).astype(F32) for x, y in zip(ra...]
    ppermute x3, starting transfers between devices: 3.56 us -> 4.91 us  [per_device(): far = lax.ppermute(joined, 'vocab', _xor(count, 1 << b))]
    ppermute x3, waiting for transfers between devices: 8.31 us -> 6.96 us  [per_device(): far = lax.ppermute(joined, 'vocab', _xor(count, 1 << b))]
  transfers between devices with their start and end apart: 19 -> 20, of which waited for: 8 -> 9; matrix products, arithmetic and copies ran while one was open for 3% -> 1% of each run, Pallas kernels for 36% -> 37%
where the time goes in v5:
time: 88.8 us; the launch traced here: 88.5 us
  Pallas kernels  45.9 us (52%)
  starting transfers between devices  23.7 us (27%)
  waiting for transfers between devices  14.5 us (16%)
  other arithmetic  3.31 us (4%)
  between operations  0.92 us (1%)
    pallas_call x18, Pallas kernels, _call(): pl.pallas_call(body, in_specs=specs, out_specs=out_specs, out_shape=out_s...  45.9 us
    ppermute x3, starting transfers between devices, per_device(): far = lax.ppermute(h, 'vocab', perm)  7.58 us
    ppermute x3, waiting for transfers between devices, per_device(): far = lax.ppermute(joined, 'vocab', _xor(count, 1 << b))  6.96 us
    ppermute x3, starting transfers between devices, per_device(): far = lax.ppermute(joined, 'vocab', _xor(count, 1 << b))  4.91 us
    ppermute x3, starting transfers between devices, per_device(): far = lax.ppermute(keep[d].astype(BF16), 'vocab', _xor(count, 2 * d))  4.11 us
    ppermute x2, waiting for transfers between devices, per_device(): far_packed = lax.ppermute(packed, 'vocab', perm)  4.02 us
    ppermute x2, starting transfers between devices, per_device(): far_raw = tuple((lax.ppermute(x, 'vocab', perm) for x in raw))  2.92 us
    ppermute x6, starting transfers between devices, swapped(): return lax.ppermute(x, 'row', swap)  1.88 us
  transfers between devices with their start and end apart: 20, of which 9 were waited for; matrix products, arithmetic and copies ran while one was open for 1% of the time, Pallas kernels for 37%

profile of v5, /device:TPU:0, one launch (start us, length us, event | category | flops | bytes accessed | tf_op | source)
XLA Modules:
  0.0 88.5 jit_solution(9208218213898696408)
XLA Ops:
  0.6 4.1 %collective-permute-start = (bf16[1,32,1024]{2,1,0:T(8,128)(2,1)}, bf16[1,32,1024]{2,1,0:T(8,128)(2,1)S(1)}, u32[]{:S(2)}, u32[]{:S(2)}) collective-permute-start(bf16[1,32,1024]{2,1,0:T(8,128)(2,1)} %bitcast.41), channel_id=1, source_target_pairs={{0,8},{2,10},{4,12},{6,14},{8,0},{10,2},{12,4},{14,6},{1,9},{3,11}... | collective-permute-start | bytes 196616 | tf_op jit(solution)/shard_map/ppermute | solution.py:489
  4.8 2.8 %collective-permute-start.1 = (s32[4,128]{1,0:T(4,128)}, s32[4,128]{1,0:T(4,128)S(1)}, u32[]{:S(2)}, u32[]{:S(2)}) collective-permute-start(s32[4,128]{1,0:T(4,128)} %bitcast.44), channel_id=1, source_target_pairs={{0,8},{2,10},{4,12},{6,14},{8,0},{10,2},{12,4},{14,6},{1,9},{3,11}... | collective-permute-start | bytes 6152 | tf_op jit(solution)/shard_map/ppermute | solution.py:492
  7.7 1.8 %collective-permute-done.2 = f32[4,128]{1,0:T(4,128)S(1)} collective-permute-done((f32[4,128]{1,0:T(4,128)}, f32[4,128]{1,0:T(4,128)S(1)}, u32[]{:S(2)}, u32[]{:S(2)}) %collective-permute-start.2) | collective-permute-done | bytes 2080 | tf_op jit(solution)/shard_map/ppermute | solution.py:492
  11.1 1.9 %collective-permute-start.3 = (bf16[2,32,1024]{2,1,0:T(8,128)(2,1)S(1)}, bf16[2,32,1024]{2,1,0:T(8,128)(2,1)S(1)}, u32[]{:S(2)}, u32[]{:S(2)}) collective-permute-start(bf16[2,32,1024]{2,1,0:T(8,128)(2,1)S(1)} %maximum_bitcast_fusion), channel_id=1, source_target_pairs={{0,4},{2,6},{4,0},{6,2},{8,12},{10,14},{12,8},{14,10},{1,5},{3,7},... | collective-permute-start | bytes 393224 | tf_op jit(solution)/shard_map/ppermute | solution.py:489
  13.9 3.5 %collective-permute-done.4 = f32[2,8,128]{2,1,0:T(8,128)S(1)} collective-permute-done((f32[2,8,128]{2,1,0:T(8,128)S(1)}, f32[2,8,128]{2,1,0:T(8,128)S(1)}, u32[]{:S(2)}, u32[]{:S(2)}) %collective-permute-start.4) | collective-permute-done | bytes 8224 | tf_op jit(solution)/shard_map/ppermute | solution.py:496
  17.5 1.6 %collective-permute-start.5 = (bf16[4,32,1024]{2,1,0:T(8,128)(2,1)S(1)}, bf16[4,32,1024]{2,1,0:T(8,128)(2,1)S(1)}, u32[]{:S(2)}, u32[]{:S(2)}) collective-permute-start(bf16[4,32,1024]{2,1,0:T(8,128)(2,1)S(1)} %bitcast.40), channel_id=1, source_target_pairs={{0,2},{2,0},{4,6},{6,4},{8,10},{10,8},{12,14},{14,12},{1,3},{3,1},... | collective-permute-start | bytes 786440 | tf_op jit(solution)/shard_map/ppermute | solution.py:489
  19.6 3.9 %fetch_weight.1 = (bf16[1024,2304]{1,0:T(8,128)(2,1)S(1)}, bf16[1024,2560]{1,0:T(8,128)(2,1)S(1)}) custom-call(bf16[1024,9728]{1,0:T(8,128)(2,1)} %w_ref.3), custom_call_target="tpu_custom_call" | custom-call | bytes 9961472 | tf_op jit(solution)/shard_map/fetch_weight/pallas_call | solution.py:76
  24.3 2.8 %partial_logits.6 = (f32[128,2560]{1,0:T(8,128)S(1)}, f32[128,2560]{1,0:T(8,128)S(1)}, bf16[1024,2560]{1,0:T(8,128)(2,1)S(1)}) custom-call(bf16[256,1024]{1,0:T(8,128)(2,1)S(1)} %bitcast.36, bf16[1024,2560]{1,0:T(8,128)(2,1)S(1)} %get-tuple-element.64.refs_1_, bf16[1024,9728]{1,0:T(8,128)(2,1)} %w_ref.3), custom_call_target="tpu_custom_call" | custom-call | flops 1342177280 | bytes 7864320 | tf_op jit(solution)/shard_map/partial_logits/pallas_call | solution.py:76
  27.2 1.5 %partial_logits.7 = (f32[128,2560]{1,0:T(8,128)S(1)}, f32[128,2560]{1,0:T(8,128)S(1)}) custom-call(bf16[256,1024]{1,0:T(8,128)(2,1)S(1)} %bitcast.37, bf16[1024,2560]{1,0:T(8,128)(2,1)S(1)} %get-tuple-element.72.refs_0_), custom_call_target="tpu_custom_call" | custom-call | flops 1342177280 | bytes 7864320 | tf_op jit(solution)/shard_map/partial_logits/pallas_call | solution.py:76
  29.2 2.6 %partial_logits.4 = (f32[128,2304]{1,0:T(8,128)S(1)}, f32[128,2304]{1,0:T(8,128)S(1)}, bf16[1024,256]{1,0:T(8,128)(2,1)}, bf16[1024,2304]{1,0:T(8,128)(2,1)S(1)}) custom-call(bf16[256,1024]{1,0:T(8,128)(2,1)S(1)} %bitcast.38, bf16[1024,2304]{1,0:T(8,128)(2,1)S(1)} %get-tuple-element.55.refs_1_, bf16[1024,9728]{1,0:T(8,128)(2,1)} %w_ref.3), custom_call_target="tpu_custom_call" | custom-call | flops 1207959552 | bytes 7077888 | tf_op jit(solution)/shard_map/partial_logits/pallas_call | solution.py:76
  38.0 1.4 %exponentials.7 = (f32[128,2560]{1,0:T(8,128)S(1)}, f32[128,128]{1,0:T(8,128)S(1)}, f32[128,128]{1,0:T(8,128)S(1)}, f32[8,128]{1,0:T(8,128)S(1)}) custom-call(f32[128,2560]{1,0:T(8,128)S(1)} %get-tuple-element.73.refs_0_, f32[128,2560]{1,0:T(8,128)S(1)} %collective-permute-done.10.refs_1_, s32[128,128]{1,0:T(8,128)S(1)} %get-tuple-element.62.refs_2_.refs_9_.refs_5_, ...), custom_call_target="tpu_custom_call" | custom-call | flops 2621440 | bytes 3932160 | tf_op jit(solution)/shard_map/exponentials/pallas_call | solution.py:76
  39.5 1.5 %collective-permute-start.11 = (f32[8,128]{1,0:T(8,128)S(1)}, f32[8,128]{1,0:T(8,128)S(1)}, u32[]{:S(2)}, u32[]{:S(2)}) collective-permute-start(f32[8,128]{1,0:T(8,128)S(1)} %maximum_maximum_fusion.a_ref), channel_id=1, source_target_pairs={{0,2},{2,0},{4,6},{6,4},{8,10},{10,8},{12,14},{14,12},{1,3},{3,1},... | collective-permute-start | bytes 12296 | tf_op jit(solution)/shard_map/ppermute | solution.py:543
  41.0 2.1 %collective-permute-done.11.b_ref = f32[8,128]{1,0:T(8,128)S(1)} collective-permute-done((f32[8,128]{1,0:T(8,128)S(1)}, f32[8,128]{1,0:T(8,128)S(1)}, u32[]{:S(2)}, u32[]{:S(2)}) %collective-permute-start.11) | collective-permute-done | bytes 4128 | tf_op jit(solution)/shard_map/ppermute | solution.py:543
  43.8 3.0 %collective-permute-done.12.b_ref = f32[8,128]{1,0:T(8,128)S(1)} collective-permute-done((f32[8,128]{1,0:T(8,128)S(1)}, f32[8,128]{1,0:T(8,128)S(1)}, u32[]{:S(2)}, u32[]{:S(2)}) %collective-permute-start.12) | collective-permute-done | bytes 4128 | tf_op jit(solution)/shard_map/ppermute | solution.py:543
  46.8 2.7 %collective-permute-start.13 = (f32[8,128]{1,0:T(8,128)S(1)}, f32[8,128]{1,0:T(8,128)S(1)}, u32[]{:S(2)}, u32[]{:S(2)}) collective-permute-start(f32[8,128]{1,0:T(8,128)S(1)} %join_stats.4.a_ref), channel_id=1, source_target_pairs={{0,8},{2,10},{4,12},{6,14},{8,0},{10,2},{12,4},{14,6},{1,9},{3,11}... | collective-permute-start | bytes 12296 | tf_op jit(solution)/shard_map/ppermute | solution.py:543
  49.4 1.9 %collective-permute-done.13.b_ref = f32[8,128]{1,0:T(8,128)S(1)} collective-permute-done((f32[8,128]{1,0:T(8,128)S(1)}, f32[8,128]{1,0:T(8,128)S(1)}, u32[]{:S(2)}, u32[]{:S(2)}) %collective-permute-start.13) | collective-permute-done | bytes 4128 | tf_op jit(solution)/shard_map/ppermute | solution.py:543
  51.4 2.4 %logit_grad.3.own_ref = bf16[128,4864]{1,0:T(8,128)(2,1)S(1)} custom-call(f32[128,2304]{1,0:T(8,128)S(1)} %get-tuple-element.68.refs_5_.refs_8_.refs_0_, f32[128,2560]{1,0:T(8,128)S(1)} %get-tuple-element.70.refs_6_.refs_9_.refs_1_, f32[128,128]{1,0:T(8,128)S(1)} %get-tuple-element.76.refs_5_.refs_4_.refs_2_, ...), custom_call_target="tpu_custom_call" | custom-call | flops 4980736 | bytes 3735552 | tf_op jit(solution)/shard_map/logit_grad/pallas_call | solution.py:76
  53.9 2.6 %logit_grad.2.own_ref = bf16[128,4864]{1,0:T(8,128)(2,1)S(1)} custom-call(f32[128,2304]{1,0:T(8,128)S(1)} %get-tuple-element.71.refs_10_.refs_2_.refs_0_, f32[128,2560]{1,0:T(8,128)S(1)} %get-tuple-element.79.refs_3_.refs_1_, f32[128,128]{1,0:T(8,128)S(1)} %get-tuple-element.78.refs_7_.refs_6_.refs_2_, f32[128,128]{1,0:T(8,128)S(1)} %get-tuple-element.80.refs_7_.refs_3_, ...), custom_call_target="tpu_custom_call" | custom-call | flops 4980736 | bytes 3735552 | tf_op jit(solution)/shard_map/logit_grad/pallas_call | solution.py:76
  57.1 5.2 %feature_terms.2.refs_0_ = f32[256,1024]{1,0:T(8,128)S(1)} custom-call(bf16[128,4864]{1,0:T(8,128)(2,1)S(1)} %logit_grad.3.own_ref, bf16[128,4864]{1,0:T(8,128)(2,1)} %collective-permute-done.15.far_ref, bf16[1024,9728]{1,0:T(8,128)(2,1)} %w_ref.3), custom_call_target="tpu_custom_call" | custom-call | flops 2550136832 | bytes 12451840 | tf_op jit(solution)/shard_map/feature_terms/pallas_call | solution.py:76
  62.3 6.7 %feature_terms.3 = (f32[128,1024]{1,0:T(8,128)}, bf16[128,1024]{1,0:T(8,128)(2,1)}) custom-call(bf16[128,4864]{1,0:T(8,128)(2,1)S(1)} %logit_grad.2.own_ref, bf16[128,4864]{1,0:T(8,128)(2,1)} %collective-permute-done.14.far_ref, bf16[1024,9728]{1,0:T(8,128)(2,1)} %w_ref.3, f32[256,1024]{1,0:T(8,128)S(1)} %feature_terms.2.refs_0_, s32[8]{0:T(128)S(1)} %xor_xor_fusion.refs_1_), custom_call_target="tpu_custom_call" | custom-call | flops 2550136832 | bytes 12451840 | tf_op jit(solution)/shard_map/feature_terms/pallas_call | solution.py:76
  69.0 1.6 %collective-permute-start.16 = (bf16[128,1024]{1,0:T(8,128)(2,1)}, bf16[128,1024]{1,0:T(8,128)(2,1)S(1)}, u32[]{:S(2)}, u32[]{:S(2)}) collective-permute-start(bf16[128,1024]{1,0:T(8,128)(2,1)} %get-tuple-element.84), channel_id=1, source_target_pairs={{0,2},{2,0},{4,6},{6,4},{8,10},{10,8},{12,14},{14,12},{1,3},{3,1},... | collective-permute-start | bytes 786440 | tf_op jit(solution)/shard_map/ppermute | solution.py:565
  70.6 6.1 %weight_grad.2.refs_0_ = bf16[1024,9728]{1,0:T(8,128)(2,1)} custom-call(bf16[1024,256]{1,0:T(8,128)(2,1)} %get-tuple-element.85.ht_ref, bf16[128,4864]{1,0:T(8,128)(2,1)S(1)} %logit_grad.3.own_ref, bf16[128,4864]{1,0:T(8,128)(2,1)} %collective-permute-done.15.far_ref), custom_call_target="tpu_custom_call" | custom-call | flops 2550136832 | bytes 12451840 | tf_op jit(solution)/shard_map/weight_grad/pallas_call | solution.py:76
  78.4 3.4 %collective-permute-start.19 = (bf16[32,1024]{1,0:T(8,128)(2,1)S(1)}, bf16[32,1024]{1,0:T(8,128)(2,1)S(1)}, u32[]{:S(2)}, u32[]{:S(2)}) collective-permute-start(bf16[32,1024]{1,0:T(8,128)(2,1)S(1)} %get-tuple-element.91), channel_id=1, source_target_pairs={{0,12},{2,14},{4,8},{6,10},{8,4},{10,6},{12,0},{14,2},{1,13},{3,15... | collective-permute-start | bytes 196616 | tf_op jit(solution)/shard_map/ppermute | solution.py:571
  81.8 6.0 %weight_grad.3 = bf16[1024,9728]{1,0:T(8,128)(2,1)} custom-call(bf16[1024,256]{1,0:T(8,128)(2,1)} %get-tuple-element.85.ht_ref, bf16[128,4864]{1,0:T(8,128)(2,1)S(1)} %logit_grad.2.own_ref, bf16[128,4864]{1,0:T(8,128)(2,1)} %collective-permute-done.14.far_ref, bf16[1024,9728]{1,0:T(8,128)(2,1)} %weight_grad.2.refs_0_), custom_call_target="tpu_custom_call", output_to_operand_aliasing={{}: (3, {})} | custom-call | flops 2550136832 | bytes 12451840 | tf_op jit(solution)/shard_map/weight_grad/pallas_call | solution.py:76
  (64 shorter events, 14.5 us)
Async XLA Ops:
  0.6 18.9 %copy-start.3 = (f32[2]{0:T(128)S(1)}, f32[2]{0:T(128)}, u32[]{:S(2)}) copy-start(f32[2]{0:T(128)} %constant.22.clone) | copy-start | bytes 28
  0.6 8.9 %collective-permute-start = (bf16[1,32,1024]{2,1,0:T(8,128)(2,1)}, bf16[1,32,1024]{2,1,0:T(8,128)(2,1)S(1)}, u32[]{:S(2)}, u32[]{:S(2)}) collective-permute-start(bf16[1,32,1024]{2,1,0:T(8,128)(2,1)} %bitcast.41), channel_id=1, source_target_pairs={{0,8},{2,10},{4,12},{6,14},{8,0},{10,2},{12,4},{14,6},{1,9},{3,11}... | collective-permute-start | bytes 196616 | tf_op jit(solution)/shard_map/ppermute | solution.py:489
  4.7 4.7 %collective-permute-start.2 = (f32[4,128]{1,0:T(4,128)}, f32[4,128]{1,0:T(4,128)S(1)}, u32[]{:S(2)}, u32[]{:S(2)}) collective-permute-start(f32[4,128]{1,0:T(4,128)} %bitcast.42), channel_id=1, source_target_pairs={{0,8},{2,10},{4,12},{6,14},{8,0},{10,2},{12,4},{14,6},{1,9},{3,11}... | collective-permute-start | bytes 6152 | tf_op jit(solution)/shard_map/ppermute | solution.py:492
  4.8 4.7 %collective-permute-start.1 = (s32[4,128]{1,0:T(4,128)}, s32[4,128]{1,0:T(4,128)S(1)}, u32[]{:S(2)}, u32[]{:S(2)}) collective-permute-start(s32[4,128]{1,0:T(4,128)} %bitcast.44), channel_id=1, source_target_pairs={{0,8},{2,10},{4,12},{6,14},{8,0},{10,2},{12,4},{14,6},{1,9},{3,11}... | collective-permute-start | bytes 6152 | tf_op jit(solution)/shard_map/ppermute | solution.py:492
  11.1 6.3 %collective-permute-start.3 = (bf16[2,32,1024]{2,1,0:T(8,128)(2,1)S(1)}, bf16[2,32,1024]{2,1,0:T(8,128)(2,1)S(1)}, u32[]{:S(2)}, u32[]{:S(2)}) collective-permute-start(bf16[2,32,1024]{2,1,0:T(8,128)(2,1)S(1)} %maximum_bitcast_fusion), channel_id=1, source_target_pairs={{0,4},{2,6},{4,0},{6,2},{8,12},{10,14},{12,8},{14,10},{1,5},{3,7},... | collective-permute-start | bytes 393224 | tf_op jit(solution)/shard_map/ppermute | solution.py:489
  13.7 3.7 %collective-permute-start.4 = (f32[2,8,128]{2,1,0:T(8,128)S(1)}, f32[2,8,128]{2,1,0:T(8,128)S(1)}, u32[]{:S(2)}, u32[]{:S(2)}) collective-permute-start(f32[2,8,128]{2,1,0:T(8,128)S(1)} %pad_maximum_fusion.3), channel_id=1, source_target_pairs={{0,4},{2,6},{4,0},{6,2},{8,12},{10,14},{12,8},{14,10},{1,5},{3,7},... | collective-permute-start | bytes 24584 | tf_op jit(solution)/shard_map/ppermute | solution.py:496
  17.5 6.6 %collective-permute-start.5 = (bf16[4,32,1024]{2,1,0:T(8,128)(2,1)S(1)}, bf16[4,32,1024]{2,1,0:T(8,128)(2,1)S(1)}, u32[]{:S(2)}, u32[]{:S(2)}) collective-permute-start(bf16[4,32,1024]{2,1,0:T(8,128)(2,1)S(1)} %bitcast.40), channel_id=1, source_target_pairs={{0,2},{2,0},{4,6},{6,4},{8,10},{10,8},{12,14},{14,12},{1,3},{3,1},... | collective-permute-start | bytes 786440 | tf_op jit(solution)/shard_map/ppermute | solution.py:489
  19.0 5.0 %collective-permute-start.6 = (f32[2,16,128]{2,1,0:T(8,128)S(1)}, f32[2,16,128]{2,1,0:T(8,128)S(1)}, u32[]{:S(2)}, u32[]{:S(2)}) collective-permute-start(f32[2,16,128]{2,1,0:T(8,128)S(1)} %pad_maximum_fusion.2), channel_id=1, source_target_pairs={{0,2},{2,0},{4,6},{6,4},{8,10},{10,8},{12,14},{14,12},{1,3},{3,1},... | collective-permute-start | bytes 49160 | tf_op jit(solution)/shard_map/ppermute | solution.py:496
  27.1 8.8 %collective-permute-start.9 = (f32[128,2560]{1,0:T(8,128)S(1)}, f32[128,2560]{1,0:T(8,128)S(1)}, u32[]{:S(2)}, u32[]{:S(2)}) collective-permute-start(f32[128,2560]{1,0:T(8,128)S(1)} %get-tuple-element.66), channel_id=1, source_target_pairs={{0,1},{1,0},{2,3},{3,2},{4,5},{5,4},{6,7},{7,6},{8,9},{9,8},{10,11... | collective-permute-start | bytes 3932168 | tf_op jit(solution)/shard_map/ppermute | solution.py:516
  28.7 9.3 %collective-permute-start.10 = (f32[128,2560]{1,0:T(8,128)S(1)}, f32[128,2560]{1,0:T(8,128)S(1)}, u32[]{:S(2)}, u32[]{:S(2)}) collective-permute-start(f32[128,2560]{1,0:T(8,128)S(1)} %get-tuple-element.74), channel_id=1, source_target_pairs={{0,1},{1,0},{2,3},{3,2},{4,5},{5,4},{6,7},{7,6},{8,9},{9,8},{10,11... | collective-permute-start | bytes 3932168 | tf_op jit(solution)/shard_map/ppermute | solution.py:516
  31.8 2.9 %collective-permute-start.8 = (f32[128,2304]{1,0:T(8,128)S(1)}, f32[128,2304]{1,0:T(8,128)S(1)}, u32[]{:S(2)}, u32[]{:S(2)}) collective-permute-start(f32[128,2304]{1,0:T(8,128)S(1)} %get-tuple-element.60), channel_id=1, source_target_pairs={{0,1},{1,0},{2,3},{3,2},{4,5},{5,4},{6,7},{7,6},{8,9},{9,8},{10,11... | collective-permute-start | bytes 3538952 | tf_op jit(solution)/shard_map/ppermute | solution.py:516
  31.9 2.0 %copy-start.1 = (f32[128]{0:T(128)S(1)}, f32[128]{0:T(128)}, u32[]{:S(2)}) copy-start(f32[128]{0:T(128)} %param.12) | copy-start | bytes 1540
  31.9 2.0 %copy-start.2 = (s32[128]{0:T(128)S(1)}, s32[128]{0:T(128)}, u32[]{:S(2)}) copy-start(s32[128]{0:T(128)} %param.11) | copy-start | bytes 1540
  33.3 3.6 %collective-permute-start.7 = (f32[128,2304]{1,0:T(8,128)S(1)}, f32[128,2304]{1,0:T(8,128)S(1)}, u32[]{:S(2)}, u32[]{:S(2)}) collective-permute-start(f32[128,2304]{1,0:T(8,128)S(1)} %get-tuple-element.58), channel_id=1, source_target_pairs={{0,1},{1,0},{2,3},{3,2},{4,5},{5,4},{6,7},{7,6},{8,9},{9,8},{10,11... | collective-permute-start | bytes 3538952 | tf_op jit(solution)/shard_map/ppermute | solution.py:516
  39.5 3.6 %collective-permute-start.11 = (f32[8,128]{1,0:T(8,128)S(1)}, f32[8,128]{1,0:T(8,128)S(1)}, u32[]{:S(2)}, u32[]{:S(2)}) collective-permute-start(f32[8,128]{1,0:T(8,128)S(1)} %maximum_maximum_fusion.a_ref), channel_id=1, source_target_pairs={{0,2},{2,0},{4,6},{6,4},{8,10},{10,8},{12,14},{14,12},{1,3},{3,1},... | collective-permute-start | bytes 12296 | tf_op jit(solution)/shard_map/ppermute | solution.py:543
  43.1 3.7 %collective-permute-start.12 = (f32[8,128]{1,0:T(8,128)S(1)}, f32[8,128]{1,0:T(8,128)S(1)}, u32[]{:S(2)}, u32[]{:S(2)}) collective-permute-start(f32[8,128]{1,0:T(8,128)S(1)} %join_stats.3.a_ref), channel_id=1, source_target_pairs={{0,4},{2,6},{4,0},{6,2},{8,12},{10,14},{12,8},{14,10},{1,5},{3,7},... | collective-permute-start | bytes 12296 | tf_op jit(solution)/shard_map/ppermute | solution.py:543
  46.8 4.6 %collective-permute-start.13 = (f32[8,128]{1,0:T(8,128)S(1)}, f32[8,128]{1,0:T(8,128)S(1)}, u32[]{:S(2)}, u32[]{:S(2)}) collective-permute-start(f32[8,128]{1,0:T(8,128)S(1)} %join_stats.4.a_ref), channel_id=1, source_target_pairs={{0,8},{2,10},{4,12},{6,14},{8,0},{10,2},{12,4},{14,6},{1,9},{3,11}... | collective-permute-start | bytes 12296 | tf_op jit(solution)/shard_map/ppermute | solution.py:543
  53.8 3.3 %collective-permute-start.15 = (bf16[128,4864]{1,0:T(8,128)(2,1)S(1)}, bf16[128,4864]{1,0:T(8,128)(2,1)}, u32[]{:S(2)}, u32[]{:S(2)}) collective-permute-start(bf16[128,4864]{1,0:T(8,128)(2,1)S(1)} %logit_grad.3.own_ref), channel_id=1, source_target_pairs={{0,1},{1,0},{2,3},{3,2},{4,5},{5,4},{6,7},{7,6},{8,9},{9,8},{10,11... | collective-permute-start | bytes 3735560 | tf_op jit(solution)/shard_map/ppermute | solution.py:516
  56.5 5.8 %collective-permute-start.14 = (bf16[128,4864]{1,0:T(8,128)(2,1)S(1)}, bf16[128,4864]{1,0:T(8,128)(2,1)}, u32[]{:S(2)}, u32[]{:S(2)}) collective-permute-start(bf16[128,4864]{1,0:T(8,128)(2,1)S(1)} %logit_grad.2.own_ref), channel_id=1, source_target_pairs={{0,1},{1,0},{2,3},{3,2},{4,5},{5,4},{6,7},{7,6},{8,9},{9,8},{10,11... | collective-permute-start | bytes 3735560 | tf_op jit(solution)/shard_map/ppermute | solution.py:516
  69.0 8.5 %collective-permute-start.16 = (bf16[128,1024]{1,0:T(8,128)(2,1)}, bf16[128,1024]{1,0:T(8,128)(2,1)S(1)}, u32[]{:S(2)}, u32[]{:S(2)}) collective-permute-start(bf16[128,1024]{1,0:T(8,128)(2,1)} %get-tuple-element.84), channel_id=1, source_target_pairs={{0,2},{2,0},{4,6},{6,4},{8,10},{10,8},{12,14},{14,12},{1,3},{3,1},... | collective-permute-start | bytes 786440 | tf_op jit(solution)/shard_map/ppermute | solution.py:565
  70.6 6.9 %copy-start = (f32[128,1024]{1,0:T(8,128)S(1)}, f32[128,1024]{1,0:T(8,128)}, u32[]{:S(2)}) copy-start(f32[128,1024]{1,0:T(8,128)} %get-tuple-element.83) | copy-start | bytes 1572868
  77.7 10.2 %collective-permute-start.17 = (bf16[32,1024]{1,0:T(8,128)(2,1)S(1)}, bf16[32,1024]{1,0:T(8,128)(2,1)S(1)}, u32[]{:S(2)}, u32[]{:S(2)}) collective-permute-start(bf16[32,1024]{1,0:T(8,128)(2,1)S(1)} %get-tuple-element.90), channel_id=1, source_target_pairs={{0,4},{2,6},{4,0},{6,2},{8,12},{10,14},{12,8},{14,10},{1,5},{3,7},... | collective-permute-start | bytes 196616 | tf_op jit(solution)/shard_map/ppermute | solution.py:571
  78.4 9.5 %collective-permute-start.19 = (bf16[32,1024]{1,0:T(8,128)(2,1)S(1)}, bf16[32,1024]{1,0:T(8,128)(2,1)S(1)}, u32[]{:S(2)}, u32[]{:S(2)}) collective-permute-start(bf16[32,1024]{1,0:T(8,128)(2,1)S(1)} %get-tuple-element.91), channel_id=1, source_target_pairs={{0,12},{2,14},{4,8},{6,10},{8,4},{10,6},{12,0},{14,2},{1,13},{3,15... | collective-permute-start | bytes 196616 | tf_op jit(solution)/shard_map/ppermute | solution.py:571
  81.8 6.1 %collective-permute-start.18 = (bf16[32,1024]{1,0:T(8,128)(2,1)S(1)}, bf16[32,1024]{1,0:T(8,128)(2,1)S(1)}, u32[]{:S(2)}, u32[]{:S(2)}) collective-permute-start(bf16[32,1024]{1,0:T(8,128)(2,1)S(1)} %get-tuple-element.92), channel_id=1, source_target_pairs={{0,8},{2,10},{4,12},{6,14},{8,0},{10,2},{12,4},{14,6},{1,9},{3,11}... | collective-permute-start | bytes 196616 | tf_op jit(solution)/shard_map/ppermute | solution.py:571
